TPU v7x, 32 devices: a whole 2x2x4 slice. The times are simulated.
32 devices in a mesh: face: 4 (over x, core), tile: 8 (over z, y).
Axes of the slice: x: 2, y: 2, z: 4, core: 2. Of those that a mesh axis runs over, the one named last changes fastest.
Arguments:
- atmos: bfloat16 [64, 192, 2048], P(None, 'tile', 'face'), may hold values from -6 to 6
- ocean: bfloat16 [64, 65536], P(None, ('face', 'tile')), may hold values from -6 to 6
- surface_heat_weight: float32 [64], replicated, may hold values from -4 to 4
- air_conv_first_weight: bfloat16 [3, 3, 64, 64], replicated, may hold values from -0.25 to 0.25
- air_conv_second_weight: bfloat16 [3, 3, 64, 64], replicated, may hold values from -0.25 to 0.25
- marine_conv_first_weight: bfloat16 [9, 64, 64], replicated, may hold values from -0.25 to 0.25
- marine_conv_second_weight: bfloat16 [9, 64, 64], replicated, may hold values from -0.25 to 0.25
- marine_coupling_slot: int32 [65536], P(('face', 'tile')), may hold values from 0 to 4095, as said below
- coupling_air_cells: int32 [32, 4096], P(('face', 'tile')), may hold values from 0 to 12287
- marine_neighbour_index: int32 [9, 65536], P(None, ('face', 'tile')), may hold values from 0 to 2559, as said below
Outputs:
- atmos_next: bfloat16 [64, 192, 2048], P(None, 'tile', 'face')
- ocean_next: bfloat16 [64, 65536], P(None, ('face', 'tile'))
Inputs may be any that keep to these rules, and one draw needn't show every extreme that they name: `marine_coupling_slot`: within one ocean device's 2048 entries the values are distinct; value // 128 is the atmosphere device serving the cell, so no atmosphere device serves more than 128 cells of one ocean device, and on every ocean device some atmosphere device serves exactly 128. `marine_neighbour_index`: entry [k, g] lies within 256 of the cell's own position 256 + g % 2048; every device's entries reach both ends.
All inputs are finite; a program needn't handle non-finite values.
Results may differ from a plain program's by a relative error of at most 0.0064.
Values may be sent and summed in bfloat16 or wider, within the bound.
No kernel may reach another device: no remote copies, remote signals or barrier semaphores. Data moves between devices by JAX's collectives and lax.ppermute only.
A program may use at most 128 MiB of HBM per device.

v0:
```python
import math

import jax
import jax.numpy as jnp
from jax import lax
from jax.sharding import PartitionSpec as P

HALO = 256


def with_halo(cells, sides, width, closed):
    for axis, dim in sides:
        count = lax.axis_size(axis)
        ends = count if closed else count - 1
        head = lax.slice_in_dim(cells, 0, width, axis=dim)
        tail = lax.slice_in_dim(cells, cells.shape[dim] - width, cells.shape[dim], axis=dim)
        cells = jnp.concatenate(
            [
                lax.ppermute(tail, axis, [(i, (i + 1) % count) for i in range(ends)]),
                cells,
                lax.ppermute(head, axis, [((i + 1) % count, i) for i in range(ends)]),
            ],
            axis=dim,
        )
    return cells


def valid_conv(extended, weight, row_total, column_total):
    summed = jnp.zeros((extended.shape[0], row_total, column_total), jnp.float32)
    for row_tap in range(3):
        for col_tap in range(3):
            window = extended[:, row_tap : row_tap + row_total, col_tap : col_tap + column_total]
            summed = summed + jnp.einsum(
                "oc,crw->orw", weight[row_tap, col_tap], window, preferred_element_type=jnp.float32
            )
    return summed


def atmosphere_conv(values, weight):
    with_rows = with_halo(values, (("tile", 1),), 1, False)
    extended = with_halo(with_rows, (("face", 2),), 1, True)
    return valid_conv(extended, weight, values.shape[1], values.shape[2])


def assemble(blocks):
    count, channels, block = blocks.shape
    return jnp.transpose(blocks, (1, 0, 2)).reshape(channels, count * block)


def pick_columns(data, index):
    total = index.shape[0]
    block = math.gcd(total, 1024)
    places = jnp.arange(data.shape[1], dtype=jnp.int32)

    def pick_one_block(number):
        wanted = lax.dynamic_slice_in_dim(index, number * block, block, 0)
        select = (places[:, None] == wanted[None, :]).astype(jnp.bfloat16)
        return jnp.dot(data, select, preferred_element_type=jnp.float32)

    return assemble(lax.map(pick_one_block, jnp.arange(total // block, dtype=jnp.int32)))


def add_columns(data, index, width):
    block = math.gcd(width, 1024)
    places = jnp.arange(block, dtype=jnp.int32)

    def add_one_block(number):
        select = (index[:, None] == number * block + places[None, :]).astype(jnp.bfloat16)
        return jnp.dot(data, select, preferred_element_type=jnp.float32)

    return assemble(lax.map(add_one_block, jnp.arange(width // block, dtype=jnp.int32)))


def neighbour_mix(values, taps, weight, out_len, reach):
    block = math.gcd(out_len, 256)
    span = block + 2 * reach
    places = jnp.arange(span, dtype=jnp.int32)

    def neighbour_one_block(number):
        first = number * block
        window = lax.dynamic_slice_in_dim(values, first, span, 1)
        local_taps = lax.dynamic_slice_in_dim(taps, first, block, 1) - first
        summed = jnp.zeros((values.shape[0], block), jnp.float32)
        for tap in range(weight.shape[0]):
            select = (places[:, None] == local_taps[tap][None, :]).astype(jnp.bfloat16)
            picked = jnp.dot(window, select, preferred_element_type=jnp.float32).astype(
                jnp.bfloat16
            )
            summed = summed + jnp.dot(weight[tap], picked, preferred_element_type=jnp.float32)
        return summed

    return assemble(lax.map(neighbour_one_block, jnp.arange(out_len // block, dtype=jnp.int32)))


def ocean_conv(values, weight, neighbours, reach):
    extended = with_halo(values, ((("face", "tile"), 1),), reach, False)
    return neighbour_mix(extended, neighbours, weight, values.shape[1], reach)


def shards(
    atmos,
    ocean,
    surface_heat_weight,
    air_conv_first_weight,
    air_conv_second_weight,
    marine_conv_first_weight,
    marine_conv_second_weight,
    marine_coupling_slot,
    coupling_air_cells,
    marine_neighbour_index,
):
    devices = lax.axis_size(("face", "tile"))
    slot_space = coupling_air_cells.shape[1]
    capacity = slot_space // devices
    channels, row_total, column_total = atmos.shape
    cell_count = row_total * column_total
    cell_total = ocean.shape[1]
    reach = marine_neighbour_index.shape[1] and HALO
    heat_pair = jnp.stack([ocean[0], jnp.ones((cell_total,), jnp.bfloat16)], axis=0)
    slot_table = add_columns(heat_pair, marine_coupling_slot, slot_space)
    surface_heat_value = slot_table[0].reshape(devices, capacity)
    live_slots = slot_table[1].reshape(devices, capacity)
    got_values, got_live = (
        lax.all_to_all(
            surface_heat_value.astype(jnp.bfloat16),
            ("face", "tile"),
            split_axis=0,
            concat_axis=0,
            tiled=True,
        ).astype(surface_heat_value.dtype),
        lax.all_to_all(
            live_slots.astype(jnp.bfloat16),
            ("face", "tile"),
            split_axis=0,
            concat_axis=0,
            tiled=True,
        ).astype(live_slots.dtype),
    )
    targets = coupling_air_cells[0]
    arrived_pair = jnp.stack([got_values.reshape(-1), got_live.reshape(-1)], axis=0).astype(
        jnp.bfloat16
    )
    cell_table = add_columns(arrived_pair, targets, cell_count)
    overall_sums = cell_table[0]
    running_counts = cell_table[1]
    surface_heat_field = (overall_sums / jnp.maximum(running_counts, 1.0)).reshape(
        row_total, column_total
    )
    begin_offset = (
        atmos.astype(jnp.float32) + surface_heat_weight[:, None, None] * surface_heat_field[None]
    ).astype(jnp.bfloat16)
    hidden = jax.nn.gelu(atmosphere_conv(begin_offset, air_conv_first_weight)).astype(jnp.bfloat16)
    atmos_next = (
        begin_offset.astype(jnp.float32) + atmosphere_conv(hidden, air_conv_second_weight)
    ).astype(jnp.bfloat16)
    outgoing = (
        pick_columns(atmos_next.reshape(channels, cell_count), targets)
        .astype(jnp.bfloat16)
        .reshape(channels, devices, capacity)
    )
    arrived = lax.all_to_all(
        outgoing, ("face", "tile"), split_axis=1, concat_axis=1, tiled=True
    ).reshape(channels, slot_space)
    forcing = pick_columns(arrived, marine_coupling_slot).astype(jnp.bfloat16)
    ocean_start = (ocean.astype(jnp.float32) + forcing.astype(jnp.float32)).astype(jnp.bfloat16)
    ocean_hidden = jax.nn.gelu(
        ocean_conv(ocean_start, marine_conv_first_weight, marine_neighbour_index, reach)
    ).astype(jnp.bfloat16)
    ocean_next = (
        ocean_start.astype(jnp.float32)
        + ocean_conv(ocean_hidden, marine_conv_second_weight, marine_neighbour_index, reach)
    ).astype(jnp.bfloat16)
    return (atmos_next, ocean_next)


def solution(mesh):
    placed = (
        P(None, "tile", "face"),
        P(None, ("face", "tile")),
        P(),
        P(),
        P(),
        P(),
        P(),
        P(("face", "tile")),
        P(("face", "tile"), None),
        P(None, ("face", "tile")),
    )
    return jax.shard_map(
        shards,
        mesh=mesh,
        in_specs=placed,
        out_specs=(P(None, "tile", "face"), P(None, ("face", "tile"))),
        check_vma=False,
    )
```

profile of v0, /device:TPU:29, one launch (start us, length us, event | category | flops | bytes accessed | tf_op | source)
XLA Modules:
  0.0 343.6 jit_solution(17508527532110102629)
XLA Ops:
  1.5 13.4 %while.68 = (s32[]{:T(128)}, bf16[4,2,1024]{2,1,0:T(2,128)(2,1)S(1)}, s32[2048]{0:T(1024)}, s32[4]{0:T(128)S(1)}, bf16[2,2048]{1,0:T(2,128)(2,1)S(1)}, /*index=5*/s32[]{:T(128)}, s32[1]{0:T(128)}) while((s32[]{:T(128)}, bf16[4,2,1024]{2,1,0:T(2,128)(2,1)S(1)}, s32[2048]{0:T(1024)}, s32[4]{0:T(128)S(1)}, ...), condition=%wide.region_1.2_spmd.clone, body=%wide.region_0.1_spmd.clone.sunk | while | flops 10486787 | bytes 32877 | solution.py:71
  15.6 8.8 %all_to_all.17 = bf16[32,1,128]{2,1,0:T(2,128)(2,1)S(1)} all-to-all(bf16[32,1,128]{2,1,0:T(2,128)(2,1)S(1)} %bitcast.364), channel_id=1, replica_groups=mesh['face'=4,'tile'=8] {'face','tile'}, dimensions={0} | all-to-all | bytes 16384 | tf_op jit(solution)/shard_map/all_to_all | solution.py:124
  24.4 6.9 %all-to-all-start.1 = ((bf16[32,1,128]{2,1,0:T(2,128)(2,1)}), bf16[32,1,128]{2,1,0:T(2,128)(2,1)S(1)}, u32[]{:S(2)}, u32[]{:S(2)}) async-start(bf16[32,1,128]{2,1,0:T(2,128)(2,1)} %bitcast.3), calls=%async_computation.1 | async-start | bytes 32768 | tf_op jit(solution)/shard_map/all_to_all | solution.py:131
  31.2 2.7 all-to-all-done.1
  34.0 46.5 %while.69 = (s32[]{:T(128)}, f32[12,2,1024]{2,1,0:T(2,128)S(1)}, s32[1,4096]{1,0:T(1,128)S(1)}, s32[12]{0:T(128)S(1)}, bf16[2,4096]{1,0:T(2,128)(2,1)S(1)}, /*index=5*/s32[]{:T(128)}, s32[1]{0:T(128)}) while((s32[]{:T(128)}, f32[12,2,1024]{2,1,0:T(2,128)S(1)}, s32[1,4096]{1,0:T(1,128)S(1)}, s32[12]{0:T(128)S(1)}, ...), condition=%wide.region_3.4_spmd.clone, body=%wide.region_2.3_spmd.clone.sunk | while | flops 20972548 | bytes 49261 | solution.py:71
  43.0 2.6 fusion.358
  46.9 2.6 fusion.358
  50.8 2.6 fusion.358
  82.7 4.0 %collective-permute-start.1 = (bf16[64,1,512]{2,0,1:T(8,128)(2,1)S(1)}, bf16[64,1,512]{2,0,1:T(8,128)(2,1)S(1)}, u32[]{:S(2)}, u32[]{:S(2)}) collective-permute-start(bf16[64,1,512]{2,0,1:T(8,128)(2,1)S(1)} %get-tuple-element.485), channel_id=1, source_target_pairs={{1,0},{2,1},{3,2},{4,3},{5,4},{6,5},{7,6},{9,8},{10,9},{11,10},{12... | collective-permute-start | bytes 196616 | tf_op jit(solution)/shard_map/ppermute | solution.py:21
  91.9 5.8 %collective-permute-done.2 = bf16[64,26,1]{2,0,1:T(8,128)(2,1)S(1)} collective-permute-done((bf16[64,26,1]{2,0,1:T(8,128)(2,1)S(1)}, bf16[64,26,1]{2,0,1:T(8,128)(2,1)S(1)}, u32[]{:S(2)}, u32[]{:S(2)}) %collective-permute-start.2) | collective-permute-done | bytes 3360 | tf_op jit(solution)/shard_map/ppermute | solution.py:19
  97.7 3.9 %collective-permute-done.3 = bf16[64,26,1]{2,0,1:T(8,128)(2,1)S(1)} collective-permute-done((bf16[64,26,1]{2,0,1:T(8,128)(2,1)S(1)}, bf16[64,26,1]{2,0,1:T(8,128)(2,1)S(1)}, u32[]{:S(2)}, u32[]{:S(2)}) %collective-permute-start.3) | collective-permute-done | bytes 3360 | tf_op jit(solution)/shard_map/ppermute | solution.py:21
  111.4 5.1 %fusion.197 = bf16[64,24,512]{2,0,1:T(8,128)(2,1)S(1)} fusion(f32[24,512,64]{1,2,0:T(8,128)S(1)} %fusion.221, f32[24,512,64]{1,2,0:T(8,128)S(1)} %fusion.223, f32[24,512,64]{1,2,0:T(8,128)} %fusion.225, f32[24,512,64]{1,2,0:T(8,128)S(1)} %fusion.259, f32[24,512,64]{1,2,0:T(8,128)S(1)} %fusion.227, f32[24,512,64]{1,2,0:T(8,128)} %fusion.229, ...), kind=kOutput, calls=%fused_computation.188 | convolution fusion | flops 114032640 | bytes 28327936 | tf_op jit(solution)/shard_map/oc,crw->orw/dot_general | solution.py:33
  117.8 4.6 %collective-permute-start.5 = (bf16[64,1,512]{2,0,1:T(8,128)(2,1)S(1)}, bf16[64,1,512]{2,0,1:T(8,128)(2,1)S(1)}, u32[]{:S(2)}, u32[]{:S(2)}) collective-permute-start(bf16[64,1,512]{2,0,1:T(8,128)(2,1)S(1)} %get-tuple-element.483), channel_id=1, source_target_pairs={{1,0},{2,1},{3,2},{4,3},{5,4},{6,5},{7,6},{9,8},{10,9},{11,10},{12... | collective-permute-start | bytes 196616 | tf_op jit(solution)/shard_map/ppermute | solution.py:21
  127.1 7.1 %collective-permute-done.6 = bf16[64,26,1]{2,0,1:T(8,128)(2,1)S(1)} collective-permute-done((bf16[64,26,1]{2,0,1:T(8,128)(2,1)S(1)}, bf16[64,26,1]{2,0,1:T(8,128)(2,1)S(1)}, u32[]{:S(2)}, u32[]{:S(2)}) %collective-permute-start.6) | collective-permute-done | bytes 3360 | tf_op jit(solution)/shard_map/ppermute | solution.py:19
  134.2 2.6 collective-permute-done.7
  148.2 5.8 %fusion.198 = bf16[64,24,512]{2,0,1:T(8,128)(2,1)S(1)} fusion(f32[24,512,64]{1,2,0:T(8,128)S(1)} %fusion.203, f32[24,512,64]{1,2,0:T(8,128)S(1)} %fusion.205, f32[24,512,64]{1,2,0:T(8,128)} %fusion.207, f32[24,512,64]{1,2,0:T(8,128)S(1)} %fusion.249, f32[24,512,64]{1,2,0:T(8,128)} %fusion.209, f32[24,512,64]{1,2,0:T(8,128)} %fusion.211, ...), kind=kOutput, calls=%fused_computation.190 | convolution fusion | flops 109314048 | bytes 29900800 | tf_op jit(solution)/shard_map/oc,crw->orw/dot_general | solution.py:33
  154.2 39.9 %while.70 = (s32[]{:T(128)}, bf16[4,64,1024]{2,1,0:T(8,128)(2,1)}, s32[4]{0:T(128)S(1)}, s32[4096]{0:T(1024)S(1)}, bf16[64,12288]{1,0:T(8,128)(2,1)S(1)}, /*index=5*/s32[]{:T(128)}, s32[1]{0:T(128)}, s32[]{:T(128)}, s32[]{:T(128)}) while((s32[]{:T(128)}, bf16[4,64,1024]{2,1,0:T(8,128)(2,1)}, s32[4]{0:T(128)S(1)}, ...), condition=%wide.region_5.6_spmd.clone, body=%wide.region_4.5_spmd.clone.sunk | while | flops 1623195648 | bytes 1847963 | solution.py:60
  155.7 8.7 %fusion.360 = bf16[4,64,1024]{2,1,0:T(8,128)(2,1)} fusion(bf16[4,64,1024]{2,1,0:T(8,128)(2,1)} %get-tuple-element.778, s32[]{:T(128)} %get-tuple-element.777, bf16[64,12288]{1,0:T(8,128)(2,1)S(1)} %get-tuple-element.790, s32[1024]{0:T(1024)S(1)} %dynamic_slice.145), kind=kOutput, calls=%fused_computation.24.clone.1 | convolution fusion | flops 1623195648 | bytes 1839616 | tf_op jit(solution)/shard_map/while/body/eval_jaxpr/dot_general | solution.py:58
  165.6 8.7 %fusion.360 = bf16[4,64,1024]{2,1,0:T(8,128)(2,1)} fusion(bf16[4,64,1024]{2,1,0:T(8,128)(2,1)} %get-tuple-element.778, s32[]{:T(128)} %get-tuple-element.777, bf16[64,12288]{1,0:T(8,128)(2,1)S(1)} %get-tuple-element.790, s32[1024]{0:T(1024)S(1)} %dynamic_slice.145), kind=kOutput, calls=%fused_computation.24.clone.1 | convolution fusion | flops 1623195648 | bytes 1839616 | tf_op jit(solution)/shard_map/while/body/eval_jaxpr/dot_general | solution.py:58
  175.5 8.7 %fusion.360 = bf16[4,64,1024]{2,1,0:T(8,128)(2,1)} fusion(bf16[4,64,1024]{2,1,0:T(8,128)(2,1)} %get-tuple-element.778, s32[]{:T(128)} %get-tuple-element.777, bf16[64,12288]{1,0:T(8,128)(2,1)S(1)} %get-tuple-element.790, s32[1024]{0:T(1024)S(1)} %dynamic_slice.145), kind=kOutput, calls=%fused_computation.24.clone.1 | convolution fusion | flops 1623195648 | bytes 1839616 | tf_op jit(solution)/shard_map/while/body/eval_jaxpr/dot_general | solution.py:58
  185.4 8.7 %fusion.360 = bf16[4,64,1024]{2,1,0:T(8,128)(2,1)} fusion(bf16[4,64,1024]{2,1,0:T(8,128)(2,1)} %get-tuple-element.778, s32[]{:T(128)} %get-tuple-element.777, bf16[64,12288]{1,0:T(8,128)(2,1)S(1)} %get-tuple-element.790, s32[1024]{0:T(1024)S(1)} %dynamic_slice.145), kind=kOutput, calls=%fused_computation.24.clone.1 | convolution fusion | flops 1623195648 | bytes 1839616 | tf_op jit(solution)/shard_map/while/body/eval_jaxpr/dot_general | solution.py:58
  196.8 9.0 %all-to-all-start.2 = ((bf16[64,32,128]{2,0,1:T(8,128)(2,1)}), bf16[64,32,128]{2,0,1:T(8,128)(2,1)S(1)}, u32[]{:S(2)}, u32[]{:S(2)}) async-start(bf16[64,32,128]{2,0,1:T(8,128)(2,1)} %copy.39), calls=%async_computation.2 | async-start | bytes 1048576 | tf_op jit(solution)/shard_map/all_to_all | solution.py:161
  205.8 12.6 %all-to-all-done.2 = bf16[64,32,128]{2,0,1:T(8,128)(2,1)S(1)} async-done(((bf16[64,32,128]{2,0,1:T(8,128)(2,1)}), bf16[64,32,128]{2,0,1:T(8,128)(2,1)S(1)}, u32[]{:S(2)}, u32[]{:S(2)}) %all-to-all-start.2) | async-done | bytes 524320 | tf_op jit(solution)/shard_map/all_to_all | solution.py:161
  218.5 8.1 %while.71 = (s32[]{:T(128)}, bf16[2,64,1024]{2,1,0:T(8,128)(2,1)S(1)}, s32[2]{0:T(128)S(1)}, s32[2048]{0:T(1024)S(1)}, bf16[64,4096]{1,0:T(8,128)(2,1)S(1)}, /*index=5*/s32[]{:T(128)}, s32[1]{0:T(128)}, s32[]{:T(128)}, s32[]{:T(128)}) while((s32[]{:T(128)}, bf16[2,64,1024]{2,1,0:T(8,128)(2,1)S(1)}, s32[2]{0:T(128)S(1)}, ...), condition=%wide.region_7.8_spmd.clone, body=%wide.region_6.7_spmd.clone.sunk | while | flops 541065216 | bytes 798879 | solution.py:60
  219.7 2.8 fusion.362
  223.8 2.8 fusion.362
  226.7 5.7 %collective-permute-start.8 = (bf16[64,256]{1,0:T(8,128)(2,1)S(1)}, bf16[64,256]{1,0:T(8,128)(2,1)S(1)}, u32[]{:S(2)}, u32[]{:S(2)}) collective-permute-start(bf16[64,256]{1,0:T(8,128)(2,1)S(1)} %get-tuple-element.488), channel_id=1, source_target_pairs={{0,1},{1,2},{2,3},{3,4},{4,5},{5,6},{6,7},{7,8},{8,9},{9,10},{10,1... | collective-permute-start | bytes 98312 | tf_op jit(solution)/shard_map/ppermute | solution.py:19
  234.4 6.9 %collective-permute-done.9 = bf16[64,256]{1,0:T(8,128)(2,1)S(1)} collective-permute-done((bf16[64,256]{1,0:T(8,128)(2,1)S(1)}, bf16[64,256]{1,0:T(8,128)(2,1)S(1)}, u32[]{:S(2)}, u32[]{:S(2)}) %collective-permute-start.9) | collective-permute-done | bytes 32800 | tf_op jit(solution)/shard_map/ppermute | solution.py:21
  241.3 45.1 %while.72 = (s32[]{:T(128)}, f32[8,64,256]{2,1,0:T(8,128)S(1)}, s32[8]{0:T(128)S(1)}, bf16[64,2560]{1,0:T(8,128)(2,1)S(1)}, s32[9,2048]{1,0:T(8,128)}, /*index=5...) while((s32[]{:T(128)}, f32[8,64,256]{2,1,0:T(8,128)S(1)}, ...), condition=%wide.region_9.10_spmd.clone.clone, body=%wide.region_8.9_spmd.clone.clone.sunk | while | flops 247417088 | bytes 2192624 | solution.py:92
  288.7 3.4 collective-permute-start.11
  294.0 3.4 %collective-permute-done.11 = bf16[64,256]{1,0:T(8,128)(2,1)S(1)} collective-permute-done((bf16[64,256]{1,0:T(8,128)(2,1)S(1)}, bf16[64,256]{1,0:T(8,128)(2,1)S(1)}, u32[]{:S(2)}, u32[]{:S(2)}) %collective-permute-start.11) | collective-permute-done | bytes 32800 | tf_op jit(solution)/shard_map/ppermute | solution.py:21
  297.6 45.0 %while.73 = (s32[]{:T(128)}, f32[8,64,256]{2,1,0:T(8,128)S(1)}, s32[8]{0:T(128)S(1)}, bf16[64,2560]{1,0:T(8,128)(2,1)S(1)}, s32[9,2048]{1,0:T(8,128)}, /*index=5...) while((s32[]{:T(128)}, f32[8,64,256]{2,1,0:T(8,128)S(1)}, ...), condition=%wide.region_11.12_spmd.clone.clone, body=%wide.region_10.11_spmd.clone.clone.sunk | while | flops 247417088 | bytes 2192624 | solution.py:92
  (338 shorter events, 169.3 us)
Async XLA Ops:
  1.5 32.5 %copy-start.5 = (s32[1,4096]{1,0:T(1,128)S(1)}, s32[1,4096]{1,0:T(1,128)}, u32[]{:S(2)}) copy-start(s32[1,4096]{1,0:T(1,128)} %param.30) | copy-start | bytes 49156
  24.4 9.6 %all-to-all-start.1 = ((bf16[32,1,128]{2,1,0:T(2,128)(2,1)}), bf16[32,1,128]{2,1,0:T(2,128)(2,1)S(1)}, u32[]{:S(2)}, u32[]{:S(2)}) async-start(bf16[32,1,128]{2,1,0:T(2,128)(2,1)} %bitcast.3), calls=%async_computation.1 | async-start | bytes 32768 | tf_op jit(solution)/shard_map/all_to_all | solution.py:131
  34.0 46.7 %copy-start = (bf16[64,24,512]{2,1,0:T(8,128)(2,1)S(1)}, bf16[64,24,512]{2,1,0:T(8,128)(2,1)}, u32[]{:S(2)}) copy-start(bf16[64,24,512]{2,1,0:T(8,128)(2,1)} %param.22) | copy-start | bytes 4718596
  34.0 46.7 %copy-start.6 = (f32[64]{0:T(128)S(1)}, f32[64]{0:T(128)}, u32[]{:S(2)}) copy-start(f32[64]{0:T(128)} %param.24) | copy-start | bytes 772
  80.5 6.2 %copy-start.2 = (bf16[3,3,64,64]{3,2,1,0:T(8,128)(2,1)S(1)}, bf16[3,3,64,64]{3,2,1,0:T(8,128)(2,1)}, u32[]{:S(2)}) copy-start(bf16[3,3,64,64]{3,2,1,0:T(8,128)(2,1)} %param.25) | copy-start | bytes 221188
  81.4 5.9 %collective-permute-start = (bf16[64,1,512]{2,0,1:T(8,128)(2,1)S(1)}, bf16[64,1,512]{2,0,1:T(8,128)(2,1)S(1)}, u32[]{:S(2)}, u32[]{:S(2)}) collective-permute-start(bf16[64,1,512]{2,0,1:T(8,128)(2,1)S(1)} %get-tuple-element.484), channel_id=1, source_target_pairs={{0,1},{1,2},{2,3},{3,4},{4,5},{5,6},{6,7},{8,9},{9,10},{10,11},{11... | collective-permute-start | bytes 196616 | tf_op jit(solution)/shard_map/ppermute | solution.py:19
  82.7 5.7 %collective-permute-start.1 = (bf16[64,1,512]{2,0,1:T(8,128)(2,1)S(1)}, bf16[64,1,512]{2,0,1:T(8,128)(2,1)S(1)}, u32[]{:S(2)}, u32[]{:S(2)}) collective-permute-start(bf16[64,1,512]{2,0,1:T(8,128)(2,1)S(1)} %get-tuple-element.485), channel_id=1, source_target_pairs={{1,0},{2,1},{3,2},{4,3},{5,4},{6,5},{7,6},{9,8},{10,9},{11,10},{12... | collective-permute-start | bytes 196616 | tf_op jit(solution)/shard_map/ppermute | solution.py:21
  88.7 9.0 %collective-permute-start.2 = (bf16[64,26,1]{2,0,1:T(8,128)(2,1)S(1)}, bf16[64,26,1]{2,0,1:T(8,128)(2,1)S(1)}, u32[]{:S(2)}, u32[]{:S(2)}) collective-permute-start(bf16[64,26,1]{2,0,1:T(8,128)(2,1)S(1)} %get-tuple-element.481), channel_id=1, source_target_pairs={{0,8},{8,16},{16,24},{24,0},{1,9},{9,17},{17,25},{25,1},{2,10},{10... | collective-permute-start | bytes 9992 | tf_op jit(solution)/shard_map/ppermute | solution.py:19
  90.4 11.3 %collective-permute-start.3 = (bf16[64,26,1]{2,0,1:T(8,128)(2,1)S(1)}, bf16[64,26,1]{2,0,1:T(8,128)(2,1)S(1)}, u32[]{:S(2)}, u32[]{:S(2)}) collective-permute-start(bf16[64,26,1]{2,0,1:T(8,128)(2,1)S(1)} %get-tuple-element.480), channel_id=1, source_target_pairs={{8,0},{16,8},{24,16},{0,24},{9,1},{17,9},{25,17},{1,25},{10,2},{18... | collective-permute-start | bytes 9992 | tf_op jit(solution)/shard_map/ppermute | solution.py:21
  111.4 11.1 %copy-start.3 = (bf16[3,3,64,64]{3,2,1,0:T(8,128)(2,1)S(1)}, bf16[3,3,64,64]{3,2,1,0:T(8,128)(2,1)}, u32[]{:S(2)}) copy-start(bf16[3,3,64,64]{3,2,1,0:T(8,128)(2,1)} %param.26) | copy-start | bytes 221188
  116.5 6.5 %collective-permute-start.4 = (bf16[64,1,512]{2,0,1:T(8,128)(2,1)S(1)}, bf16[64,1,512]{2,0,1:T(8,128)(2,1)S(1)}, u32[]{:S(2)}, u32[]{:S(2)}) collective-permute-start(bf16[64,1,512]{2,0,1:T(8,128)(2,1)S(1)} %get-tuple-element.482), channel_id=1, source_target_pairs={{0,1},{1,2},{2,3},{3,4},{4,5},{5,6},{6,7},{8,9},{9,10},{10,11},{11... | collective-permute-start | bytes 196616 | tf_op jit(solution)/shard_map/ppermute | solution.py:19
  117.8 6.9 %collective-permute-start.5 = (bf16[64,1,512]{2,0,1:T(8,128)(2,1)S(1)}, bf16[64,1,512]{2,0,1:T(8,128)(2,1)S(1)}, u32[]{:S(2)}, u32[]{:S(2)}) collective-permute-start(bf16[64,1,512]{2,0,1:T(8,128)(2,1)S(1)} %get-tuple-element.483), channel_id=1, source_target_pairs={{1,0},{2,1},{3,2},{4,3},{5,4},{6,5},{7,6},{9,8},{10,9},{11,10},{12... | collective-permute-start | bytes 196616 | tf_op jit(solution)/shard_map/ppermute | solution.py:21
  125.0 9.2 %collective-permute-start.6 = (bf16[64,26,1]{2,0,1:T(8,128)(2,1)S(1)}, bf16[64,26,1]{2,0,1:T(8,128)(2,1)S(1)}, u32[]{:S(2)}, u32[]{:S(2)}) collective-permute-start(bf16[64,26,1]{2,0,1:T(8,128)(2,1)S(1)} %get-tuple-element.477), channel_id=1, source_target_pairs={{0,8},{8,16},{16,24},{24,0},{1,9},{9,17},{17,25},{25,1},{2,10},{10... | collective-permute-start | bytes 9992 | tf_op jit(solution)/shard_map/ppermute | solution.py:19
  126.0 10.9 %collective-permute-start.7 = (bf16[64,26,1]{2,0,1:T(8,128)(2,1)S(1)}, bf16[64,26,1]{2,0,1:T(8,128)(2,1)S(1)}, u32[]{:S(2)}, u32[]{:S(2)}) collective-permute-start(bf16[64,26,1]{2,0,1:T(8,128)(2,1)S(1)} %get-tuple-element.476), channel_id=1, source_target_pairs={{8,0},{16,8},{24,16},{0,24},{9,1},{17,9},{25,17},{1,25},{10,2},{18... | collective-permute-start | bytes 9992 | tf_op jit(solution)/shard_map/ppermute | solution.py:21
  194.1 24.3 %copy-start.4 = (s32[2048]{0:T(1024)S(1)}, s32[2048]{0:T(1024)}, u32[]{:S(2)}) copy-start(s32[2048]{0:T(1024)} %get-tuple-element.907) | copy-start | bytes 24580
  196.8 21.6 %all-to-all-start.2 = ((bf16[64,32,128]{2,0,1:T(8,128)(2,1)}), bf16[64,32,128]{2,0,1:T(8,128)(2,1)S(1)}, u32[]{:S(2)}, u32[]{:S(2)}) async-start(bf16[64,32,128]{2,0,1:T(8,128)(2,1)} %copy.39), calls=%async_computation.2 | async-start | bytes 1048576 | tf_op jit(solution)/shard_map/all_to_all | solution.py:161
  218.4 8.2 %copy-start.1 = (bf16[64,2048]{1,0:T(8,128)(2,1)S(1)}, bf16[64,2048]{1,0:T(8,128)(2,1)}, u32[]{:S(2)}) copy-start(bf16[64,2048]{1,0:T(8,128)(2,1)} %param.23) | copy-start | bytes 786436
  226.5 14.8 %copy-start.7 = (bf16[9,64,64]{2,1,0:T(8,128)(2,1)S(1)}, bf16[9,64,64]{2,1,0:T(8,128)(2,1)}, u32[]{:S(2)}) copy-start(bf16[9,64,64]{2,1,0:T(8,128)(2,1)} %param.27) | copy-start | bytes 221188
  226.7 7.6 %collective-permute-start.8 = (bf16[64,256]{1,0:T(8,128)(2,1)S(1)}, bf16[64,256]{1,0:T(8,128)(2,1)S(1)}, u32[]{:S(2)}, u32[]{:S(2)}) collective-permute-start(bf16[64,256]{1,0:T(8,128)(2,1)S(1)} %get-tuple-element.488), channel_id=1, source_target_pairs={{0,1},{1,2},{2,3},{3,4},{4,5},{5,6},{6,7},{7,8},{8,9},{9,10},{10,1... | collective-permute-start | bytes 98312 | tf_op jit(solution)/shard_map/ppermute | solution.py:19
  232.4 8.8 %collective-permute-start.9 = (bf16[64,256]{1,0:T(8,128)(2,1)S(1)}, bf16[64,256]{1,0:T(8,128)(2,1)S(1)}, u32[]{:S(2)}, u32[]{:S(2)}) collective-permute-start(bf16[64,256]{1,0:T(8,128)(2,1)S(1)} %get-tuple-element.489), channel_id=1, source_target_pairs={{1,0},{2,1},{3,2},{4,3},{5,4},{6,5},{7,6},{8,7},{9,8},{10,9},{11,1... | collective-permute-start | bytes 98312 | tf_op jit(solution)/shard_map/ppermute | solution.py:21
  286.5 11.1 %copy-start.8 = (bf16[9,64,64]{2,1,0:T(8,128)(2,1)S(1)}, bf16[9,64,64]{2,1,0:T(8,128)(2,1)}, u32[]{:S(2)}) copy-start(bf16[9,64,64]{2,1,0:T(8,128)(2,1)} %param.28) | copy-start | bytes 221188
  286.7 7.3 %collective-permute-start.10 = (bf16[64,256]{1,0:T(8,128)(2,1)S(1)}, bf16[64,256]{1,0:T(8,128)(2,1)S(1)}, u32[]{:S(2)}, u32[]{:S(2)}) collective-permute-start(bf16[64,256]{1,0:T(8,128)(2,1)S(1)} %get-tuple-element.486), channel_id=1, source_target_pairs={{0,1},{1,2},{2,3},{3,4},{4,5},{5,6},{6,7},{7,8},{8,9},{9,10},{10,1... | collective-permute-start | bytes 98312 | tf_op jit(solution)/shard_map/ppermute | solution.py:19
  288.7 8.8 %collective-permute-start.11 = (bf16[64,256]{1,0:T(8,128)(2,1)S(1)}, bf16[64,256]{1,0:T(8,128)(2,1)S(1)}, u32[]{:S(2)}, u32[]{:S(2)}) collective-permute-start(bf16[64,256]{1,0:T(8,128)(2,1)S(1)} %get-tuple-element.487), channel_id=1, source_target_pairs={{1,0},{2,1},{3,2},{4,3},{5,4},{6,5},{7,6},{8,7},{9,8},{10,9},{11,1... | collective-permute-start | bytes 98312 | tf_op jit(solution)/shard_map/ppermute | solution.py:21
where the time goes:
time: 351 us; the launch traced here: 344 us
  matrix products  169 us (48%)
  waiting for transfers between devices  48 us (14%)
  starting transfers between devices  43 us (12%)
  local copies, waits for them, and re-layouts  28.4 us (8%)
  loops' own time  26.6 us (8%)
  other arithmetic  18.3 us (5%)
  blocking collectives  8.76 us (2%)
    dot_general x144, matrix products, neighbour_one_block(): jnp.dot(weight[tap], picked, preferred_element_type=jnp.float32)  57.1 us
    dot_general x6, matrix products, pick_one_block(): return jnp.dot(data, select, preferred_element_type=jnp.float32)  40.2 us
    dot_general x16, matrix products, add_one_block(): return jnp.dot(data, select, preferred_element_type=jnp.float32)  39.9 us
    dot_general x18, matrix products, valid_conv(): jnp.einsum('oc,crw->orw', weight[row_tap, col_tap], window, preferred_ele...  31.9 us
    ppermute x6, waiting for transfers between devices, with_halo(): lax.ppermute(head, axis, [((i + 1) % count, i) for i in range(ends)])  19.8 us
    ppermute x6, starting transfers between devices, with_halo(): lax.ppermute(head, axis, [((i + 1) % count, i) for i in range(ends)])  14.3 us
    ppermute x6, waiting for transfers between devices, with_halo(): lax.ppermute(tail, axis, [(i, (i + 1) % count) for i in range(ends)])  12.9 us
    ppermute x6, starting transfers between devices, with_halo(): lax.ppermute(tail, axis, [(i, (i + 1) % count) for i in range(ends)])  12.9 us
  transfers between devices with their start and end apart: 14, of which 10 were waited for; matrix products, arithmetic and copies ran while one was open for 2% of the time, Pallas kernels for 0%

commit v1 on v0

v1 whole, which is shorter than its diff:
```python
import jax
import jax.numpy as jnp
import numpy as np
from jax import lax
from jax.experimental import pallas as pl
from jax.experimental.pallas import tpu as pltpu
from jax.sharding import PartitionSpec as P

HALO = 256
LANES = 128
BF = jnp.bfloat16
F32 = jnp.float32
NEIGHBOURS = ((0, 0), (-1, 0), (1, 0), (0, -1), (0, 1), (-1, -1), (1, -1), (-1, 1), (1, 1))
VMEM_LIMIT = 20 * 1024 * 1024
VMEM_WHOLE = 60 * 1024 * 1024

VMEM = pl.BlockSpec(memory_space=pltpu.VMEM)
ANY = pl.BlockSpec(memory_space=pl.ANY)
HBM = pl.BlockSpec(memory_space=pltpu.HBM)


def call(body, outs, ins, scratch=(), parts=None, untouched=(), out_specs=None, limit=VMEM_LIMIT):
    parts = parts or {}
    held = [i for i in range(len(ins)) if i not in untouched]
    shapes = [
        tuple(len(range(*cut.indices(n))) for cut, n in zip(parts[i], ins[i].shape))
        if i in parts
        else ins[i].shape
        for i in held
    ]
    count = len(jax.tree.leaves(outs))

    def kernel(*refs):
        sources, refs = refs[: len(ins)], refs[len(ins) :]
        results, refs = refs[:count], refs[count:]
        copies, refs, done = refs[: len(held)], refs[len(held) : -1], refs[-1]
        moves = {}
        for k, i in enumerate(held):
            source = sources[i].at[parts[i]] if i in parts else sources[i]
            moves[i] = pltpu.make_async_copy(source, copies[k], done.at[k])
            moves[i].start()
        waiting = set(held)

        def wait(*which):
            for i in which:
                waiting.remove(i)
                moves[i].wait()

        body(wait, *copies, *results, *refs)
        assert not waiting

    return pl.pallas_call(
        kernel,
        out_shape=outs,
        in_specs=[ANY] * len(ins),
        out_specs=out_specs or jax.tree.map(lambda _: VMEM, outs),
        scratch_shapes=[pltpu.VMEM(shape, ins[i].dtype) for shape, i in zip(shapes, held)]
        + list(scratch)
        + [pltpu.SemaphoreType.DMA((len(held),))],
        compiler_params=pltpu.CompilerParams(vmem_limit_bytes=limit),
    )(*ins)


def one_hot(index_row, size):
    places = lax.broadcasted_iota(jnp.int32, (size, index_row.shape[1]), 0)
    return jnp.where(places == index_row, 1.0, 0.0).astype(BF)


def nt_dot(a, b):
    return lax.dot_general(a, b, (((1,), (1,)), ((), ())), preferred_element_type=F32)


def gelu(x):
    inner = x * (0.7978845608028654 + 0.035677408136300125 * (x * x))
    return (0.5 * x) * (1.0 + jnp.tanh(inner))


def slot_values(heat_ref, slot_ref, rows):
    heat = heat_ref[...].astype(F32)[0:1]
    slot = slot_ref[...]
    places = lax.broadcasted_iota(jnp.int32, (rows, slot.shape[1]), 0)
    match = places == (slot >> 7)
    left = jnp.concatenate([jnp.where(match, heat, 0.0), jnp.where(match, 1.0, 0.0)], axis=0)
    return nt_dot(left.astype(BF), one_hot(slot & 127, LANES))


def or_inf(value, live):
    return jnp.where(live > 0.5, value, jnp.inf).astype(BF)


def slot_table_body(wait, heat_ref, slot_ref, out_ref):
    wait(0, 1)
    rows = out_ref.shape[0]
    table = slot_values(heat_ref, slot_ref, rows)
    out_ref[...] = or_inf(table[:rows], table[rows:])


def spread_table_body(wait, heat_ref, slot_ref, spread_ref, out_ref):
    wait(0, 1)
    count, rows = spread_ref.shape
    table = slot_values(heat_ref, slot_ref, rows)
    pair = jnp.concatenate([table[:rows], table[rows:]], axis=1).astype(BF)
    wait(2)
    spread = jnp.dot(spread_ref[...], pair, preferred_element_type=F32)
    out_ref[...] = or_inf(spread[:, :LANES], spread[:, LANES:]).reshape(out_ref.shape)


def neighbourhoods(faces, tiles):
    around = np.full((faces * tiles, 16), -1)
    for f in range(faces):
        for t in range(tiles):
            for n, (dr, dc) in enumerate(NEIGHBOURS):
                if 0 <= t + dr < tiles:
                    around[f * tiles + t, n] = (f + dc) % faces * tiles + t + dr
    return around


def heat_table(ocean, slots, capacity, faces, tiles):
    devices = faces * tiles
    around = neighbourhoods(faces, tiles)
    ins = [ocean, slots.reshape(1, -1)]
    if capacity == LANES:
        spread = (around.reshape(-1, 1) == np.arange(devices)).astype(np.float32)
        return call(
            spread_table_body,
            jax.ShapeDtypeStruct((devices, 16, LANES), BF),
            ins + [jnp.asarray(spread, BF)],
            parts={0: (slice(0, 16), slice(None))},
            limit=VMEM_WHOLE,
        )
    rows = devices * capacity // LANES
    out = jax.ShapeDtypeStruct((rows, LANES), BF)
    table = call(slot_table_body, out, ins, parts={0: (slice(0, 16), slice(None))})
    table = table.reshape(devices, capacity)
    return jnp.where((around >= 0)[:, :, None], table[np.maximum(around, 0)], jnp.inf).astype(BF)


def heat_slots(table, both):
    capacity = table.shape[2]
    got = lax.all_to_all(table, both, split_axis=0, concat_axis=0, tiled=True)
    if capacity != LANES:
        got = jnp.transpose(got, (1, 0, 2)).reshape(16, -1, LANES)
        got = jnp.transpose(got, (1, 0, 2))
    return got


def live_entry(value, cell, cols, rows, dr):
    live = value < jnp.inf
    value = jnp.where(live, value, 0.0)
    row, col = cell >> (cols.bit_length() - 1), cell & (cols - 1)
    if dr == -1:
        live = live & (row >= rows - 2)
    if dr == 1:
        live = live & (row < 2)
    return value, live, row + (rows * dr + 2), col


def for_chunks(count, many, body):
    def step(i, carry):
        for part in range(many):
            body(i * many + part)
        return carry

    lax.fori_loop(0, count // many, step, 0)


def lanes_at(e, width=LANES):
    return pl.ds(pl.multiple_of(e * width, width), width)


def scatter_body(
    wait, vals_ref, cell_ref, above_ref, below_ref, out_ref, targets, left, right, prod, prod_ends
):
    rows, cols = out_ref.shape[0] - 8, out_ref.shape[1]
    blocks = cols // LANES
    span = rows * blocks
    wait(2, 3)
    targets[0] = decoded(above_ref[0:64, cols:])
    targets[1] = decoded(below_ref[0:64, cols:])
    wait(0, 1)

    def chunk(e):
        lanes = lanes_at(e)
        values = vals_ref[e].astype(F32)
        for n, (dr, _) in enumerate(NEIGHBOURS[:3]):
            cell = targets[n - 1, pl.ds(e, 1), :] if n else cell_ref[:, lanes]
            value, live, row, col = live_entry(values[n : n + 1], cell, cols, rows, dr)
            block = col >> 7
            if n == 0:
                high, size, start = block * rows + row - 2, span, 0
            else:
                high, size = 2 * block + row - (0 if dr < 0 else rows + 2), 8
                start = 2 * span + 16 * (n - 1)
            match = lax.broadcasted_iota(jnp.int32, (size, LANES), 0) == jnp.where(live, high, -1)
            left[start : start + 2 * size, lanes] = jnp.concatenate(
                [jnp.where(match, value, 0.0), jnp.where(match, 1.0, 0.0)], axis=0
            ).astype(BF)
            right[n * LANES : (n + 1) * LANES, lanes] = one_hot(col & 127, LANES)

    for_chunks(vals_ref.shape[0], 2, chunk)
    prod[...] = nt_dot(left[0 : 2 * span], right[0:LANES])
    prod_ends[...] = nt_dot(left[2 * span :], right[LANES:])

    def mean(ref, first, count, rows_on, lanes):
        return ref[first : first + count, lanes] / jnp.maximum(
            ref[first + rows_on : first + rows_on + count, lanes], 1.0
        )

    first, second = slice(0, LANES), slice(LANES, 2 * LANES)
    for b in range(blocks):
        to = slice(b * LANES, (b + 1) * LANES)
        out_ref[2 : rows + 2, to] = mean(prod, b * rows, rows, span, first)
        out_ref[0:2, to] = mean(prod_ends, 2 * b, 2, 8, first)
        out_ref[rows + 2 : rows + 4, to] = mean(prod_ends, 16 + 2 * b, 2, 8, second)


def scatter_heat(vals, cells, above, below, rows):
    slots = cells.size
    cols = above.shape[1] - LANES
    span = rows * (cols // LANES)
    return call(
        scatter_body,
        jax.ShapeDtypeStruct((rows + 8, cols), F32),
        [vals, cells, above, below],
        scratch=[
            pltpu.VMEM((2, slots // LANES, LANES), jnp.int32),
            pltpu.VMEM((2 * span + 32, slots), BF),
            pltpu.VMEM((3 * LANES, slots), BF),
            pltpu.VMEM((2 * span, LANES), F32),
            pltpu.VMEM((32, 2 * LANES), F32),
        ],
    )


def scatter_beside(vals_ref, west_ref, east_ref, targets, left, right, rows, cols):
    for ref, places in ((west_ref, (0, 2, 3)), (east_ref, (1, 4, 5))):
        first = ref.shape[0] - 3 * 64
        for part, place in enumerate(places):
            targets[place] = decoded(ref[first + 64 * part : first + 64 * (part + 1)])

    def chunk(e):
        lanes = lanes_at(e)
        values = vals_ref[e].astype(F32)
        place = lax.broadcasted_iota(jnp.int32, (64, LANES), 0)
        halves = [jnp.zeros((64, LANES), F32)] * 2
        heats = []
        for k, (dr, dc) in enumerate(NEIGHBOURS[3:]):
            value, live, row, col = live_entry(
                values[k + 3 : k + 4], targets[k, pl.ds(e, 1), :], cols, rows, dr
            )
            side = 0 if dc < 0 else 1
            col = col if side else col - (cols - 2)
            live = live & ((col < 2) if side else (col >= 0))
            code = jnp.where(live, 2 * row + col, -1)
            halves[side] = jnp.where(place == code, 1.0, halves[side])
            heats += [value, jnp.where(live, 1.0, 0.0)]
        heats.append(jnp.zeros((16 - len(heats), LANES), F32))
        left[:, lanes] = jnp.concatenate(heats, axis=0).astype(BF)
        right[:, lanes] = jnp.concatenate(halves, axis=0).astype(BF)

    for_chunks(vals_ref.shape[0], 2, chunk)
    prod = nt_dot(left[...], right[...])
    lane = lax.broadcasted_iota(jnp.int32, (1, LANES), 1)
    place = lane & 63
    around = jnp.zeros((1, LANES), F32)
    for k, (dr, dc) in enumerate(NEIGHBOURS[3:]):
        first, last = {-1: (0, 4), 0: (4, 2 * rows + 4), 1: (2 * rows + 4, 2 * rows + 8)}[dr]
        here = (place >= first) & (place < last) & ((lane >= 64) == (dc > 0))
        mean = prod[2 * k : 2 * k + 1] / jnp.maximum(prod[2 * k + 1 : 2 * k + 2], 1.0)
        around = jnp.where(here, mean, around)
    return around


def end_columns(field):
    high, cols = field.shape
    row = lax.broadcasted_iota(jnp.int32, (high, LANES), 0)
    lane = lax.broadcasted_iota(jnp.int32, (high, LANES), 1)
    here = row < high - 4
    own = jnp.where(here & (lane == 2 * row), field[:, 0:1], 0.0) + jnp.where(
        here & (lane == 2 * row + 65), field[:, cols - 1 : cols], 0.0
    )
    return jnp.sum(own, axis=0, keepdims=True)


def coded(cells):
    return jnp.concatenate([cells >> 7, cells & 127], axis=0).astype(BF)


def decoded(code):
    half = code.shape[0] // 2
    return (code[:half].astype(F32) * 128.0 + code[half:].astype(F32)).astype(jnp.int32)


def side_body(
    wait, first_ref, last_ref, above_ref, below_ref, cell_ref, west_ref, east_ref
):
    rows, channels, _ = first_ref.shape
    cols = above_ref.shape[1] - LANES
    wait(0, 1, 2, 3, 4)

    def column(i, lanes, air_ref):
        if i < 2:
            return above_ref[i * channels : (i + 1) * channels, lanes]
        if i < rows + 2:
            return air_ref[i - 2]
        i = i - rows - 2
        return below_ref[i * channels : (i + 1) * channels, lanes]

    lane = lax.broadcasted_iota(jnp.int32, (channels, LANES), 1)
    for ref, air_ref, lanes, shift, half in (
        (west_ref, first_ref, slice(0, LANES), 0, 0),
        (east_ref, last_ref, slice(cols - LANES, cols), 66, 32),
    ):
        total = jnp.zeros((channels, LANES), F32)
        for i in range(rows + 4):
            moved = pltpu.roll(column(i, lanes, air_ref).astype(F32), (2 * i + shift) % LANES, 1)
            total = jnp.where(lane >> 1 == i + half, moved, total)
        ref[0:channels] = total.astype(BF)
        first = channels
        for part in (coded(cell_ref[...]), above_ref[0:64, cols:], below_ref[0:64, cols:]):
            ref[first : first + 64] = part
            first += 64


def sides(air, above, below, cells):
    channels, cols = air.shape[1:]
    every = slice(None)
    return call(
        side_body,
        (jax.ShapeDtypeStruct((channels + 3 * 64, LANES), BF),) * 2,
        [air, air, above, below, cells],
        parts={0: (every, every, slice(0, LANES)), 1: (every, every, slice(cols - LANES, cols))},
    )


def shifted(center, from_left, from_right, at_left, at_right, left_lane, right_lane):
    width = center.shape[1]
    left = pltpu.roll(from_left, 1, 1)
    right = pltpu.roll(from_right, width - 1, 1)
    lane = lax.broadcasted_iota(jnp.int32, at_left.shape, 1)
    first = jnp.where(lane == 0, pltpu.roll(at_left, LANES - left_lane, 1), left[:, :LANES])
    last = jnp.where(
        lane == LANES - 1, pltpu.roll(at_right, LANES - 1 - right_lane, 1), right[:, -LANES:]
    )
    left = jnp.concatenate([first, left[:, LANES:]], axis=1)
    right = jnp.concatenate([right[:, :-LANES], last], axis=1)
    return center + (left + right)


def stack_weight(weight_ref, out):
    taps, _, channels, _ = weight_ref.shape
    none = jnp.zeros((channels, channels), F32)
    for u in range(taps):
        rows = [weight_ref[p, u].astype(F32) for p in range(taps)]
        for k, line in enumerate((rows + [none], [none] + rows)):
            first = (k * taps + u) * channels
            out[first : first + channels] = jnp.concatenate(line, axis=1).astype(BF)


def atmosphere_body(
    wait, air_ref, above_ref, below_ref, west_ref, east_ref, own_west_ref, own_east_ref, field,
    vals_ref, cell_ref, heat_weight_ref, weight1_ref, weight2_ref,
    next_out, send_ref,
    next_ref, out_done, start, hidden, edge1, edge2, first_ref, second_ref, targets, left, right,
):
    rows, channels, cols = next_ref.shape
    taps = 3 * channels
    tile, tiles = lax.axis_index("tile"), lax.axis_size("tile")
    edge_ref = [jnp.where(tile > 0, 1.0, 0.0), jnp.where(tile < tiles - 1, 1.0, 0.0)]
    wait(3, 4, 8)
    around = scatter_beside(vals_ref, west_ref, east_ref, targets, left, right, rows, cols)
    wait(11, 12)
    stack_weight(weight1_ref, first_ref)
    stack_weight(weight2_ref, second_ref)
    wait(0, 1, 2, 5, 6, 7, 9, 10)
    lane = lax.broadcasted_iota(jnp.int32, (channels, LANES), 1)
    row = lax.broadcasted_iota(jnp.int32, (channels, channels), 0)
    same = row == lax.broadcasted_iota(jnp.int32, (channels, channels), 1)
    weights = jnp.sum(jnp.where(same, heat_weight_ref[...], 0.0), axis=1, keepdims=True)
    heat_weight = jnp.broadcast_to(weights, (channels, cols))

    beside = jnp.where(
        lane < 64, east_ref[0:channels].astype(F32), west_ref[0:channels].astype(F32)
    )
    beside = pltpu.roll(beside, 64, 1)
    own = own_west_ref[0:channels].astype(F32) + own_east_ref[0:channels].astype(F32)
    narrow = heat_weight[:, 0:LANES]
    beside = beside + narrow * around
    own = own + narrow * end_columns(field[...])

    def three_rows(x):
        return jnp.concatenate(
            [x, pltpu.roll(x, LANES - 2, 1), pltpu.roll(x, LANES - 4, 1)], axis=0
        ).astype(BF)

    plain = jnp.dot(
        first_ref[0:taps, 0:taps],
        jnp.concatenate([three_rows(beside), three_rows(own)], axis=1),
        preferred_element_type=F32,
    )

    def tap(u, of_own):
        return plain[u * channels : (u + 1) * channels, of_own * LANES : (of_own + 1) * LANES]

    def back(x):
        return pltpu.roll(x, LANES - 1, 1)

    edge1[0] = tap(0, 0)
    edge1[1] = tap(2, 0)
    at_left = tap(0, 0) + back(tap(1, 0)) + tap(2, 1)
    at_right = back(tap(0, 1)) + tap(1, 0) + back(tap(2, 0))
    place = lane & 63
    inside = jnp.where(
        place == 0, edge_ref[0], jnp.where(place == 2 * (rows + 1), edge_ref[1], 1.0)
    )
    hidden_beside = gelu(jnp.where(lane < 64, at_left, at_right)) * inside
    plain = jnp.dot(
        second_ref[0:taps, 0:taps], three_rows(hidden_beside), preferred_element_type=F32
    )
    edge2[0] = plain[0:channels]
    edge2[1] = plain[2 * channels : taps]

    for i in range(2):
        for ref, r in ((above_ref, i), (below_ref, rows + 2 + i)):
            x = ref[i * channels : (i + 1) * channels, 0:cols].astype(F32)
            start[r] = (x + heat_weight * field[r : r + 1, :]).astype(BF)

    def first_stage(j):
        for k in range(2):
            r = 2 * j + k
            x = air_ref[r].astype(F32) + heat_weight * field[pl.ds(r + 2, 1), :]
            start[r + 2] = x.astype(BF)

    def mixed(weight_ref, source, j):
        window = source[pl.ds(2 * j, 4)].reshape(4 * channels, cols)
        return jnp.dot(weight_ref[...], window, preferred_element_type=F32)

    def parts(product, k):
        return [
            product[(3 * k + u) * channels : (3 * k + u + 1) * channels] for u in (1, 0, 2)
        ]

    def second_stage(j):
        product = mixed(first_ref, start, j)
        for k in range(2):
            h = 2 * j + k
            inside = jnp.where(h == 0, edge_ref[0], jnp.where(h == rows + 1, edge_ref[1], 1.0))
            total = shifted(*parts(product, k), edge1[0], edge1[1], 2 * h + 1, 64 + 2 * h)
            hidden[h] = (gelu(total) * inside).astype(BF)

    def third_stage(j):
        product = mixed(second_ref, hidden, j)
        for k in range(2):
            r = 2 * j + k
            total = shifted(*parts(product, k), edge2[0], edge2[1], 2 * r, 64 + 2 * r)
            next_ref[r] = (start[r + 2].astype(F32) + total).astype(BF)

    def steps(first, last, *stages):
        def step(j, carry):
            for stage, late in stages:
                stage(j - late)
            return carry

        lax.fori_loop(first, last, step, 0)

    half = rows // 2
    one, two, three = (first_stage, 0), (second_stage, 1), (third_stage, 3)
    steps(0, 1, one)
    steps(1, 3, two, one)
    steps(3, half, three, two, one)
    steps(half, half + 2, three, two)
    steps(half + 2, half + 3, three)


    copy = pltpu.make_async_copy(next_ref, next_out, out_done.at[0])
    copy.start()
    gather_cells(next_ref, cell_ref, send_ref)
    copy.wait()


def gather_cells(next_ref, cell_ref, send_ref):
    rows, channels, cols = next_ref.shape
    shift = cols.bit_length() - 1
    width = 256
    group = 6

    def pick(tile):
        cell = cell_ref[:, lanes_at(tile, width)]
        low = one_hot(cell & (cols - 1), cols)
        high = (cell >> shift).astype(F32).astype(BF)
        total = jnp.zeros((channels, width), BF)
        for g in range(0, rows, group):
            block = next_ref[g : g + group].reshape(group * channels, cols)
            got = jnp.dot(block, low, preferred_element_type=F32).astype(BF)
            for r in range(group):
                here = high == jnp.asarray(g + r, BF)
                total = jnp.where(here, got[r * channels : (r + 1) * channels], total)
        for part in range(width // LANES):
            send_ref[tile * (width // LANES) + part] = total[:, part * LANES : (part + 1) * LANES]

    for_chunks(cell_ref.shape[1] // width, 4, pick)


def atmosphere(
    air, above, below, west, east, to_west, to_east, field, vals, cells, heat_weight, first, second
):
    rows, channels, cols = air.shape
    slots = cells.size
    stacked = pltpu.VMEM((6 * channels, 4 * channels), BF)
    return call(
        atmosphere_body,
        (
            jax.ShapeDtypeStruct((rows, channels, cols), BF),
            jax.ShapeDtypeStruct((slots // LANES, channels, LANES), BF),
        ),
        [
            air, above, below, west, east, to_west, to_east, field, vals, cells,
            heat_weight.reshape(1, -1), first, second,
        ],
        out_specs=(HBM, VMEM),
        limit=VMEM_WHOLE,
        scratch=[
            pltpu.VMEM((rows, channels, cols), BF),
            pltpu.SemaphoreType.DMA((1,)),
            pltpu.VMEM((rows + 4, channels, cols), BF),
            pltpu.VMEM((rows + 2, channels, cols), BF),
            pltpu.VMEM((2, channels, LANES), F32),
            pltpu.VMEM((2, channels, LANES), F32),
            stacked,
            stacked,
            pltpu.VMEM((6, slots // LANES, LANES), jnp.int32),
            pltpu.VMEM((16, slots), BF),
            pltpu.VMEM((LANES, slots), BF),
        ],
    )


def forcing_body(
    wait, arrived_ref, slot_ref, ocean_ref, index_ref, out_ref, head_ref, tail_ref, table
):
    groups, channels, depth = table.shape
    wait(0, 1, 2, 3)
    parts = depth // LANES
    for g in range(groups):
        for p in range(parts):
            table[g, :, p * LANES : (p + 1) * LANES] = arrived_ref[g * parts + p]
    shift = depth.bit_length() - 1
    width = 256

    def block(b, carry):
        lanes = pl.ds(pl.multiple_of(b * width, width), width)
        slot = slot_ref[:, lanes]
        low = one_hot(slot & (depth - 1), depth)
        high = slot >> shift
        got = jnp.dot(
            table[...].reshape(groups * channels, depth), low, preferred_element_type=F32
        )
        total = got[0:channels]
        for g in range(1, groups):
            total = jnp.where(high == g, got[g * channels : (g + 1) * channels], total)
        out_ref[:, lanes] = (ocean_ref[:, lanes].astype(F32) + total).astype(BF)
        return carry

    channels, cells = ocean_ref.shape
    lax.fori_loop(0, cells // width, block, 0)
    reach = 2 * HALO
    for ref, first, start in ((head_ref, 0, 0), (tail_ref, cells - reach, cells - HALO)):
        ref[0:channels] = out_ref[:, first : first + reach]
        index = index_ref[:, start : start + HALO]
        far = index - start - lax.broadcasted_iota(jnp.int32, index.shape, 1)
        rest = jnp.zeros((ref.shape[0] - channels - index.shape[0], reach), F32)
        code = jnp.concatenate([far & (HALO - 1), far >> 8], axis=1).astype(F32)
        ref[channels:] = jnp.concatenate([code, rest], axis=0).astype(BF)


def add_forcing(arrived, slots, ocean, index, *ready):
    channels = ocean.shape[0]
    depth = 512
    end = jax.ShapeDtypeStruct((channels + 16, 2 * HALO), BF)
    return call(
        forcing_body,
        (jax.ShapeDtypeStruct(ocean.shape, BF), end, end),
        [arrived, slots.reshape(1, -1), ocean, index, *ready],
        untouched=range(4, 4 + len(ready)),
        scratch=[pltpu.VMEM((arrived.shape[0] * LANES // depth, channels, depth), BF)],
    )


def neighbour_block(source, b, local, weight):
    channels, width = source.shape[1:]
    window = source[pl.ds(b, 3)].reshape(3 * channels, width)
    picked = []
    for k in range(local.shape[0]):
        where = local[k : k + 1, :]
        got = jnp.dot(window, one_hot(where & (width - 1), width), preferred_element_type=F32)
        high = where >> 8
        picked.append(
            jnp.where(
                high == 0,
                got[0:channels],
                jnp.where(high == 1, got[channels : 2 * channels], got[2 * channels :]),
            ).astype(BF)
        )
    return jnp.dot(weight, jnp.concatenate(picked, axis=0), preferred_element_type=F32)


def own_positions(index_ref, b):
    return index_ref[:, b * HALO : (b + 1) * HALO] - b * HALO


def hide_block(hidden, at, values, b, local, weight_ref, inside=None):
    mixed = gelu(neighbour_block(values, b, local, weight_ref[...]))
    hidden[at] = (mixed if inside is None else mixed * inside).astype(BF)


def inner_body(
    wait, own_ref, index_ref, first_ref, second_ref, hidden_ref, out_ref, values, local
):
    wait(0, 1, 2, 3)
    taps = index_ref.shape[0]
    blocks = values.shape[0]
    for b in range(blocks):
        values[b] = own_ref[:, b * HALO : (b + 1) * HALO]
    for b in range(blocks - 2):
        local[b, 0:taps] = own_positions(index_ref, b + 1)

    def hide(b, carry):
        hide_block(hidden_ref, b, values, b, local[b, 0:taps], first_ref)
        return carry

    lax.fori_loop(0, blocks - 2, hide, 0)

    def finish(b, carry):
        mixed = neighbour_block(hidden_ref, b, local[b + 1, 0:taps], second_ref[...])
        lanes = pl.ds(pl.multiple_of(b * HALO, HALO), HALO)
        out_ref[:, lanes] = (values[b + 2].astype(F32) + mixed).astype(BF)
        return carry

    lax.fori_loop(0, blocks - 4, finish, 0)


def ocean_inner(own, index, first, second):
    channels, cells = own.shape
    blocks = cells // HALO
    return call(
        inner_body,
        (
            jax.ShapeDtypeStruct((blocks - 2, channels, HALO), BF),
            jax.ShapeDtypeStruct((channels, cells - 4 * HALO), BF),
        ),
        [own, index, first, second],
        scratch=[
            pltpu.VMEM((blocks, channels, HALO), BF),
            pltpu.VMEM((blocks - 2, 16, HALO), jnp.int32),
        ],
    )


def outer_body(
    wait, own_ref, inner_ref, done_ref, before_ref, after_ref, index_ref, first_ref, second_ref,
    out_ref, values, hidden, local,
):
    width = HALO
    both = ("face", "tile")
    number, devices = lax.axis_index(both), lax.axis_size(both)
    edge_ref = [jnp.where(number > 0, 1.0, 0.0), jnp.where(number < devices - 1, 1.0, 0.0)]
    wait(*range(8))
    channels, blocks = own_ref.shape[0], own_ref.shape[1] // width
    taps = index_ref.shape[0]
    for b in range(2):
        lanes = slice(b * width, (b + 1) * width)
        values[b] = before_ref[0:channels, lanes]
        values[2 + b] = own_ref[:, lanes]
        values[4 + b] = own_ref[:, (blocks - 2 + b) * width : (blocks - 1 + b) * width]
        values[6 + b] = after_ref[0:channels, lanes]
        hidden[2 + b] = inner_ref[b]
        hidden[4 + b] = inner_ref[blocks - 4 + b]
    out_ref[:, 2 * width : (blocks - 2) * width] = done_ref[...]
    for i, b in enumerate((0, 1, blocks - 2, blocks - 1)):
        local[1 + i, 0:taps] = own_positions(index_ref, b)
    place = lax.broadcasted_iota(jnp.int32, (taps, width), 1)
    for i, ref in ((0, before_ref), (5, after_ref)):
        code = ref[channels:].astype(F32).astype(jnp.int32)[0:taps]
        local[i, 0:taps] = place + code[:, :width] + (code[:, width:] << 8)
    for at, first, i, inside in (
        (0, 0, 0, edge_ref[0]), (1, 1, 1, None), (6, 4, 4, None), (7, 5, 5, edge_ref[1])
    ):
        hide_block(hidden, at, values, first, local[i, 0:taps], first_ref, inside)
    for b, first, i in ((0, 0, 1), (1, 1, 2), (blocks - 2, 4, 3), (blocks - 1, 5, 4)):
        mixed = neighbour_block(hidden, first, local[i, 0:taps], second_ref[...])
        lanes = slice(b * width, (b + 1) * width)
        out_ref[:, lanes] = (own_ref[:, lanes].astype(F32) + mixed).astype(BF)


def flat_weight(weight):
    taps, out, inner = weight.shape
    return jnp.transpose(weight, (1, 0, 2)).reshape(out, taps * inner)


def ocean_outer(own, inner, done, before, after, index, first, second):
    channels = own.shape[0]
    return call(
        outer_body,
        jax.ShapeDtypeStruct(own.shape, BF),
        [own, inner, done, before, after, index, first, second],
        scratch=[
            pltpu.VMEM((8, channels, HALO), BF),
            pltpu.VMEM((8, channels, HALO), BF),
            pltpu.VMEM((6, 16, HALO), jnp.int32),
        ],
    )


def from_neighbours(low, high, axis, closed=False):
    count = lax.axis_size(axis)
    ends = count if closed else count - 1
    before = lax.ppermute(high, axis, [(i, (i + 1) % count) for i in range(ends)])
    after = lax.ppermute(low, axis, [((i + 1) % count, i) for i in range(ends)])
    return before, after


def shards(
    atmos,
    ocean,
    surface_heat_weight,
    air_conv_first_weight,
    air_conv_second_weight,
    marine_conv_first_weight,
    marine_conv_second_weight,
    marine_coupling_slot,
    coupling_air_cells,
    marine_neighbour_index,
):
    both = ("face", "tile")
    devices = lax.axis_size(both)
    faces, tiles = lax.axis_size("face"), lax.axis_size("tile")
    slot_space = coupling_air_cells.shape[1]
    capacity = slot_space // devices
    channels, rows, cols = atmos.shape

    own_cells = coupling_air_cells.reshape(-1, LANES)
    code = coded(own_cells)
    code = jnp.concatenate([code, jnp.zeros((2 * channels - code.shape[0], LANES), BF)], axis=0)

    def two_rows(first):
        two = jnp.transpose(atmos[:, first : first + 2], (1, 0, 2)).reshape(2 * channels, cols)
        return jnp.concatenate([two, code], axis=1)

    low, high, heats = lax.optimization_barrier((two_rows(0), two_rows(rows - 2), ocean))
    above, below = from_neighbours(low, high, "tile")

    table = heat_table(heats, marine_coupling_slot, capacity, faces, tiles)
    table, above = lax.optimization_barrier((table, above))
    heat = heat_slots(table, both)

    air = jnp.transpose(atmos, (1, 0, 2))
    to_west, to_east = sides(air, above, below, own_cells)
    west, east = from_neighbours(to_west, to_east, "face", closed=True)

    field = scatter_heat(heat, coupling_air_cells, above, below, rows)
    air_next, outgoing = atmosphere(
        air, above, below, west, east, to_west, to_east, field, heat, coupling_air_cells,
        surface_heat_weight, air_conv_first_weight, air_conv_second_weight,
    )
    air_out = jnp.transpose(air_next, (1, 0, 2))

    def by_device(blocks):
        many = LANES // capacity
        split = blocks.reshape(-1, channels, many, capacity)
        return jnp.transpose(split, (0, 2, 1, 3)).reshape(devices, channels, capacity)

    def by_lanes(blocks):
        many = LANES // capacity
        split = blocks.reshape(-1, many, channels, capacity)
        return jnp.transpose(split, (0, 2, 1, 3)).reshape(-1, channels, LANES)

    if capacity != LANES:
        outgoing = by_device(outgoing)
    arrived = lax.all_to_all(outgoing, both, split_axis=0, concat_axis=0, tiled=True)
    if capacity != LANES:
        arrived = by_lanes(arrived)

    first_mix = flat_weight(marine_conv_first_weight)
    second_mix = flat_weight(marine_conv_second_weight)
    ocean_start, head, tail = add_forcing(
        arrived, marine_coupling_slot, ocean, marine_neighbour_index, air_out, first_mix, second_mix
    )
    before, after = from_neighbours(head, tail, both)
    inner, done = ocean_inner(ocean_start, marine_neighbour_index, first_mix, second_mix)
    ocean_next = ocean_outer(
        ocean_start,
        inner,
        done,
        before,
        after,
        marine_neighbour_index,
        first_mix,
        second_mix,
    )
    return (air_out, ocean_next)


def solution(mesh):
    placed = (
        P(None, "tile", "face"),
        P(None, ("face", "tile")),
        P(),
        P(),
        P(),
        P(),
        P(),
        P(("face", "tile")),
        P(("face", "tile"), None),
        P(None, ("face", "tile")),
    )
    return jax.shard_map(
        shards,
        mesh=mesh,
        in_specs=placed,
        out_specs=(P(None, "tile", "face"), P(None, ("face", "tile"))),
        check_vma=False,
    )
```

time: 351 us -> 98.9 us (0.28)
  the two profiles are of different devices: /device:TPU:29 before, /device:TPU:1 now
where the time goes in v1:
time: 98.9 us; the launch traced here: 98.4 us
  Pallas kernels  41 us (41%)
  starting transfers between devices  29 us (29%)
  waiting for transfers between devices  20.2 us (20%)
  local copies, waits for them, and re-layouts  6.14 us (6%)
  between operations  1.13 us (1%)
    pallas_call x7, Pallas kernels, call(): pl.pallas_call(kernel, out_shape=outs, in_specs=[ANY] * len(ins), out_spe...  41 us
    all_to_all x1, waiting for transfers between devices, shards(): lax.all_to_all(outgoing, both, split_axis=0, concat_axis=0, tiled=True)  12.8 us
    ppermute x3, starting transfers between devices, from_neighbours(): lax.ppermute(high, axis, [(i, (i + 1) % count) for i in range(ends)])  8.8 us
    all_to_all x1, starting transfers between devices, heat_slots(): got = lax.all_to_all(table, both, split_axis=0, concat_axis=0, tiled=True)  8.1 us
    ppermute x3, starting transfers between devices, from_neighbours(): after = lax.ppermute(low, axis, [((i + 1) % count, i) for i in range(ends)])  6.83 us
    ppermute x3, waiting for transfers between devices, from_neighbours(): after = lax.ppermute(low, axis, [((i + 1) % count, i) for i in range(ends)])  6.68 us
    all_to_all x1, starting transfers between devices, shards(): lax.all_to_all(outgoing, both, split_axis=0, concat_axis=0, tiled=True)  5.31 us
    pallas_call x1, local copies, waits for them, and re-layouts, call(): pl.pallas_call(kernel, out_shape=outs, in_specs=[ANY] * len(ins), out_spe...  2.32 us
  transfers between devices with their start and end apart: 8, of which 3 were waited for; matrix products, arithmetic and copies ran while one was open for 3% of the time, Pallas kernels for 13%

profile of v1, /device:TPU:1, one launch (start us, length us, event | category | flops | bytes accessed | tf_op | source)
XLA Modules:
  0.0 98.4 jit_solution(8271280342754887849)
XLA Ops:
  0.6 0.0 copy-start.12
  0.6 0.8 shift-right-arithmetic_convert_fusion
  1.5 1.4 %slice_bitcast_fusion = (bf16[2,64,512]{2,0,1:T(2,128)(2,1)S(1)}, bf16[2,64,512]{2,0,1:T(2,128)(2,1)S(1)}) fusion(bf16[64,24,512]{2,1,0:T(8,128)(2,1)} %param.11), kind=kLoop, calls=%fused_computation.4 | loop fusion | bytes 524288 | tf_op jit(solution)/shard_map/transpose | solution.py:746
  3.0 4.0 %collective-permute-start = (bf16[128,640]{1,0:T(8,128)(2,1)S(1)}, bf16[128,640]{1,0:T(8,128)(2,1)S(1)}, u32[]{:S(2)}, u32[]{:S(2)}) collective-permute-start(bf16[128,640]{1,0:T(8,128)(2,1)S(1)} %get-tuple-element.17), channel_id=1, source_target_pairs={{0,1},{1,2},{2,3},{3,4},{4,5},{5,6},{6,7},{8,9},{9,10},{10,11},{11... | collective-permute-start | bytes 491528 | tf_op jit(solution)/shard_map/ppermute | solution.py:717
  7.0 2.1 %shard_map.122 = bf16[32,16,128]{2,1,0:T(8,128)(2,1)} custom-call(bf16[64,2048]{1,0:T(8,128)(2,1)} %refs_2_.2, s32[1,2048]{1,0:T(1,128)} %bitcast.26, bf16[512,32]{1,0:T(8,128)(2,1)} %constant.8.clone.refs_2_), custom_call_target="tpu_custom_call" | custom-call | tf_op jit(solution)/shard_map/pallas_call | solution.py:52
  9.1 0.7 collective-permute-done.refs_2_.refs_1_
  9.8 8.1 %all-to-all-start = ((bf16[32,16,128]{2,1,0:T(8,128)(2,1)}), bf16[32,16,128]{2,1,0:T(8,128)(2,1)S(1)}, u32[]{:S(2)}, u32[]{:S(2)}) async-start(bf16[32,16,128]{2,1,0:T(8,128)(2,1)} %shard_map.122), calls=%async_computation | async-start | bytes 262144 | tf_op jit(solution)/shard_map/all_to_all | solution.py:140
  17.9 0.0 copy-start.7
  17.9 1.3 %collective-permute-start.1 = (bf16[128,640]{1,0:T(8,128)(2,1)S(1)}, bf16[128,640]{1,0:T(8,128)(2,1)S(1)}, u32[]{:S(2)}, u32[]{:S(2)}) collective-permute-start(bf16[128,640]{1,0:T(8,128)(2,1)S(1)} %get-tuple-element.19), channel_id=1, source_target_pairs={{1,0},{2,1},{3,2},{4,3},{5,4},{6,5},{7,6},{9,8},{10,9},{11,10},{12... | collective-permute-start | bytes 491528 | tf_op jit(solution)/shard_map/ppermute | solution.py:718
  19.3 0.5 copy.34
  19.8 0.0 copy-start
  19.8 6.7 %collective-permute-done.1.refs_3_.refs_2_ = bf16[128,640]{1,0:T(8,128)(2,1)S(1)} collective-permute-done((bf16[128,640]{1,0:T(8,128)(2,1)S(1)}, bf16[128,640]{1,0:T(8,128)(2,1)S(1)}, u32[]{:S(2)}, u32[]{:S(2)}) %collective-permute-start.1) | collective-permute-done | bytes 163872 | tf_op jit(solution)/shard_map/ppermute | solution.py:718
  26.4 0.9 shard_map.123
  27.4 1.9 %collective-permute-start.2 = (bf16[256,128]{1,0:T(8,128)(2,1)S(1)}, bf16[256,128]{1,0:T(8,128)(2,1)S(1)}, u32[]{:S(2)}, u32[]{:S(2)}) collective-permute-start(bf16[256,128]{1,0:T(8,128)(2,1)S(1)} %get-tuple-element.20.refs_6_), channel_id=1, source_target_pairs={{0,8},{8,16},{16,24},{24,0},{1,9},{9,17},{17,25},{25,1},{2,10},{10... | collective-permute-start | bytes 196616 | tf_op jit(solution)/shard_map/ppermute | solution.py:717
  29.4 3.8 %shard_map.124.refs_7_ = f32[32,512]{1,0:T(8,128)S(1)} custom-call(bf16[32,16,128]{2,1,0:T(8,128)(2,1)S(1)} %all-to-all-done.refs_0_.refs_8_, s32[1,4096]{1,0:T(1,128)S(1)} %copy-done.7, bf16[128,640]{1,0:T(8,128)(2,1)S(1)} %collective-permute-done.refs_2_.refs_1_, bf16[128,640]{1,0:T(8,128)(2,1)S(1)} %collective-permute-done.1.refs_3_.refs_2_), custom_call_target="tpu_custom_call" | custom-call | tf_op jit(solution)/shard_map/pallas_call | solution.py:52
  33.2 0.6 copy-done.8
  33.8 0.6 copy-done.15
  34.4 0.0 copy-done.16
  34.4 19.9 %shard_map.125 = (bf16[24,64,512]{2,1,0:T(8,128)(2,1)}, bf16[32,64,128]{2,1,0:T(8,128)(2,1)}) custom-call(bf16[24,64,512]{2,1,0:T(8,128)(2,1)} %bitcast.21, bf16[128,640]{1,0:T(8,128)(2,1)} %copy-done.2, bf16[128,640]{1,0:T(8,128)(2,1)} %copy-done.3, bf16[256,128]{1,0:T(8,128)(2,1)} %copy-done.15, bf16[256,128]{1,0:T(8,128)(2,1)} %copy-done.16, ...), custom_call_target="tpu_custom_call" | custom-call | tf_op jit(solution)/shard_map/pallas_call | solution.py:52
  54.4 5.3 %all-to-all-start.1 = ((bf16[32,64,128]{2,1,0:T(8,128)(2,1)}), bf16[32,64,128]{2,1,0:T(8,128)(2,1)S(1)}, u32[]{:S(2)}, u32[]{:S(2)}) async-start(bf16[32,64,128]{2,1,0:T(8,128)(2,1)} %get-tuple-element.24), calls=%async_computation.1 | async-start | bytes 1048576 | tf_op jit(solution)/shard_map/all_to_all | solution.py:779
  59.7 0.1 copy.23
  59.9 0.1 copy.25.refs_5_.refs_2_.refs_6_
  60.0 0.1 copy.24
  60.2 0.1 copy.26.refs_6_.refs_3_.refs_7_
  60.3 0.0 copy-start.6
  60.4 2.3 %copy.33 = bf16[24,64,512]{2,0,1:T(8,128)(2,1)S(1)} copy(bf16[24,64,512]{2,1,0:T(8,128)(2,1)} %get-tuple-element.23) | data formatting | bytes 3145728 | tf_op jit(solution)/shard_map/pallas_call | solution.py:52
  62.7 12.8 %all-to-all-done.1.refs_0_ = bf16[32,64,128]{2,1,0:T(8,128)(2,1)S(1)} async-done(((bf16[32,64,128]{2,1,0:T(8,128)(2,1)}), bf16[32,64,128]{2,1,0:T(8,128)(2,1)S(1)}, u32[]{:S(2)}, u32[]{:S(2)}) %all-to-all-start.1) | async-done | bytes 524320 | tf_op jit(solution)/shard_map/all_to_all | solution.py:779
  75.5 2.8 %shard_map.126 = (bf16[64,2048]{1,0:T(8,128)(2,1)S(1)}, bf16[80,512]{1,0:T(8,128)(2,1)S(1)}, bf16[80,512]{1,0:T(8,128)(2,1)S(1)}) custom-call(bf16[32,64,128]{2,1,0:T(8,128)(2,1)S(1)} %all-to-all-done.1.refs_0_, s32[1,2048]{1,0:T(1,128)S(1)} %bitcast.27, bf16[64,2048]{1,0:T(8,128)(2,1)S(1)} %copy-done.6, s32[9,2048]{1,0:T(8,128)S(1)} %copy-done.5, ...), custom_call_target="tpu_custom_call" | custom-call | tf_op jit(solution)/shard_map/pallas_call | solution.py:52
  78.3 2.9 %collective-permute-start.4 = (bf16[80,512]{1,0:T(8,128)(2,1)S(1)}, bf16[80,512]{1,0:T(8,128)(2,1)S(1)}, u32[]{:S(2)}, u32[]{:S(2)}) collective-permute-start(bf16[80,512]{1,0:T(8,128)(2,1)S(1)} %get-tuple-element.28), channel_id=1, source_target_pairs={{0,1},{1,2},{2,3},{3,4},{4,5},{5,6},{6,7},{7,8},{8,9},{9,10},{10,1... | collective-permute-start | bytes 245768 | tf_op jit(solution)/shard_map/ppermute | solution.py:717
  81.2 5.5 %collective-permute-start.5 = (bf16[80,512]{1,0:T(8,128)(2,1)S(1)}, bf16[80,512]{1,0:T(8,128)(2,1)S(1)}, u32[]{:S(2)}, u32[]{:S(2)}) collective-permute-start(bf16[80,512]{1,0:T(8,128)(2,1)S(1)} %get-tuple-element.29), channel_id=1, source_target_pairs={{1,0},{2,1},{3,2},{4,3},{5,4},{6,5},{7,6},{8,7},{9,8},{10,9},{11,1... | collective-permute-start | bytes 245768 | tf_op jit(solution)/shard_map/ppermute | solution.py:718
  86.8 6.3 %shard_map.127 = (bf16[6,64,256]{2,1,0:T(8,128)(2,1)S(1)}, bf16[64,1024]{1,0:T(8,128)(2,1)S(1)}) custom-call(bf16[64,2048]{1,0:T(8,128)(2,1)S(1)} %get-tuple-element.25.refs_0_, s32[9,2048]{1,0:T(8,128)S(1)} %copy-done.5, bf16[64,576]{1,0:T(8,128)(2,1)S(1)} %copy.25.refs_5_.refs_2_.refs_6_, bf16[64,576]{1,0:T(8,128)(2,1)S(1)} %copy.26.refs_6_.refs_3_.refs_7_), custom_call_target="tpu_custom_call" | custom-call | tf_op jit(solution)/shard_map/pallas_call | solution.py:52
  93.1 5.1 %shard_map.128 = bf16[64,2048]{1,0:T(8,128)(2,1)} custom-call(bf16[64,2048]{1,0:T(8,128)(2,1)S(1)} %get-tuple-element.25.refs_0_, bf16[6,64,256]{2,1,0:T(8,128)(2,1)S(1)} %get-tuple-element.26.refs_1_, bf16[64,1024]{1,0:T(8,128)(2,1)S(1)} %get-tuple-element.27.refs_2_, bf16[80,512]{1,0:T(8,128)(2,1)S(1)} %collective-permute-done.4.refs_3_, ...), custom_call_target="tpu_custom_call" | custom-call | tf_op jit(solution)/shard_map/pallas_call | solution.py:52
  (37 shorter events, 0.1 us)
Async XLA Ops:
  0.6 18.6 %copy-start.12 = (bf16[64,24,512]{2,1,0:T(8,128)(2,1)S(1)}, bf16[64,24,512]{2,1,0:T(8,128)(2,1)}, u32[]{:S(2)}) copy-start(bf16[64,24,512]{2,1,0:T(8,128)(2,1)} %param.11) | copy-start | bytes 4718596
  3.0 6.8 %collective-permute-start = (bf16[128,640]{1,0:T(8,128)(2,1)S(1)}, bf16[128,640]{1,0:T(8,128)(2,1)S(1)}, u32[]{:S(2)}, u32[]{:S(2)}) collective-permute-start(bf16[128,640]{1,0:T(8,128)(2,1)S(1)} %get-tuple-element.17), channel_id=1, source_target_pairs={{0,1},{1,2},{2,3},{3,4},{4,5},{5,6},{6,7},{8,9},{9,10},{10,11},{11... | collective-permute-start | bytes 491528 | tf_op jit(solution)/shard_map/ppermute | solution.py:717
  9.8 19.5 %copy-start.2 = (bf16[128,640]{1,0:T(8,128)(2,1)}, bf16[128,640]{1,0:T(8,128)(2,1)S(1)}, u32[]{:S(2)}) copy-start(bf16[128,640]{1,0:T(8,128)(2,1)S(1)} %collective-permute-done.refs_2_.refs_1_) | copy-start | bytes 491524
  9.8 19.5 %all-to-all-start = ((bf16[32,16,128]{2,1,0:T(8,128)(2,1)}), bf16[32,16,128]{2,1,0:T(8,128)(2,1)S(1)}, u32[]{:S(2)}, u32[]{:S(2)}) async-start(bf16[32,16,128]{2,1,0:T(8,128)(2,1)} %shard_map.122), calls=%async_computation | async-start | bytes 262144 | tf_op jit(solution)/shard_map/all_to_all | solution.py:140
  17.9 8.5 %copy-start.7 = (s32[1,4096]{1,0:T(1,128)S(1)}, s32[1,4096]{1,0:T(1,128)}, u32[]{:S(2)}) copy-start(s32[1,4096]{1,0:T(1,128)} %refs_9_.1) | copy-start | bytes 49156
  17.9 8.5 %collective-permute-start.1 = (bf16[128,640]{1,0:T(8,128)(2,1)S(1)}, bf16[128,640]{1,0:T(8,128)(2,1)S(1)}, u32[]{:S(2)}, u32[]{:S(2)}) collective-permute-start(bf16[128,640]{1,0:T(8,128)(2,1)S(1)} %get-tuple-element.19), channel_id=1, source_target_pairs={{1,0},{2,1},{3,2},{4,3},{5,4},{6,5},{7,6},{9,8},{10,9},{11,10},{12... | collective-permute-start | bytes 491528 | tf_op jit(solution)/shard_map/ppermute | solution.py:718
  19.8 7.6 %copy-start = (bf16[64,24,512]{2,0,1:T(8,128)(2,1)}, bf16[64,24,512]{2,0,1:T(8,128)(2,1)S(1)}, u32[]{:S(2)}) copy-start(bf16[64,24,512]{2,0,1:T(8,128)(2,1)S(1)} %copy.34) | copy-start | bytes 4718596
  26.4 2.9 %copy-start.3 = (bf16[128,640]{1,0:T(8,128)(2,1)}, bf16[128,640]{1,0:T(8,128)(2,1)S(1)}, u32[]{:S(2)}) copy-start(bf16[128,640]{1,0:T(8,128)(2,1)S(1)} %collective-permute-done.1.refs_3_.refs_2_) | copy-start | bytes 491524
  27.4 6.4 %copy-start.9 = (bf16[256,128]{1,0:T(8,128)(2,1)}, bf16[256,128]{1,0:T(8,128)(2,1)S(1)}, u32[]{:S(2)}) copy-start(bf16[256,128]{1,0:T(8,128)(2,1)S(1)} %get-tuple-element.21.refs_5_) | copy-start | bytes 196612
  27.4 6.4 %copy-start.10 = (bf16[256,128]{1,0:T(8,128)(2,1)}, bf16[256,128]{1,0:T(8,128)(2,1)S(1)}, u32[]{:S(2)}) copy-start(bf16[256,128]{1,0:T(8,128)(2,1)S(1)} %get-tuple-element.20.refs_6_) | copy-start | bytes 196612
  27.4 6.4 %collective-permute-start.2 = (bf16[256,128]{1,0:T(8,128)(2,1)S(1)}, bf16[256,128]{1,0:T(8,128)(2,1)S(1)}, u32[]{:S(2)}, u32[]{:S(2)}) collective-permute-start(bf16[256,128]{1,0:T(8,128)(2,1)S(1)} %get-tuple-element.20.refs_6_), channel_id=1, source_target_pairs={{0,8},{8,16},{16,24},{24,0},{1,9},{9,17},{17,25},{25,1},{2,10},{10... | collective-permute-start | bytes 196616 | tf_op jit(solution)/shard_map/ppermute | solution.py:717
  29.3 4.4 %collective-permute-start.3 = (bf16[256,128]{1,0:T(8,128)(2,1)S(1)}, bf16[256,128]{1,0:T(8,128)(2,1)S(1)}, u32[]{:S(2)}, u32[]{:S(2)}) collective-permute-start(bf16[256,128]{1,0:T(8,128)(2,1)S(1)} %get-tuple-element.21.refs_5_), channel_id=1, source_target_pairs={{8,0},{16,8},{24,16},{0,24},{9,1},{17,9},{25,17},{1,25},{10,2},{18... | collective-permute-start | bytes 196616 | tf_op jit(solution)/shard_map/ppermute | solution.py:718
  29.4 4.5 %copy-start.4 = (bf16[32,16,128]{2,1,0:T(8,128)(2,1)}, bf16[32,16,128]{2,1,0:T(8,128)(2,1)S(1)}, u32[]{:S(2)}) copy-start(bf16[32,16,128]{2,1,0:T(8,128)(2,1)S(1)} %all-to-all-done.refs_0_.refs_8_) | copy-start | bytes 393220
  33.2 0.6 copy-start.8
  33.8 0.6 copy-start.15
  33.8 0.6 copy-start.16
  34.4 25.3 %copy-start.13 = (bf16[9,64,64]{2,1,0:T(8,128)(2,1)S(1)}, bf16[9,64,64]{2,1,0:T(8,128)(2,1)}, u32[]{:S(2)}) copy-start(bf16[9,64,64]{2,1,0:T(8,128)(2,1)} %param.16) | copy-start | bytes 221188
  34.4 25.6 %copy-start.14 = (bf16[9,64,64]{2,1,0:T(8,128)(2,1)S(1)}, bf16[9,64,64]{2,1,0:T(8,128)(2,1)}, u32[]{:S(2)}) copy-start(bf16[9,64,64]{2,1,0:T(8,128)(2,1)} %param.17) | copy-start | bytes 221188
  54.4 21.1 %all-to-all-start.1 = ((bf16[32,64,128]{2,1,0:T(8,128)(2,1)}), bf16[32,64,128]{2,1,0:T(8,128)(2,1)S(1)}, u32[]{:S(2)}, u32[]{:S(2)}) async-start(bf16[32,64,128]{2,1,0:T(8,128)(2,1)} %get-tuple-element.24), calls=%async_computation.1 | async-start | bytes 1048576 | tf_op jit(solution)/shard_map/all_to_all | solution.py:779
  60.3 15.2 %copy-start.5 = (s32[9,2048]{1,0:T(8,128)S(1)}, s32[9,2048]{1,0:T(8,128)}, u32[]{:S(2)}) copy-start(s32[9,2048]{1,0:T(8,128)} %refs_5_.1) | copy-start | bytes 221188
  60.3 15.2 %copy-start.6 = (bf16[64,2048]{1,0:T(8,128)(2,1)S(1)}, bf16[64,2048]{1,0:T(8,128)(2,1)}, u32[]{:S(2)}) copy-start(bf16[64,2048]{1,0:T(8,128)(2,1)} %refs_2_.2) | copy-start | bytes 786436
  60.3 15.2 %copy-start.11 = (s32[2048]{0:T(1024)S(1)}, s32[2048]{0:T(1024)}, u32[]{:S(2)}) copy-start(s32[2048]{0:T(1024)} %param.18) | copy-start | bytes 24580
  62.7 30.4 %copy-start.1 = (bf16[24,64,512]{2,0,1:T(8,128)(2,1)}, bf16[24,64,512]{2,0,1:T(8,128)(2,1)S(1)}, u32[]{:S(2)}) copy-start(bf16[24,64,512]{2,0,1:T(8,128)(2,1)S(1)} %copy.33) | copy-start | bytes 4718596
  78.3 14.8 %collective-permute-start.4 = (bf16[80,512]{1,0:T(8,128)(2,1)S(1)}, bf16[80,512]{1,0:T(8,128)(2,1)S(1)}, u32[]{:S(2)}, u32[]{:S(2)}) collective-permute-start(bf16[80,512]{1,0:T(8,128)(2,1)S(1)} %get-tuple-element.28), channel_id=1, source_target_pairs={{0,1},{1,2},{2,3},{3,4},{4,5},{5,6},{6,7},{7,8},{8,9},{9,10},{10,1... | collective-permute-start | bytes 245768 | tf_op jit(solution)/shard_map/ppermute | solution.py:717
  81.2 11.9 %collective-permute-start.5 = (bf16[80,512]{1,0:T(8,128)(2,1)S(1)}, bf16[80,512]{1,0:T(8,128)(2,1)S(1)}, u32[]{:S(2)}, u32[]{:S(2)}) collective-permute-start(bf16[80,512]{1,0:T(8,128)(2,1)S(1)} %get-tuple-element.29), channel_id=1, source_target_pairs={{1,0},{2,1},{3,2},{4,3},{5,4},{6,5},{7,6},{8,7},{9,8},{10,9},{11,1... | collective-permute-start | bytes 245768 | tf_op jit(solution)/shard_map/ppermute | solution.py:718

commit v2 on v1

--- a/solution.py
+++ b/solution.py
@@ -13,13 +13,28 @@
 NEIGHBOURS = ((0, 0), (-1, 0), (1, 0), (0, -1), (0, 1), (-1, -1), (1, -1), (-1, 1), (1, 1))
 VMEM_LIMIT = 20 * 1024 * 1024
 VMEM_WHOLE = 60 * 1024 * 1024
+VMEM_MOST = 62_200_000
 
 VMEM = pl.BlockSpec(memory_space=pltpu.VMEM)
 ANY = pl.BlockSpec(memory_space=pl.ANY)
 HBM = pl.BlockSpec(memory_space=pltpu.HBM)
 
 
-def call(body, outs, ins, scratch=(), parts=None, untouched=(), out_specs=None, limit=VMEM_LIMIT):
+def call(body, outs, ins, scratch=(), parts=None, untouched=(), out_specs=None, limit=None):
+    if limit is None:
+        touched = [i for i in range(len(ins)) if i not in untouched]
+
+        def plain(*refs):
+            body(lambda *_: None, *(refs[i] for i in touched), *refs[len(ins) :])
+
+        return pl.pallas_call(
+            plain,
+            out_shape=outs,
+            in_specs=[VMEM if i in touched else ANY for i in range(len(ins))],
+            out_specs=jax.tree.map(lambda _: VMEM, outs),
+            scratch_shapes=list(scratch),
+            compiler_params=pltpu.CompilerParams(vmem_limit_bytes=VMEM_LIMIT),
+        )(*ins)
     parts = parts or {}
     held = [i for i in range(len(ins)) if i not in untouched]
     shapes = [
@@ -76,7 +91,7 @@
 
 
 def slot_values(heat_ref, slot_ref, rows):
-    heat = heat_ref[...].astype(F32)[0:1]
+    heat = heat_ref[0:16, :].astype(F32)[0:1]
     slot = slot_ref[...]
     places = lax.broadcasted_iota(jnp.int32, (rows, slot.shape[1]), 0)
     match = places == (slot >> 7)
@@ -129,8 +144,7 @@
             limit=VMEM_WHOLE,
         )
     rows = devices * capacity // LANES
-    out = jax.ShapeDtypeStruct((rows, LANES), BF)
-    table = call(slot_table_body, out, ins, parts={0: (slice(0, 16), slice(None))})
+    table = call(slot_table_body, jax.ShapeDtypeStruct((rows, LANES), BF), ins)
     table = table.reshape(devices, capacity)
     return jnp.where((around >= 0)[:, :, None], table[np.maximum(around, 0)], jnp.inf).astype(BF)
 
@@ -168,65 +182,89 @@
     return pl.ds(pl.multiple_of(e * width, width), width)
 
 
-def scatter_body(
-    wait, vals_ref, cell_ref, above_ref, below_ref, out_ref, targets, left, right, prod, prod_ends
-):
-    rows, cols = out_ref.shape[0] - 8, out_ref.shape[1]
+def one_hot_heat(value, live, high, size):
+    match = lax.broadcasted_iota(jnp.int32, (size, LANES), 0) == jnp.where(live, high, -1)
+    both = [jnp.where(match, value, 0.0), jnp.where(match, 1.0, 0.0)]
+    return jnp.concatenate(both, axis=0).astype(BF)
+
+
+def mean_heat(ref, first, count, rows_on, lanes):
+    return ref[first : first + count, lanes] / jnp.maximum(
+        ref[first + rows_on : first + rows_on + count, lanes], 1.0
+    )
+
+
+def scatter_own_body(wait, vals_ref, cell_ref, out_ref, left, right, prod):
+    rows, cols = out_ref.shape
     blocks = cols // LANES
     span = rows * blocks
-    wait(2, 3)
+
+    def chunk(e):
+        lanes = lanes_at(e)
+        value, live, row, col = live_entry(
+            vals_ref[e].astype(F32)[0:1], cell_ref[:, lanes], cols, rows, 0
+        )
+        left[:, lanes] = one_hot_heat(value, live, (col >> 7) * rows + row - 2, span)
+        right[:, lanes] = one_hot(col & 127, LANES)
+
+    for_chunks(vals_ref.shape[0], 4, chunk)
+    prod[...] = nt_dot(left[...], right[...])
+    for b in range(blocks):
+        out_ref[:, b * LANES : (b + 1) * LANES] = mean_heat(prod, b * rows, rows, span, slice(None))
+
+
+def scatter_own(vals, cells, rows, cols):
+    span = rows * (cols // LANES)
+    return call(
+        scatter_own_body,
+        jax.ShapeDtypeStruct((rows, cols), F32),
+        [vals, cells],
+        scratch=[
+            pltpu.VMEM((2 * span, cells.size), BF),
+            pltpu.VMEM((LANES, cells.size), BF),
+            pltpu.VMEM((2 * span, LANES), F32),
+        ],
+    )
+
+
+def scatter_ends_body(
+    wait, own_ref, vals_ref, above_ref, below_ref, out_ref, targets, left, right, prod
+):
+    rows, cols = own_ref.shape
     targets[0] = decoded(above_ref[0:64, cols:])
     targets[1] = decoded(below_ref[0:64, cols:])
-    wait(0, 1)
+    out_ref[2 : rows + 2, :] = own_ref[...]
 
     def chunk(e):
         lanes = lanes_at(e)
         values = vals_ref[e].astype(F32)
-        for n, (dr, _) in enumerate(NEIGHBOURS[:3]):
-            cell = targets[n - 1, pl.ds(e, 1), :] if n else cell_ref[:, lanes]
-            value, live, row, col = live_entry(values[n : n + 1], cell, cols, rows, dr)
-            block = col >> 7
-            if n == 0:
-                high, size, start = block * rows + row - 2, span, 0
-            else:
-                high, size = 2 * block + row - (0 if dr < 0 else rows + 2), 8
-                start = 2 * span + 16 * (n - 1)
-            match = lax.broadcasted_iota(jnp.int32, (size, LANES), 0) == jnp.where(live, high, -1)
-            left[start : start + 2 * size, lanes] = jnp.concatenate(
-                [jnp.where(match, value, 0.0), jnp.where(match, 1.0, 0.0)], axis=0
-            ).astype(BF)
+        for n, (dr, _) in enumerate(NEIGHBOURS[1:3]):
+            value, live, row, col = live_entry(
+                values[n + 1 : n + 2], targets[n, pl.ds(e, 1), :], cols, rows, dr
+            )
+            high = 2 * (col >> 7) + row - (0 if dr < 0 else rows + 2)
+            left[16 * n : 16 * (n + 1), lanes] = one_hot_heat(value, live, high, 8)
             right[n * LANES : (n + 1) * LANES, lanes] = one_hot(col & 127, LANES)
 
-    for_chunks(vals_ref.shape[0], 2, chunk)
-    prod[...] = nt_dot(left[0 : 2 * span], right[0:LANES])
-    prod_ends[...] = nt_dot(left[2 * span :], right[LANES:])
-
-    def mean(ref, first, count, rows_on, lanes):
-        return ref[first : first + count, lanes] / jnp.maximum(
-            ref[first + rows_on : first + rows_on + count, lanes], 1.0
-        )
-
-    first, second = slice(0, LANES), slice(LANES, 2 * LANES)
-    for b in range(blocks):
+    for_chunks(vals_ref.shape[0], 4, chunk)
+    prod[...] = nt_dot(left[...], right[...])
+    for b in range(cols // LANES):
         to = slice(b * LANES, (b + 1) * LANES)
-        out_ref[2 : rows + 2, to] = mean(prod, b * rows, rows, span, first)
-        out_ref[0:2, to] = mean(prod_ends, 2 * b, 2, 8, first)
-        out_ref[rows + 2 : rows + 4, to] = mean(prod_ends, 16 + 2 * b, 2, 8, second)
-
-
-def scatter_heat(vals, cells, above, below, rows):
-    slots = cells.size
-    cols = above.shape[1] - LANES
-    span = rows * (cols // LANES)
+        out_ref[0:2, to] = mean_heat(prod, 2 * b, 2, 8, slice(0, LANES))
+        out_ref[rows + 2 : rows + 4, to] = mean_heat(prod, 16 + 2 * b, 2, 8, slice(LANES, None))
+
+
+def scatter_ends(own, vals, above, below):
+    rows, cols = own.shape
+    slots = vals.shape[0] * LANES
     return call(
-        scatter_body,
+        scatter_ends_body,
         jax.ShapeDtypeStruct((rows + 8, cols), F32),
-        [vals, cells, above, below],
+        [own, vals, above, below],
         scratch=[
             pltpu.VMEM((2, slots // LANES, LANES), jnp.int32),
-            pltpu.VMEM((2 * span + 32, slots), BF),
-            pltpu.VMEM((3 * LANES, slots), BF),
-            pltpu.VMEM((2 * span, LANES), F32),
+            pltpu.VMEM((32, slots), BF),
+            pltpu.VMEM((2 * LANES, slots), BF),
             pltpu.VMEM((32, 2 * LANES), F32),
         ],
     )
@@ -291,29 +329,25 @@
     return (code[:half].astype(F32) * 128.0 + code[half:].astype(F32)).astype(jnp.int32)
 
 
-def side_body(
-    wait, first_ref, last_ref, above_ref, below_ref, cell_ref, west_ref, east_ref
-):
-    rows, channels, _ = first_ref.shape
-    cols = above_ref.shape[1] - LANES
-    wait(0, 1, 2, 3, 4)
-
-    def column(i, lanes, air_ref):
+def side_body(wait, air_ref, above_ref, below_ref, cell_ref, west_ref, east_ref):
+    rows, channels, cols = air_ref.shape
+
+    def column(i, lanes):
         if i < 2:
             return above_ref[i * channels : (i + 1) * channels, lanes]
         if i < rows + 2:
-            return air_ref[i - 2]
+            return air_ref[i - 2, :, lanes]
         i = i - rows - 2
         return below_ref[i * channels : (i + 1) * channels, lanes]
 
     lane = lax.broadcasted_iota(jnp.int32, (channels, LANES), 1)
-    for ref, air_ref, lanes, shift, half in (
-        (west_ref, first_ref, slice(0, LANES), 0, 0),
-        (east_ref, last_ref, slice(cols - LANES, cols), 66, 32),
+    for ref, lanes, shift, half in (
+        (west_ref, slice(0, LANES), 0, 0),
+        (east_ref, slice(cols - LANES, cols), 66, 32),
     ):
         total = jnp.zeros((channels, LANES), F32)
         for i in range(rows + 4):
-            moved = pltpu.roll(column(i, lanes, air_ref).astype(F32), (2 * i + shift) % LANES, 1)
+            moved = pltpu.roll(column(i, lanes).astype(F32), (2 * i + shift) % LANES, 1)
             total = jnp.where(lane >> 1 == i + half, moved, total)
         ref[0:channels] = total.astype(BF)
         first = channels
@@ -322,15 +356,9 @@
             first += 64
 
 
-def sides(air, above, below, cells):
-    channels, cols = air.shape[1:]
-    every = slice(None)
-    return call(
-        side_body,
-        (jax.ShapeDtypeStruct((channels + 3 * 64, LANES), BF),) * 2,
-        [air, air, above, below, cells],
-        parts={0: (every, every, slice(0, LANES)), 1: (every, every, slice(cols - LANES, cols))},
-    )
+def sides(air, above, below, cells, ready):
+    out = jax.ShapeDtypeStruct((air.shape[1] + 3 * 64, LANES), BF)
+    return call(side_body, (out, out), [air, above, below, cells, ready], untouched=(4,))
 
 
 def shifted(center, from_left, from_right, at_left, at_right, left_lane, right_lane):
@@ -456,12 +484,12 @@
             next_ref[r] = (start[r + 2].astype(F32) + total).astype(BF)
 
     def steps(first, last, *stages):
-        def step(j, carry):
+        def step(j):
             for stage, late in stages:
-                stage(j - late)
-            return carry
-
-        lax.fori_loop(first, last, step, 0)
+                stage(first + j - late)
+
+        count = last - first
+        for_chunks(count, 3 if count % 3 == 0 else 1, step)
 
     half = rows // 2
     one, two, three = (first_stage, 0), (second_stage, 1), (third_stage, 3)
@@ -482,7 +510,7 @@
     rows, channels, cols = next_ref.shape
     shift = cols.bit_length() - 1
     width = 256
-    group = 6
+    group = 12
 
     def pick(tile):
         cell = cell_ref[:, lanes_at(tile, width)]
@@ -518,7 +546,7 @@
             heat_weight.reshape(1, -1), first, second,
         ],
         out_specs=(HBM, VMEM),
-        limit=VMEM_WHOLE,
+        limit=VMEM_MOST,
         scratch=[
             pltpu.VMEM((rows, channels, cols), BF),
             pltpu.SemaphoreType.DMA((1,)),
@@ -738,7 +766,12 @@
     capacity = slot_space // devices
     channels, rows, cols = atmos.shape
 
-    own_cells = coupling_air_cells.reshape(-1, LANES)
+    table = heat_table(ocean, marine_coupling_slot, capacity, faces, tiles)
+    table, atmos, own_cells = lax.optimization_barrier(
+        (table, atmos, coupling_air_cells.reshape(-1, LANES))
+    )
+    heat = heat_slots(table, both)
+
     code = coded(own_cells)
     code = jnp.concatenate([code, jnp.zeros((2 * channels - code.shape[0], LANES), BF)], axis=0)
 
@@ -746,18 +779,14 @@
         two = jnp.transpose(atmos[:, first : first + 2], (1, 0, 2)).reshape(2 * channels, cols)
         return jnp.concatenate([two, code], axis=1)
 
-    low, high, heats = lax.optimization_barrier((two_rows(0), two_rows(rows - 2), ocean))
-    above, below = from_neighbours(low, high, "tile")
-
-    table = heat_table(heats, marine_coupling_slot, capacity, faces, tiles)
-    table, above = lax.optimization_barrier((table, above))
-    heat = heat_slots(table, both)
+    above, below = from_neighbours(two_rows(0), two_rows(rows - 2), "tile")
 
     air = jnp.transpose(atmos, (1, 0, 2))
-    to_west, to_east = sides(air, above, below, own_cells)
+    field = scatter_own(heat, coupling_air_cells, rows, cols)
+    to_west, to_east = sides(air, above, below, own_cells, field)
     west, east = from_neighbours(to_west, to_east, "face", closed=True)
 
-    field = scatter_heat(heat, coupling_air_cells, above, below, rows)
+    field = scatter_ends(field, heat, above, below)
     air_next, outgoing = atmosphere(
         air, above, below, west, east, to_west, to_east, field, heat, coupling_air_cells,
         surface_heat_weight, air_conv_first_weight, air_conv_second_weight,

time: 98.9 us -> 92 us (0.930)
  Pallas kernels: 41 us -> 38 us
  waiting for transfers between devices: 20.2 us -> 17.8 us
  starting transfers between devices: 29 us -> 27.8 us
    pallas_call x7 -> x2, Pallas kernels: 41 us -> 22 us  [call(): pl.pallas_call(kernel, out_shape=outs, in_specs=[ANY] * len(ins), out_spe...]
    pallas_call x0 -> x6, Pallas kernels: none -> 15.9 us  [call(): pl.pallas_call(plain, out_shape=outs, in_specs=[VMEM if i in touched else...]
    ppermute x3, waiting for transfers between devices: 6.68 us -> 4.89 us  [from_neighbours(): after = lax.ppermute(low, axis, [((i + 1) % count, i) for i in range(ends)])]
    all_to_all x1, starting transfers between devices: 8.1 us -> 7.1 us  [heat_slots(): got = lax.all_to_all(table, both, split_axis=0, concat_axis=0, tiled=True)]
  transfers between devices with their start and end apart: 8 -> 8, of which waited for: 3 -> 4; matrix products, arithmetic and copies ran while one was open for 3% -> 6% of each run, Pallas kernels for 13% -> 10%
where the time goes in v2:
time: 92 us; the launch traced here: 91.5 us
  Pallas kernels  38 us (41%)
  starting transfers between devices  27.8 us (30%)
  waiting for transfers between devices  17.8 us (19%)
  local copies, waits for them, and re-layouts  6.12 us (7%)
  between operations  0.96 us (1%)
    pallas_call x2, Pallas kernels, call(): pl.pallas_call(kernel, out_shape=outs, in_specs=[ANY] * len(ins), out_spe...  22 us
    pallas_call x6, Pallas kernels, call(): pl.pallas_call(plain, out_shape=outs, in_specs=[VMEM if i in touched else...  15.9 us
    all_to_all x1, waiting for transfers between devices, shards(): lax.all_to_all(outgoing, both, split_axis=0, concat_axis=0, tiled=True)  12.8 us
    ppermute x3, starting transfers between devices, from_neighbours(): lax.ppermute(high, axis, [(i, (i + 1) % count) for i in range(ends)])  8.83 us
    all_to_all x1, starting transfers between devices, heat_slots(): got = lax.all_to_all(table, both, split_axis=0, concat_axis=0, tiled=True)  7.1 us
    ppermute x3, starting transfers between devices, from_neighbours(): after = lax.ppermute(low, axis, [((i + 1) % count, i) for i in range(ends)])  6.83 us
    all_to_all x1, starting transfers between devices, shards(): lax.all_to_all(outgoing, both, split_axis=0, concat_axis=0, tiled=True)  5.05 us
    ppermute x3, waiting for transfers between devices, from_neighbours(): after = lax.ppermute(low, axis, [((i + 1) % count, i) for i in range(ends)])  4.89 us
  transfers between devices with their start and end apart: 8, of which 4 were waited for; matrix products, arithmetic and copies ran while one was open for 6% of the time, Pallas kernels for 10%

profile of v2, /device:TPU:1, one launch (start us, length us, event | category | flops | bytes accessed | tf_op | source)
XLA Modules:
  0.0 91.5 jit_solution(15557871606411896459)
XLA Ops:
  0.6 2.1 %shard_map.122 = bf16[32,16,128]{2,1,0:T(8,128)(2,1)} custom-call(bf16[64,2048]{1,0:T(8,128)(2,1)} %refs_2_.2, s32[1,2048]{1,0:T(1,128)} %bitcast.25, bf16[512,32]{1,0:T(8,128)(2,1)} %constant.8.clone.refs_2_), custom_call_target="tpu_custom_call" | custom-call | tf_op jit(solution)/shard_map/pallas_call | solution.py:67
  2.8 7.1 %all-to-all-start = ((bf16[32,16,128]{2,1,0:T(8,128)(2,1)}), bf16[32,16,128]{2,1,0:T(8,128)(2,1)S(1)}, u32[]{:S(2)}, u32[]{:S(2)}) async-start(bf16[32,16,128]{2,1,0:T(8,128)(2,1)} %shard_map.122), calls=%async_computation | async-start | bytes 262144 | tf_op jit(solution)/shard_map/all_to_all | solution.py:154
  9.9 0.8 shift-right-arithmetic_convert_fusion
  10.7 1.4 %slice_bitcast_fusion = (bf16[2,64,512]{2,0,1:T(2,128)(2,1)S(1)}, bf16[2,64,512]{2,0,1:T(2,128)(2,1)S(1)}) fusion(bf16[64,24,512]{2,1,0:T(8,128)(2,1)} %param.11), kind=kLoop, calls=%fused_computation.4 | loop fusion | bytes 524288 | tf_op jit(solution)/shard_map/transpose | solution.py:779
  12.2 3.3 %collective-permute-start = (bf16[128,640]{1,0:T(8,128)(2,1)S(1)}, bf16[128,640]{1,0:T(8,128)(2,1)S(1)}, u32[]{:S(2)}, u32[]{:S(2)}) collective-permute-start(bf16[128,640]{1,0:T(8,128)(2,1)S(1)} %get-tuple-element.29), channel_id=1, source_target_pairs={{0,1},{1,2},{2,3},{3,4},{4,5},{5,6},{6,7},{8,9},{9,10},{10,11},{11... | collective-permute-start | bytes 491528 | tf_op jit(solution)/shard_map/ppermute | solution.py:745
  15.6 1.3 %collective-permute-start.1 = (bf16[128,640]{1,0:T(8,128)(2,1)S(1)}, bf16[128,640]{1,0:T(8,128)(2,1)S(1)}, u32[]{:S(2)}, u32[]{:S(2)}) collective-permute-start(bf16[128,640]{1,0:T(8,128)(2,1)S(1)} %get-tuple-element.28), channel_id=1, source_target_pairs={{1,0},{2,1},{3,2},{4,3},{5,4},{6,5},{7,6},{9,8},{10,9},{11,10},{12... | collective-permute-start | bytes 491528 | tf_op jit(solution)/shard_map/ppermute | solution.py:746
  16.9 0.5 copy.34
  17.4 0.0 copy-start
  17.4 0.1 all-to-all-done.refs_0_.refs_1_.refs_8_
  17.5 1.5 %shard_map.123.refs_4_.refs_0_ = f32[24,512]{1,0:T(8,128)S(1)} custom-call(bf16[32,16,128]{2,1,0:T(8,128)(2,1)S(1)} %all-to-all-done.refs_0_.refs_1_.refs_8_, s32[1,4096]{1,0:T(1,128)S(1)} %copy-done.7), custom_call_target="tpu_custom_call" | custom-call | tf_op jit(solution)/shard_map/pallas_call | solution.py:30
  18.9 0.0 copy-start.3
  19.0 3.6 %collective-permute-done.1.refs_2_.refs_3_ = bf16[128,640]{1,0:T(8,128)(2,1)S(1)} collective-permute-done((bf16[128,640]{1,0:T(8,128)(2,1)S(1)}, bf16[128,640]{1,0:T(8,128)(2,1)S(1)}, u32[]{:S(2)}, u32[]{:S(2)}) %collective-permute-start.1) | collective-permute-done | bytes 163872 | tf_op jit(solution)/shard_map/ppermute | solution.py:746
  22.6 0.3 shard_map.124
  22.9 2.6 %collective-permute-start.2 = (bf16[256,128]{1,0:T(8,128)(2,1)S(1)}, bf16[256,128]{1,0:T(8,128)(2,1)S(1)}, u32[]{:S(2)}, u32[]{:S(2)}) collective-permute-start(bf16[256,128]{1,0:T(8,128)(2,1)S(1)} %get-tuple-element.17.refs_6_), channel_id=1, source_target_pairs={{0,8},{8,16},{16,24},{24,0},{1,9},{9,17},{17,25},{25,1},{2,10},{10... | collective-permute-start | bytes 196616 | tf_op jit(solution)/shard_map/ppermute | solution.py:745
  25.5 1.8 %shard_map.125.refs_7_ = f32[32,512]{1,0:T(8,128)S(1)} custom-call(f32[24,512]{1,0:T(8,128)S(1)} %shard_map.123.refs_4_.refs_0_, bf16[32,16,128]{2,1,0:T(8,128)(2,1)S(1)} %all-to-all-done.refs_0_.refs_1_.refs_8_, bf16[128,640]{1,0:T(8,128)(2,1)S(1)} %collective-permute-done.refs_1_.refs_2_, bf16[128,640]{1,0:T(8,128)(2,1)S(1)} %collective-permute-done.1.refs_2_.refs_3_), custom_call_target="tpu_custom_call" | custom-call | tf_op jit(solution)/shard_map/pallas_call | solution.py:30
  27.3 0.6 copy-done.8
  27.9 1.3 %collective-permute-done.3.refs_4_ = bf16[256,128]{1,0:T(8,128)(2,1)S(1)} collective-permute-done((bf16[256,128]{1,0:T(8,128)(2,1)S(1)}, bf16[256,128]{1,0:T(8,128)(2,1)S(1)}, u32[]{:S(2)}, u32[]{:S(2)}) %collective-permute-start.3) | collective-permute-done | bytes 65568 | tf_op jit(solution)/shard_map/ppermute | solution.py:746
  29.3 0.6 copy-done.16
  29.8 19.9 %shard_map.126 = (bf16[24,64,512]{2,1,0:T(8,128)(2,1)}, bf16[32,64,128]{2,1,0:T(8,128)(2,1)}) custom-call(bf16[24,64,512]{2,1,0:T(8,128)(2,1)} %bitcast.20, bf16[128,640]{1,0:T(8,128)(2,1)} %copy-done.3, bf16[128,640]{1,0:T(8,128)(2,1)} %copy-done.4, bf16[256,128]{1,0:T(8,128)(2,1)} %copy-done.15, bf16[256,128]{1,0:T(8,128)(2,1)} %copy-done.16, ...), custom_call_target="tpu_custom_call" | custom-call | tf_op jit(solution)/shard_map/pallas_call | solution.py:67
  49.8 5.1 %all-to-all-start.1 = ((bf16[32,64,128]{2,1,0:T(8,128)(2,1)}), bf16[32,64,128]{2,1,0:T(8,128)(2,1)S(1)}, u32[]{:S(2)}, u32[]{:S(2)}) async-start(bf16[32,64,128]{2,1,0:T(8,128)(2,1)} %get-tuple-element.20), calls=%async_computation.1 | async-start | bytes 1048576 | tf_op jit(solution)/shard_map/all_to_all | solution.py:808
  54.8 0.1 copy.23
  55.0 0.1 copy.25.refs_5_.refs_2_.refs_6_
  55.1 0.1 copy.24
  55.3 0.1 copy.26.refs_6_.refs_3_.refs_7_
  55.5 0.0 copy-start.6
  55.5 2.3 %copy.33 = bf16[24,64,512]{2,0,1:T(8,128)(2,1)S(1)} copy(bf16[24,64,512]{2,1,0:T(8,128)(2,1)} %get-tuple-element.19) | data formatting | bytes 3145728 | tf_op jit(solution)/shard_map/pallas_call | solution.py:67
  57.8 12.8 %all-to-all-done.1.refs_0_ = bf16[32,64,128]{2,1,0:T(8,128)(2,1)S(1)} async-done(((bf16[32,64,128]{2,1,0:T(8,128)(2,1)}), bf16[32,64,128]{2,1,0:T(8,128)(2,1)S(1)}, u32[]{:S(2)}, u32[]{:S(2)}) %all-to-all-start.1) | async-done | bytes 524320 | tf_op jit(solution)/shard_map/all_to_all | solution.py:808
  70.6 2.5 %shard_map.127 = (bf16[64,2048]{1,0:T(8,128)(2,1)S(1)}, bf16[80,512]{1,0:T(8,128)(2,1)S(1)}, bf16[80,512]{1,0:T(8,128)(2,1)S(1)}) custom-call(bf16[32,64,128]{2,1,0:T(8,128)(2,1)S(1)} %all-to-all-done.1.refs_0_, s32[1,2048]{1,0:T(1,128)S(1)} %bitcast.26, bf16[64,2048]{1,0:T(8,128)(2,1)S(1)} %copy-done.6, s32[9,2048]{1,0:T(8,128)S(1)} %copy-done.5, ...), custom_call_target="tpu_custom_call" | custom-call | tf_op jit(solution)/shard_map/pallas_call | solution.py:30
  73.2 2.9 %collective-permute-start.4 = (bf16[80,512]{1,0:T(8,128)(2,1)S(1)}, bf16[80,512]{1,0:T(8,128)(2,1)S(1)}, u32[]{:S(2)}, u32[]{:S(2)}) collective-permute-start(bf16[80,512]{1,0:T(8,128)(2,1)S(1)} %get-tuple-element.24), channel_id=1, source_target_pairs={{0,1},{1,2},{2,3},{3,4},{4,5},{5,6},{6,7},{7,8},{8,9},{9,10},{10,1... | collective-permute-start | bytes 245768 | tf_op jit(solution)/shard_map/ppermute | solution.py:745
  76.1 5.5 %collective-permute-start.5 = (bf16[80,512]{1,0:T(8,128)(2,1)S(1)}, bf16[80,512]{1,0:T(8,128)(2,1)S(1)}, u32[]{:S(2)}, u32[]{:S(2)}) collective-permute-start(bf16[80,512]{1,0:T(8,128)(2,1)S(1)} %get-tuple-element.25), channel_id=1, source_target_pairs={{1,0},{2,1},{3,2},{4,3},{5,4},{6,5},{7,6},{8,7},{9,8},{10,9},{11,1... | collective-permute-start | bytes 245768 | tf_op jit(solution)/shard_map/ppermute | solution.py:746
  81.6 5.9 %shard_map.128 = (bf16[6,64,256]{2,1,0:T(8,128)(2,1)S(1)}, bf16[64,1024]{1,0:T(8,128)(2,1)S(1)}) custom-call(bf16[64,2048]{1,0:T(8,128)(2,1)S(1)} %get-tuple-element.21.refs_0_, s32[9,2048]{1,0:T(8,128)S(1)} %copy-done.5, bf16[64,576]{1,0:T(8,128)(2,1)S(1)} %copy.25.refs_5_.refs_2_.refs_6_, bf16[64,576]{1,0:T(8,128)(2,1)S(1)} %copy.26.refs_6_.refs_3_.refs_7_), custom_call_target="tpu_custom_call" | custom-call | tf_op jit(solution)/shard_map/pallas_call | solution.py:30
  87.5 4.0 %shard_map.129 = bf16[64,2048]{1,0:T(8,128)(2,1)} custom-call(bf16[64,2048]{1,0:T(8,128)(2,1)S(1)} %get-tuple-element.21.refs_0_, bf16[6,64,256]{2,1,0:T(8,128)(2,1)S(1)} %get-tuple-element.22.refs_1_, bf16[64,1024]{1,0:T(8,128)(2,1)S(1)} %get-tuple-element.23.refs_2_, bf16[80,512]{1,0:T(8,128)(2,1)S(1)} %collective-permute-done.4.refs_3_, ...), custom_call_target="tpu_custom_call" | custom-call | tf_op jit(solution)/shard_map/pallas_call | solution.py:30
  (38 shorter events, 0.1 us)
Async XLA Ops:
  2.8 14.7 %all-to-all-start = ((bf16[32,16,128]{2,1,0:T(8,128)(2,1)}), bf16[32,16,128]{2,1,0:T(8,128)(2,1)S(1)}, u32[]{:S(2)}, u32[]{:S(2)}) async-start(bf16[32,16,128]{2,1,0:T(8,128)(2,1)} %shard_map.122), calls=%async_computation | async-start | bytes 262144 | tf_op jit(solution)/shard_map/all_to_all | solution.py:154
  9.9 7.0 %copy-start.12 = (bf16[64,24,512]{2,1,0:T(8,128)(2,1)S(1)}, bf16[64,24,512]{2,1,0:T(8,128)(2,1)}, u32[]{:S(2)}) copy-start(bf16[64,24,512]{2,1,0:T(8,128)(2,1)} %param.11) | copy-start | bytes 4718596
  12.2 6.7 %collective-permute-start = (bf16[128,640]{1,0:T(8,128)(2,1)S(1)}, bf16[128,640]{1,0:T(8,128)(2,1)S(1)}, u32[]{:S(2)}, u32[]{:S(2)}) collective-permute-start(bf16[128,640]{1,0:T(8,128)(2,1)S(1)} %get-tuple-element.29), channel_id=1, source_target_pairs={{0,1},{1,2},{2,3},{3,4},{4,5},{5,6},{6,7},{8,9},{9,10},{10,11},{11... | collective-permute-start | bytes 491528 | tf_op jit(solution)/shard_map/ppermute | solution.py:745
  15.5 1.9 %copy-start.7 = (s32[1,4096]{1,0:T(1,128)S(1)}, s32[1,4096]{1,0:T(1,128)}, u32[]{:S(2)}) copy-start(s32[1,4096]{1,0:T(1,128)} %refs_9_.1) | copy-start | bytes 49156
  15.6 7.0 %collective-permute-start.1 = (bf16[128,640]{1,0:T(8,128)(2,1)S(1)}, bf16[128,640]{1,0:T(8,128)(2,1)S(1)}, u32[]{:S(2)}, u32[]{:S(2)}) collective-permute-start(bf16[128,640]{1,0:T(8,128)(2,1)S(1)} %get-tuple-element.28), channel_id=1, source_target_pairs={{1,0},{2,1},{3,2},{4,3},{5,4},{6,5},{7,6},{9,8},{10,9},{11,10},{12... | collective-permute-start | bytes 491528 | tf_op jit(solution)/shard_map/ppermute | solution.py:746
  17.4 11.8 %copy-start = (bf16[64,24,512]{2,0,1:T(8,128)(2,1)}, bf16[64,24,512]{2,0,1:T(8,128)(2,1)S(1)}, u32[]{:S(2)}) copy-start(bf16[64,24,512]{2,0,1:T(8,128)(2,1)S(1)} %copy.34) | copy-start | bytes 4718596
  17.5 11.7 %copy-start.2 = (bf16[32,16,128]{2,1,0:T(8,128)(2,1)}, bf16[32,16,128]{2,1,0:T(8,128)(2,1)S(1)}, u32[]{:S(2)}) copy-start(bf16[32,16,128]{2,1,0:T(8,128)(2,1)S(1)} %all-to-all-done.refs_0_.refs_1_.refs_8_) | copy-start | bytes 393220
  18.9 10.3 %copy-start.3 = (bf16[128,640]{1,0:T(8,128)(2,1)}, bf16[128,640]{1,0:T(8,128)(2,1)S(1)}, u32[]{:S(2)}) copy-start(bf16[128,640]{1,0:T(8,128)(2,1)S(1)} %collective-permute-done.refs_1_.refs_2_) | copy-start | bytes 491524
  22.6 6.7 %copy-start.4 = (bf16[128,640]{1,0:T(8,128)(2,1)}, bf16[128,640]{1,0:T(8,128)(2,1)S(1)}, u32[]{:S(2)}) copy-start(bf16[128,640]{1,0:T(8,128)(2,1)S(1)} %collective-permute-done.1.refs_2_.refs_3_) | copy-start | bytes 491524
  22.9 6.4 %copy-start.9 = (bf16[256,128]{1,0:T(8,128)(2,1)}, bf16[256,128]{1,0:T(8,128)(2,1)S(1)}, u32[]{:S(2)}) copy-start(bf16[256,128]{1,0:T(8,128)(2,1)S(1)} %get-tuple-element.18.refs_5_) | copy-start | bytes 196612
  22.9 6.4 %copy-start.10 = (bf16[256,128]{1,0:T(8,128)(2,1)}, bf16[256,128]{1,0:T(8,128)(2,1)S(1)}, u32[]{:S(2)}) copy-start(bf16[256,128]{1,0:T(8,128)(2,1)S(1)} %get-tuple-element.17.refs_6_) | copy-start | bytes 196612
  22.9 5.0 %collective-permute-start.2 = (bf16[256,128]{1,0:T(8,128)(2,1)S(1)}, bf16[256,128]{1,0:T(8,128)(2,1)S(1)}, u32[]{:S(2)}, u32[]{:S(2)}) collective-permute-start(bf16[256,128]{1,0:T(8,128)(2,1)S(1)} %get-tuple-element.17.refs_6_), channel_id=1, source_target_pairs={{0,8},{8,16},{16,24},{24,0},{1,9},{9,17},{17,25},{25,1},{2,10},{10... | collective-permute-start | bytes 196616 | tf_op jit(solution)/shard_map/ppermute | solution.py:745
  25.5 3.7 %collective-permute-start.3 = (bf16[256,128]{1,0:T(8,128)(2,1)S(1)}, bf16[256,128]{1,0:T(8,128)(2,1)S(1)}, u32[]{:S(2)}, u32[]{:S(2)}) collective-permute-start(bf16[256,128]{1,0:T(8,128)(2,1)S(1)} %get-tuple-element.18.refs_5_), channel_id=1, source_target_pairs={{8,0},{16,8},{24,16},{0,24},{9,1},{17,9},{25,17},{1,25},{10,2},{18... | collective-permute-start | bytes 196616 | tf_op jit(solution)/shard_map/ppermute | solution.py:746
  27.3 0.6 copy-start.8
  27.9 1.3 %copy-start.15 = (bf16[256,128]{1,0:T(8,128)(2,1)}, bf16[256,128]{1,0:T(8,128)(2,1)S(1)}, u32[]{:S(2)}) copy-start(bf16[256,128]{1,0:T(8,128)(2,1)S(1)} %collective-permute-done.2.refs_3_) | copy-start | bytes 196612
  29.2 0.6 copy-start.16
  29.8 25.0 %copy-start.13 = (bf16[9,64,64]{2,1,0:T(8,128)(2,1)S(1)}, bf16[9,64,64]{2,1,0:T(8,128)(2,1)}, u32[]{:S(2)}) copy-start(bf16[9,64,64]{2,1,0:T(8,128)(2,1)} %param.16) | copy-start | bytes 221188
  29.8 25.3 %copy-start.14 = (bf16[9,64,64]{2,1,0:T(8,128)(2,1)S(1)}, bf16[9,64,64]{2,1,0:T(8,128)(2,1)}, u32[]{:S(2)}) copy-start(bf16[9,64,64]{2,1,0:T(8,128)(2,1)} %param.17) | copy-start | bytes 221188
  49.8 20.8 %all-to-all-start.1 = ((bf16[32,64,128]{2,1,0:T(8,128)(2,1)}), bf16[32,64,128]{2,1,0:T(8,128)(2,1)S(1)}, u32[]{:S(2)}, u32[]{:S(2)}) async-start(bf16[32,64,128]{2,1,0:T(8,128)(2,1)} %get-tuple-element.20), calls=%async_computation.1 | async-start | bytes 1048576 | tf_op jit(solution)/shard_map/all_to_all | solution.py:808
  55.4 15.2 %copy-start.5 = (s32[9,2048]{1,0:T(8,128)S(1)}, s32[9,2048]{1,0:T(8,128)}, u32[]{:S(2)}) copy-start(s32[9,2048]{1,0:T(8,128)} %refs_5_.1) | copy-start | bytes 221188
  55.5 15.2 %copy-start.6 = (bf16[64,2048]{1,0:T(8,128)(2,1)S(1)}, bf16[64,2048]{1,0:T(8,128)(2,1)}, u32[]{:S(2)}) copy-start(bf16[64,2048]{1,0:T(8,128)(2,1)} %refs_2_.2) | copy-start | bytes 786436
  55.5 15.2 %copy-start.11 = (s32[2048]{0:T(1024)S(1)}, s32[2048]{0:T(1024)}, u32[]{:S(2)}) copy-start(s32[2048]{0:T(1024)} %param.18) | copy-start | bytes 24580
  57.8 29.7 %copy-start.1 = (bf16[24,64,512]{2,0,1:T(8,128)(2,1)}, bf16[24,64,512]{2,0,1:T(8,128)(2,1)S(1)}, u32[]{:S(2)}) copy-start(bf16[24,64,512]{2,0,1:T(8,128)(2,1)S(1)} %copy.33) | copy-start | bytes 4718596
  73.2 14.4 %collective-permute-start.4 = (bf16[80,512]{1,0:T(8,128)(2,1)S(1)}, bf16[80,512]{1,0:T(8,128)(2,1)S(1)}, u32[]{:S(2)}, u32[]{:S(2)}) collective-permute-start(bf16[80,512]{1,0:T(8,128)(2,1)S(1)} %get-tuple-element.24), channel_id=1, source_target_pairs={{0,1},{1,2},{2,3},{3,4},{4,5},{5,6},{6,7},{7,8},{8,9},{9,10},{10,1... | collective-permute-start | bytes 245768 | tf_op jit(solution)/shard_map/ppermute | solution.py:745
  76.1 11.5 %collective-permute-start.5 = (bf16[80,512]{1,0:T(8,128)(2,1)S(1)}, bf16[80,512]{1,0:T(8,128)(2,1)S(1)}, u32[]{:S(2)}, u32[]{:S(2)}) collective-permute-start(bf16[80,512]{1,0:T(8,128)(2,1)S(1)} %get-tuple-element.25), channel_id=1, source_target_pairs={{1,0},{2,1},{3,2},{4,3},{5,4},{6,5},{7,6},{8,7},{9,8},{10,9},{11,1... | collective-permute-start | bytes 245768 | tf_op jit(solution)/shard_map/ppermute | solution.py:746

commit v3 on v2

--- a/solution.py
+++ b/solution.py
@@ -20,7 +20,7 @@
 HBM = pl.BlockSpec(memory_space=pltpu.HBM)
 
 
-def call(body, outs, ins, scratch=(), parts=None, untouched=(), out_specs=None, limit=None):
+def call(body, outs, ins, scratch=(), parts=None, untouched=(), scalars=(), out_specs=None, limit=None):
     if limit is None:
         touched = [i for i in range(len(ins)) if i not in untouched]
 
@@ -69,7 +69,10 @@
         out_shape=outs,
         in_specs=[ANY] * len(ins),
         out_specs=out_specs or jax.tree.map(lambda _: VMEM, outs),
-        scratch_shapes=[pltpu.VMEM(shape, ins[i].dtype) for shape, i in zip(shapes, held)]
+        scratch_shapes=[
+            (pltpu.SMEM if i in scalars else pltpu.VMEM)(shape, ins[i].dtype)
+            for shape, i in zip(shapes, held)
+        ]
         + list(scratch)
         + [pltpu.SemaphoreType.DMA((len(held),))],
         compiler_params=pltpu.CompilerParams(vmem_limit_bytes=limit),
@@ -103,21 +106,52 @@
     return jnp.where(live > 0.5, value, jnp.inf).astype(BF)
 
 
-def slot_table_body(wait, heat_ref, slot_ref, out_ref):
-    wait(0, 1)
+def fold(rows):
+    return jnp.concatenate([rows[e : e + 8] for e in range(0, rows.shape[0], 8)], axis=1)
+
+
+def unfold(block):
+    cols = block.shape[1]
+    return jnp.concatenate([block[:, at : at + LANES] for at in range(0, cols, LANES)], axis=0)
+
+
+def unfolded(code):
+    code = code.astype(F32)
+    return jnp.concatenate([unfold(code[:8]), unfold(code[8:])], axis=0)
+
+
+def payload_body(cell_ref, rows, payloads):
+    count = cell_ref.shape[1] // LANES
+    cells = jnp.concatenate(
+        [cell_ref[:, e * LANES : (e + 1) * LANES] for e in range(count)], axis=0
+    )
+    code = coded(fold(cells))
+    for row_ref, out_ref in zip(rows, payloads):
+        size = row_ref.shape[0]
+        out_ref[0:size] = row_ref[...]
+        out_ref[size:] = code
+
+
+def slot_table_body(
+    wait, heat_ref, slot_ref, cell_ref, low_ref, high_ref, out_ref, low_out, high_out
+):
     rows = out_ref.shape[0]
     table = slot_values(heat_ref, slot_ref, rows)
     out_ref[...] = or_inf(table[:rows], table[rows:])
-
-
-def spread_table_body(wait, heat_ref, slot_ref, spread_ref, out_ref):
+    payload_body(cell_ref, (low_ref, high_ref), (low_out, high_out))
+
+
+def spread_table_body(
+    wait, heat_ref, slot_ref, cell_ref, low_ref, high_ref, spread_ref, out_ref, low_out, high_out
+):
     wait(0, 1)
     count, rows = spread_ref.shape
     table = slot_values(heat_ref, slot_ref, rows)
     pair = jnp.concatenate([table[:rows], table[rows:]], axis=1).astype(BF)
-    wait(2)
+    wait(2, 3, 4, 5)
     spread = jnp.dot(spread_ref[...], pair, preferred_element_type=F32)
     out_ref[...] = or_inf(spread[:, :LANES], spread[:, LANES:]).reshape(out_ref.shape)
+    payload_body(cell_ref, (low_ref, high_ref), (low_out, high_out))
 
 
 def neighbourhoods(faces, tiles):
@@ -130,23 +164,27 @@
     return around
 
 
-def heat_table(ocean, slots, capacity, faces, tiles):
+def heat_table(ocean, slots, cells, low, high, capacity, faces, tiles):
     devices = faces * tiles
     around = neighbourhoods(faces, tiles)
-    ins = [ocean, slots.reshape(1, -1)]
+    ins = [ocean, slots.reshape(1, -1), cells, low, high]
+    payload = jax.ShapeDtypeStruct((low.shape[0] + 16, low.shape[1]), BF)
     if capacity == LANES:
         spread = (around.reshape(-1, 1) == np.arange(devices)).astype(np.float32)
         return call(
             spread_table_body,
-            jax.ShapeDtypeStruct((devices, 16, LANES), BF),
+            (jax.ShapeDtypeStruct((devices, 16, LANES), BF), payload, payload),
             ins + [jnp.asarray(spread, BF)],
             parts={0: (slice(0, 16), slice(None))},
             limit=VMEM_WHOLE,
         )
     rows = devices * capacity // LANES
-    table = call(slot_table_body, jax.ShapeDtypeStruct((rows, LANES), BF), ins)
+    table, low, high = call(
+        slot_table_body, (jax.ShapeDtypeStruct((rows, LANES), BF), payload, payload), ins
+    )
     table = table.reshape(devices, capacity)
-    return jnp.where((around >= 0)[:, :, None], table[np.maximum(around, 0)], jnp.inf).astype(BF)
+    table = jnp.where((around >= 0)[:, :, None], table[np.maximum(around, 0)], jnp.inf)
+    return table.astype(BF), low, high
 
 
 def heat_slots(table, both):
@@ -158,15 +196,8 @@
     return got
 
 
-def live_entry(value, cell, cols, rows, dr):
-    live = value < jnp.inf
-    value = jnp.where(live, value, 0.0)
-    row, col = cell >> (cols.bit_length() - 1), cell & (cols - 1)
-    if dr == -1:
-        live = live & (row >= rows - 2)
-    if dr == 1:
-        live = live & (row < 2)
-    return value, live, row + (rows * dr + 2), col
+def row_and_column(cell, cols):
+    return cell >> (cols.bit_length() - 1), cell & (cols - 1)
 
 
 def for_chunks(count, many, body):
@@ -194,35 +225,81 @@
     )
 
 
-def scatter_own_body(wait, vals_ref, cell_ref, out_ref, left, right, prod):
+def scatter_own_body(
+    wait, vals_ref, cell_ref, weight1_ref, weight2_ref,
+    out_ref, first_ref, second_ref, before_ref, list_ref, left, right, prod, lives, packed, places,
+):
     rows, cols = out_ref.shape
     blocks = cols // LANES
     span = rows * blocks
+    chunks = vals_ref.shape[0]
 
     def chunk(e):
         lanes = lanes_at(e)
-        value, live, row, col = live_entry(
-            vals_ref[e].astype(F32)[0:1], cell_ref[:, lanes], cols, rows, 0
-        )
-        left[:, lanes] = one_hot_heat(value, live, (col >> 7) * rows + row - 2, span)
+        value = vals_ref[e].astype(F32)[0:1]
+        live = value < jnp.inf
+        row, col = row_and_column(cell_ref[:, lanes], cols)
+        high = (col >> 7) * rows + row
+        left[:, lanes] = one_hot_heat(jnp.where(live, value, 0.0), live, high, span)
         right[:, lanes] = one_hot(col & 127, LANES)
-
-    for_chunks(vals_ref.shape[0], 4, chunk)
+        lives[pl.ds(e, 1), :] = jnp.where(live, 1.0, 0.0)
+
+    for_chunks(chunks, 4, chunk)
+
+    def triangle(size, above):
+        row = lax.broadcasted_iota(jnp.int32, (size, size), 0)
+        column = lax.broadcasted_iota(jnp.int32, (size, size), 1)
+        return jnp.where(row < column if above else row > column, 1.0, 0.0).astype(BF)
+
+    live = lives[...].astype(BF)
+    in_row = jnp.dot(live, triangle(LANES, True), preferred_element_type=F32)
+    rows_above = jnp.dot(triangle(chunks, False), live, preferred_element_type=F32)
+    rows_above = jnp.sum(rows_above, axis=1, keepdims=True)
+    before_ref[...] = (in_row + rows_above).astype(jnp.int32)
+    tiles, width = list_ref.shape
+
+    def pack(e):
+        lanes = lanes_at(e)
+        place = jnp.where(lives[pl.ds(e, 1), :] > 0.5, before_ref[pl.ds(e, 1), :], -1)
+        cell = cell_ref[:, lanes]
+        match = lax.broadcasted_iota(jnp.int32, (tiles, LANES), 0) == place >> 8
+        parts = [jnp.where(match, part.astype(F32), 0.0) for part in (cell >> 7, cell & 127)]
+        packed[:, lanes] = jnp.concatenate(parts, axis=0).astype(BF)
+        places[:, lanes] = one_hot(place & (width - 1), width)
+
+    for_chunks(chunks, 4, pack)
+    cells = nt_dot(packed[...], places[...])
+    list_ref[...] = (cells[:tiles] * 128.0 + cells[tiles:]).astype(jnp.int32)
+    stack_weight(weight1_ref, first_ref)
+    stack_weight(weight2_ref, second_ref)
     prod[...] = nt_dot(left[...], right[...])
     for b in range(blocks):
         out_ref[:, b * LANES : (b + 1) * LANES] = mean_heat(prod, b * rows, rows, span, slice(None))
 
 
-def scatter_own(vals, cells, rows, cols):
+def scatter_own(vals, cells, first, second, rows, cols):
     span = rows * (cols // LANES)
+    channels = first.shape[2]
+    slots = cells.size
+    chunks, tiles = slots // LANES, slots // 256
+    stacked = jax.ShapeDtypeStruct((6 * channels, 4 * channels), BF)
     return call(
         scatter_own_body,
-        jax.ShapeDtypeStruct((rows, cols), F32),
-        [vals, cells],
+        (
+            jax.ShapeDtypeStruct((rows, cols), F32),
+            stacked,
+            stacked,
+            jax.ShapeDtypeStruct((chunks, LANES), jnp.int32),
+            jax.ShapeDtypeStruct((tiles, 256), jnp.int32),
+        ),
+        [vals, cells, first, second],
         scratch=[
-            pltpu.VMEM((2 * span, cells.size), BF),
-            pltpu.VMEM((LANES, cells.size), BF),
+            pltpu.VMEM((2 * span, slots), BF),
+            pltpu.VMEM((LANES, slots), BF),
             pltpu.VMEM((2 * span, LANES), F32),
+            pltpu.VMEM((chunks, LANES), F32),
+            pltpu.VMEM((2 * tiles, slots), BF),
+            pltpu.VMEM((256, slots), BF),
         ],
     )
 
@@ -231,20 +308,26 @@
     wait, own_ref, vals_ref, above_ref, below_ref, out_ref, targets, left, right, prod
 ):
     rows, cols = own_ref.shape
-    targets[0] = decoded(above_ref[0:64, cols:])
-    targets[1] = decoded(below_ref[0:64, cols:])
     out_ref[2 : rows + 2, :] = own_ref[...]
+    for n, (ref, dr) in enumerate(((above_ref, -1), (below_ref, 1))):
+        code = unfolded(ref[ref.shape[0] - 16 :])
+        row, col = row_and_column(decoded(code), cols)
+        row = row - (rows - 2) if dr < 0 else row
+        near = (row >= 0) & (row < 2)
+        targets[2 * n] = jnp.where(near, 2 * (col >> 7) + row, -1)
+        targets[2 * n + 1] = col & 127
 
     def chunk(e):
         lanes = lanes_at(e)
         values = vals_ref[e].astype(F32)
-        for n, (dr, _) in enumerate(NEIGHBOURS[1:3]):
-            value, live, row, col = live_entry(
-                values[n + 1 : n + 2], targets[n, pl.ds(e, 1), :], cols, rows, dr
+        for n in range(2):
+            value = values[n + 1 : n + 2]
+            live = value < jnp.inf
+            high, low = (targets[2 * n + part, pl.ds(e, 1), :] for part in range(2))
+            left[16 * n : 16 * (n + 1), lanes] = one_hot_heat(
+                jnp.where(live, value, 0.0), live, high, 8
             )
-            high = 2 * (col >> 7) + row - (0 if dr < 0 else rows + 2)
-            left[16 * n : 16 * (n + 1), lanes] = one_hot_heat(value, live, high, 8)
-            right[n * LANES : (n + 1) * LANES, lanes] = one_hot(col & 127, LANES)
+            right[n * LANES : (n + 1) * LANES, lanes] = one_hot(low, LANES)
 
     for_chunks(vals_ref.shape[0], 4, chunk)
     prod[...] = nt_dot(left[...], right[...])
@@ -262,7 +345,7 @@
         jax.ShapeDtypeStruct((rows + 8, cols), F32),
         [own, vals, above, below],
         scratch=[
-            pltpu.VMEM((2, slots // LANES, LANES), jnp.int32),
+            pltpu.VMEM((4, slots // LANES, LANES), jnp.int32),
             pltpu.VMEM((32, slots), BF),
             pltpu.VMEM((2 * LANES, slots), BF),
             pltpu.VMEM((32, 2 * LANES), F32),
@@ -274,29 +357,28 @@
     for ref, places in ((west_ref, (0, 2, 3)), (east_ref, (1, 4, 5))):
         first = ref.shape[0] - 3 * 64
         for part, place in enumerate(places):
-            targets[place] = decoded(ref[first + 64 * part : first + 64 * (part + 1)])
+            dr, dc = NEIGHBOURS[3 + place]
+            cell = decoded(ref[first + 64 * part : first + 64 * (part + 1)])
+            row, col = row_and_column(cell, cols)
+            row = row + (rows * dr + 2)
+            col = col if dc > 0 else col - (cols - 2)
+            near = (row >= 0) & (row < rows + 4) & (col >= 0) & (col < 2)
+            targets[place] = jnp.where(near, 2 * row + col, -1)
 
     def chunk(e):
         lanes = lanes_at(e)
         values = vals_ref[e].astype(F32)
+        live = values < jnp.inf
+        heats = [jnp.where(live, values, 0.0), jnp.where(live, 1.0, 0.0)]
+        left[:, lanes] = jnp.concatenate(heats, axis=0).astype(BF)
         place = lax.broadcasted_iota(jnp.int32, (64, LANES), 0)
         halves = [jnp.zeros((64, LANES), F32)] * 2
-        heats = []
-        for k, (dr, dc) in enumerate(NEIGHBOURS[3:]):
-            value, live, row, col = live_entry(
-                values[k + 3 : k + 4], targets[k, pl.ds(e, 1), :], cols, rows, dr
-            )
+        for k, (_, dc) in enumerate(NEIGHBOURS[3:]):
             side = 0 if dc < 0 else 1
-            col = col if side else col - (cols - 2)
-            live = live & ((col < 2) if side else (col >= 0))
-            code = jnp.where(live, 2 * row + col, -1)
-            halves[side] = jnp.where(place == code, 1.0, halves[side])
-            heats += [value, jnp.where(live, 1.0, 0.0)]
-        heats.append(jnp.zeros((16 - len(heats), LANES), F32))
-        left[:, lanes] = jnp.concatenate(heats, axis=0).astype(BF)
+            halves[side] = jnp.where(place == targets[k, pl.ds(e, 1), :], 1.0, halves[side])
         right[:, lanes] = jnp.concatenate(halves, axis=0).astype(BF)
 
-    for_chunks(vals_ref.shape[0], 2, chunk)
+    for_chunks(vals_ref.shape[0], 4, chunk)
     prod = nt_dot(left[...], right[...])
     lane = lax.broadcasted_iota(jnp.int32, (1, LANES), 1)
     place = lane & 63
@@ -304,7 +386,7 @@
     for k, (dr, dc) in enumerate(NEIGHBOURS[3:]):
         first, last = {-1: (0, 4), 0: (4, 2 * rows + 4), 1: (2 * rows + 4, 2 * rows + 8)}[dr]
         here = (place >= first) & (place < last) & ((lane >= 64) == (dc > 0))
-        mean = prod[2 * k : 2 * k + 1] / jnp.maximum(prod[2 * k + 1 : 2 * k + 2], 1.0)
+        mean = prod[k + 3 : k + 4] / jnp.maximum(prod[k + 19 : k + 20], 1.0)
         around = jnp.where(here, mean, around)
     return around
 
@@ -329,7 +411,7 @@
     return (code[:half].astype(F32) * 128.0 + code[half:].astype(F32)).astype(jnp.int32)
 
 
-def side_body(wait, air_ref, above_ref, below_ref, cell_ref, west_ref, east_ref):
+def side_body(wait, air_ref, above_ref, below_ref, own_ref, west_ref, east_ref):
     rows, channels, cols = air_ref.shape
 
     def column(i, lanes):
@@ -351,14 +433,14 @@
             total = jnp.where(lane >> 1 == i + half, moved, total)
         ref[0:channels] = total.astype(BF)
         first = channels
-        for part in (coded(cell_ref[...]), above_ref[0:64, cols:], below_ref[0:64, cols:]):
-            ref[first : first + 64] = part
+        for payload in (own_ref, above_ref, below_ref):
+            ref[first : first + 64] = unfolded(payload[2 * channels :]).astype(BF)
             first += 64
 
 
-def sides(air, above, below, cells, ready):
+def sides(air, above, below, own, ready):
     out = jax.ShapeDtypeStruct((air.shape[1] + 3 * 64, LANES), BF)
-    return call(side_body, (out, out), [air, above, below, cells, ready], untouched=(4,))
+    return call(side_body, (out, out), [air, above, below, own, ready], untouched=(4,))
 
 
 def shifted(center, from_left, from_right, at_left, at_right, left_lane, right_lane):
@@ -387,9 +469,9 @@
 
 def atmosphere_body(
     wait, air_ref, above_ref, below_ref, west_ref, east_ref, own_west_ref, own_east_ref, field,
-    vals_ref, cell_ref, heat_weight_ref, weight1_ref, weight2_ref,
+    vals_ref, before_ref, number_ref, list_ref, heat_weight_ref, first_ref, second_ref,
     next_out, send_ref,
-    next_ref, out_done, start, hidden, edge1, edge2, first_ref, second_ref, targets, left, right,
+    next_ref, out_done, start, hidden, edge1, edge2, targets, left, right, compact,
 ):
     rows, channels, cols = next_ref.shape
     taps = 3 * channels
@@ -397,10 +479,7 @@
     edge_ref = [jnp.where(tile > 0, 1.0, 0.0), jnp.where(tile < tiles - 1, 1.0, 0.0)]
     wait(3, 4, 8)
     around = scatter_beside(vals_ref, west_ref, east_ref, targets, left, right, rows, cols)
-    wait(11, 12)
-    stack_weight(weight1_ref, first_ref)
-    stack_weight(weight2_ref, second_ref)
-    wait(0, 1, 2, 5, 6, 7, 9, 10)
+    wait(0, 1, 2, 5, 6, 7, 9, 10, 11, 12, 13, 14)
     lane = lax.broadcasted_iota(jnp.int32, (channels, LANES), 1)
     row = lax.broadcasted_iota(jnp.int32, (channels, channels), 0)
     same = row == lax.broadcasted_iota(jnp.int32, (channels, channels), 1)
@@ -488,8 +567,7 @@
             for stage, late in stages:
                 stage(first + j - late)
 
-        count = last - first
-        for_chunks(count, 3 if count % 3 == 0 else 1, step)
+        for_chunks(last - first, 1, step)
 
     half = rows // 2
     one, two, three = (first_stage, 0), (second_stage, 1), (third_stage, 3)
@@ -502,18 +580,20 @@
 
     copy = pltpu.make_async_copy(next_ref, next_out, out_done.at[0])
     copy.start()
-    gather_cells(next_ref, cell_ref, send_ref)
+    gather_live(next_ref, list_ref, number_ref, compact)
+    spread_live(compact, before_ref, number_ref, send_ref)
     copy.wait()
 
 
-def gather_cells(next_ref, cell_ref, send_ref):
+def gather_live(next_ref, list_ref, number_ref, compact):
     rows, channels, cols = next_ref.shape
     shift = cols.bit_length() - 1
-    width = 256
-    group = 12
+    tiles, width = list_ref.shape
+    group, many = 6, 2
+    compact[...] = jnp.zeros(compact.shape, BF)
 
     def pick(tile):
-        cell = cell_ref[:, lanes_at(tile, width)]
+        cell = list_ref[pl.ds(tile, 1), :]
         low = one_hot(cell & (cols - 1), cols)
         high = (cell >> shift).astype(F32).astype(BF)
         total = jnp.zeros((channels, width), BF)
@@ -523,18 +603,46 @@
             for r in range(group):
                 here = high == jnp.asarray(g + r, BF)
                 total = jnp.where(here, got[r * channels : (r + 1) * channels], total)
+        compact[tile] = total
+
+    def step(i, carry):
+        for part in range(many):
+            pick(i * many + part)
+        return carry
+
+    last = number_ref[number_ref.shape[0] - 1, number_ref.shape[1] - 1] + 1
+    tiles_live = (last + (width - 1)) >> 8
+    lax.fori_loop(0, tiles_live >> 1, step, 0)
+
+    @pl.when((tiles_live & 1) == 1)
+    def _():
+        pick(tiles_live - 1)
+
+
+def spread_live(compact, before_ref, number_ref, send_ref):
+    _, channels, width = compact.shape
+
+    def spread(i):
+        place = jnp.concatenate(
+            [before_ref[pl.ds(2 * i, 1), :], before_ref[pl.ds(2 * i + 1, 1), :]], axis=1
+        )
+        first = number_ref[2 * i, 0] >> 8
+        window = compact[pl.ds(first, 2)].reshape(2 * channels, width)
+        got = jnp.dot(window, one_hot(place & (width - 1), width), preferred_element_type=F32)
+        total = jnp.where(place >> 8 == first, got[:channels], got[channels:]).astype(BF)
         for part in range(width // LANES):
-            send_ref[tile * (width // LANES) + part] = total[:, part * LANES : (part + 1) * LANES]
-
-    for_chunks(cell_ref.shape[1] // width, 4, pick)
+            send_ref[2 * i + part] = total[:, part * LANES : (part + 1) * LANES]
+
+    for_chunks(send_ref.shape[0] * LANES // width, 4, spread)
 
 
 def atmosphere(
-    air, above, below, west, east, to_west, to_east, field, vals, cells, heat_weight, first, second
+    air, above, below, west, east, to_west, to_east, field, vals, before, cells, heat_weight,
+    first, second,
 ):
     rows, channels, cols = air.shape
-    slots = cells.size
-    stacked = pltpu.VMEM((6 * channels, 4 * channels), BF)
+    slots = before.size
+    tiles = cells.shape[0]
     return call(
         atmosphere_body,
         (
@@ -542,9 +650,10 @@
             jax.ShapeDtypeStruct((slots // LANES, channels, LANES), BF),
         ),
         [
-            air, above, below, west, east, to_west, to_east, field, vals, cells,
+            air, above, below, west, east, to_west, to_east, field, vals, before, before, cells,
             heat_weight.reshape(1, -1), first, second,
         ],
+        scalars=(10,),
         out_specs=(HBM, VMEM),
         limit=VMEM_MOST,
         scratch=[
@@ -554,11 +663,10 @@
             pltpu.VMEM((rows + 2, channels, cols), BF),
             pltpu.VMEM((2, channels, LANES), F32),
             pltpu.VMEM((2, channels, LANES), F32),
-            stacked,
-            stacked,
             pltpu.VMEM((6, slots // LANES, LANES), jnp.int32),
-            pltpu.VMEM((16, slots), BF),
+            pltpu.VMEM((32, slots), BF),
             pltpu.VMEM((LANES, slots), BF),
+            pltpu.VMEM((tiles + 1, channels, 256), BF),
         ],
     )
 
@@ -766,30 +874,27 @@
     capacity = slot_space // devices
     channels, rows, cols = atmos.shape
 
-    table = heat_table(ocean, marine_coupling_slot, capacity, faces, tiles)
-    table, atmos, own_cells = lax.optimization_barrier(
-        (table, atmos, coupling_air_cells.reshape(-1, LANES))
-    )
+    def two_rows(first):
+        return jnp.transpose(atmos[:, first : first + 2], (1, 0, 2)).reshape(2 * channels, cols)
+
+    table, low, high = heat_table(
+        ocean, marine_coupling_slot, coupling_air_cells, two_rows(0), two_rows(rows - 2),
+        capacity, faces, tiles,
+    )
+    above, below = from_neighbours(low, high, "tile")
     heat = heat_slots(table, both)
 
-    code = coded(own_cells)
-    code = jnp.concatenate([code, jnp.zeros((2 * channels - code.shape[0], LANES), BF)], axis=0)
-
-    def two_rows(first):
-        two = jnp.transpose(atmos[:, first : first + 2], (1, 0, 2)).reshape(2 * channels, cols)
-        return jnp.concatenate([two, code], axis=1)
-
-    above, below = from_neighbours(two_rows(0), two_rows(rows - 2), "tile")
-
     air = jnp.transpose(atmos, (1, 0, 2))
-    field = scatter_own(heat, coupling_air_cells, rows, cols)
-    to_west, to_east = sides(air, above, below, own_cells, field)
+    field, first, second, before, live_cells = scatter_own(
+        heat, coupling_air_cells, air_conv_first_weight, air_conv_second_weight, rows, cols
+    )
+    to_west, to_east = sides(air, above, below, low, field)
     west, east = from_neighbours(to_west, to_east, "face", closed=True)
 
     field = scatter_ends(field, heat, above, below)
     air_next, outgoing = atmosphere(
-        air, above, below, west, east, to_west, to_east, field, heat, coupling_air_cells,
-        surface_heat_weight, air_conv_first_weight, air_conv_second_weight,
+        air, above, below, west, east, to_west, to_east, field, heat, before, live_cells,
+        surface_heat_weight, first, second,
     )
     air_out = jnp.transpose(air_next, (1, 0, 2))
 
@@ -814,14 +919,14 @@
     ocean_start, head, tail = add_forcing(
         arrived, marine_coupling_slot, ocean, marine_neighbour_index, air_out, first_mix, second_mix
     )
-    before, after = from_neighbours(head, tail, both)
+    ocean_before, ocean_after = from_neighbours(head, tail, both)
     inner, done = ocean_inner(ocean_start, marine_neighbour_index, first_mix, second_mix)
     ocean_next = ocean_outer(
         ocean_start,
         inner,
         done,
-        before,
-        after,
+        ocean_before,
+        ocean_after,
         marine_neighbour_index,
         first_mix,
         second_mix,

time: 92 us -> 89.4 us (0.972)
  local copies, waits for them, and re-layouts: 6.12 us -> 8.85 us
  waiting for transfers between devices: 17.8 us -> 15.3 us
  starting transfers between devices: 27.8 us -> 26.6 us
    ppermute x3, waiting for transfers between devices: 4.89 us -> 1.36 us  [from_neighbours(): after = lax.ppermute(low, axis, [((i + 1) % count, i) for i in range(ends)])]
    pallas_call x2, Pallas kernels: 22 us -> 19.7 us  [call(): pl.pallas_call(kernel, out_shape=outs, in_specs=[ANY] * len(ins), out_spe...]
    unnamed x34 -> x47, local copies, waits for them, and re-layouts: 1.26 us -> 3.18 us
    pallas_call x6, Pallas kernels: 15.9 us -> 17.4 us  [call(): pl.pallas_call(plain, out_shape=outs, in_specs=[VMEM if i in touched else...]
    transpose x3, local copies, waits for them, and re-layouts: 1.44 us -> 2.76 us  [two_rows(): jnp.transpose(atmos[:, first:first + 2], (1, 0, 2))]
  transfers between devices with their start and end apart: 8 -> 8, of which waited for: 4 -> 4; matrix products, arithmetic and copies ran while one was open for 6% -> 5% of each run, Pallas kernels for 10% -> 12%
where the time goes in v3:
time: 89.4 us; the launch traced here: 88.9 us
  Pallas kernels  37.1 us (41%)
  starting transfers between devices  26.6 us (30%)
  waiting for transfers between devices  15.3 us (17%)
  local copies, waits for them, and re-layouts  8.85 us (10%)
  between operations  1 us (1%)
    pallas_call x2, Pallas kernels, call(): pl.pallas_call(kernel, out_shape=outs, in_specs=[ANY] * len(ins), out_spe...  19.7 us
    pallas_call x6, Pallas kernels, call(): pl.pallas_call(plain, out_shape=outs, in_specs=[VMEM if i in touched else...  17.4 us
    all_to_all x1, waiting for transfers between devices, shards(): lax.all_to_all(outgoing, both, split_axis=0, concat_axis=0, tiled=True)  12.8 us
    ppermute x3, starting transfers between devices, from_neighbours(): lax.ppermute(high, axis, [(i, (i + 1) % count) for i in range(ends)])  8.57 us
    all_to_all x1, starting transfers between devices, heat_slots(): got = lax.all_to_all(table, both, split_axis=0, concat_axis=0, tiled=True)  7.1 us
    ppermute x3, starting transfers between devices, from_neighbours(): after = lax.ppermute(low, axis, [((i + 1) % count, i) for i in range(ends)])  6.83 us
    all_to_all x1, starting transfers between devices, shards(): lax.all_to_all(outgoing, both, split_axis=0, concat_axis=0, tiled=True)  4.13 us
    unnamed x47, local copies, waits for them, and re-layouts  3.18 us
  transfers between devices with their start and end apart: 8, of which 4 were waited for; matrix products, arithmetic and copies ran while one was open for 5% of the time, Pallas kernels for 12%

profile of v3, /device:TPU:1, one launch (start us, length us, event | category | flops | bytes accessed | tf_op | source)
XLA Modules:
  0.0 88.9 jit_solution(7975083523414707988)
XLA Ops:
  0.6 1.4 %slice_bitcast_fusion = (bf16[2,64,512]{2,0,1:T(2,128)(2,1)S(1)}, bf16[2,64,512]{2,0,1:T(2,128)(2,1)S(1)}) fusion(bf16[64,24,512]{2,1,0:T(8,128)(2,1)} %param.11), kind=kLoop, calls=%fused_computation.2 | loop fusion | bytes 524288 | tf_op jit(solution)/shard_map/transpose | solution.py:878
  2.0 0.7 copy.20
  2.7 0.7 copy.21
  3.4 2.2 %shard_map.122 = (bf16[32,16,128]{2,1,0:T(8,128)(2,1)}, bf16[144,512]{1,0:T(8,128)(2,1)}, bf16[144,512]{1,0:T(8,128)(2,1)}) custom-call(bf16[64,2048]{1,0:T(8,128)(2,1)} %refs_2_.5, s32[1,2048]{1,0:T(1,128)} %bitcast.22, s32[1,4096]{1,0:T(1,128)} %refs_1_.2, bf16[128,512]{1,0:T(8,128)(2,1)} %bitcast.26, bf16[128,512]{1,0:T(8,128)(2,1)} %bitcast.27, ...), custom_call_target="tpu_custom_call" | custom-call | tf_op jit(solution)/shard_map/pallas_call | solution.py:67
  5.6 7.1 %all-to-all-start = ((bf16[32,16,128]{2,1,0:T(8,128)(2,1)}), bf16[32,16,128]{2,1,0:T(8,128)(2,1)S(1)}, u32[]{:S(2)}, u32[]{:S(2)}) async-start(bf16[32,16,128]{2,1,0:T(8,128)(2,1)} %get-tuple-element.21), calls=%async_computation | async-start | bytes 262144 | tf_op jit(solution)/shard_map/all_to_all | solution.py:192
  12.7 1.3 %collective-permute-start.1 = (bf16[144,512]{1,0:T(8,128)(2,1)}, bf16[144,512]{1,0:T(8,128)(2,1)S(1)}, u32[]{:S(2)}, u32[]{:S(2)}) collective-permute-start(bf16[144,512]{1,0:T(8,128)(2,1)} %get-tuple-element.20.refs_3_), channel_id=1, source_target_pairs={{1,0},{2,1},{3,2},{4,3},{5,4},{6,5},{7,6},{9,8},{10,9},{11,10},{12... | collective-permute-start | bytes 442376 | tf_op jit(solution)/shard_map/ppermute | solution.py:854
  14.0 0.0 copy-start.14
  14.0 4.1 %collective-permute-start = (bf16[144,512]{1,0:T(8,128)(2,1)}, bf16[144,512]{1,0:T(8,128)(2,1)S(1)}, u32[]{:S(2)}, u32[]{:S(2)}) collective-permute-start(bf16[144,512]{1,0:T(8,128)(2,1)} %get-tuple-element.19), channel_id=1, source_target_pairs={{0,1},{1,2},{2,3},{3,4},{4,5},{5,6},{6,7},{8,9},{9,10},{10,11},{11... | collective-permute-start | bytes 442376 | tf_op jit(solution)/shard_map/ppermute | solution.py:853
  18.2 1.9 %copy.34 = bf16[64,24,512]{2,0,1:T(8,128)(2,1)S(1)} copy(bf16[64,24,512]{2,1,0:T(8,128)(2,1)} %param.11) | data formatting | bytes 3145728 | tf_op args[0]
  20.1 0.2 all-to-all-done.refs_0_.refs_1_.refs_8_
  20.3 3.0 %shard_map.123 = (f32[24,512]{1,0:T(8,128)S(1)}, bf16[384,256]{1,0:T(8,128)(2,1)S(1)}, bf16[384,256]{1,0:T(8,128)(2,1)S(1)}, s32[32,128]{1,0:T(8,128)S(1)}, s32[16,256]{1,0:T(8,128)S(1)}) custom-call(bf16[32,16,128]{2,1,0:T(8,128)(2,1)S(1)} %all-to-all-done.refs_0_.refs_1_.refs_8_, s32[1,4096]{1,0:T(1,128)S(1)} %copy-done.14, ...), custom_call_target="tpu_custom_call" | custom-call | tf_op jit(solution)/shard_map/pallas_call | solution.py:30
  23.3 0.0 copy-start.8
  23.4 0.9 %collective-permute-done.refs_1_.refs_2_ = bf16[144,512]{1,0:T(8,128)(2,1)S(1)} collective-permute-done((bf16[144,512]{1,0:T(8,128)(2,1)}, bf16[144,512]{1,0:T(8,128)(2,1)S(1)}, u32[]{:S(2)}, u32[]{:S(2)}) %collective-permute-start) | collective-permute-done | bytes 147488 | tf_op jit(solution)/shard_map/ppermute | solution.py:853
  24.3 0.3 shard_map.124
  24.6 1.5 %collective-permute-start.2 = (bf16[256,128]{1,0:T(8,128)(2,1)S(1)}, bf16[256,128]{1,0:T(8,128)(2,1)S(1)}, u32[]{:S(2)}, u32[]{:S(2)}) collective-permute-start(bf16[256,128]{1,0:T(8,128)(2,1)S(1)} %get-tuple-element.23.refs_6_), channel_id=1, source_target_pairs={{0,8},{8,16},{16,24},{24,0},{1,9},{9,17},{17,25},{25,1},{2,10},{10... | collective-permute-start | bytes 196616 | tf_op jit(solution)/shard_map/ppermute | solution.py:853
  26.2 1.7 %shard_map.125.refs_7_ = f32[32,512]{1,0:T(8,128)S(1)} custom-call(f32[24,512]{1,0:T(8,128)S(1)} %get-tuple-element.22.refs_4_.refs_0_, bf16[32,16,128]{2,1,0:T(8,128)(2,1)S(1)} %all-to-all-done.refs_0_.refs_1_.refs_8_, bf16[144,512]{1,0:T(8,128)(2,1)S(1)} %collective-permute-done.refs_1_.refs_2_, bf16[144,512]{1,0:T(8,128)(2,1)S(1)} %collective-permute-done.1.refs_2_.refs_3_), custom_call_target="tpu_custom_call" | custom-call | tf_op jit(solution)/shard_map/pallas_call | solution.py:30
  27.9 0.6 copy-done.7
  28.5 1.4 %collective-permute-done.3.refs_4_ = bf16[256,128]{1,0:T(8,128)(2,1)S(1)} collective-permute-done((bf16[256,128]{1,0:T(8,128)(2,1)S(1)}, bf16[256,128]{1,0:T(8,128)(2,1)S(1)}, u32[]{:S(2)}, u32[]{:S(2)}) %collective-permute-start.3) | collective-permute-done | bytes 65568 | tf_op jit(solution)/shard_map/ppermute | solution.py:854
  29.9 0.6 copy-done.22
  30.5 17.5 %shard_map.126 = (bf16[24,64,512]{2,1,0:T(8,128)(2,1)}, bf16[32,64,128]{2,1,0:T(8,128)(2,1)}) custom-call(bf16[24,64,512]{2,1,0:T(8,128)(2,1)} %bitcast.19, bf16[144,512]{1,0:T(8,128)(2,1)} %copy-done.4, bf16[144,512]{1,0:T(8,128)(2,1)} %copy-done.3, bf16[256,128]{1,0:T(8,128)(2,1)} %copy-done.21, bf16[256,128]{1,0:T(8,128)(2,1)} %copy-done.22, ...), custom_call_target="tpu_custom_call" | custom-call | tf_op jit(solution)/shard_map/pallas_call | solution.py:67
  48.0 4.1 %all-to-all-start.1 = ((bf16[32,64,128]{2,1,0:T(8,128)(2,1)}), bf16[32,64,128]{2,1,0:T(8,128)(2,1)S(1)}, u32[]{:S(2)}, u32[]{:S(2)}) async-start(bf16[32,64,128]{2,1,0:T(8,128)(2,1)} %get-tuple-element.30), calls=%async_computation.1 | async-start | bytes 1048576 | tf_op jit(solution)/shard_map/all_to_all | solution.py:913
  52.2 0.1 copy.23
  52.3 0.1 copy.25.refs_5_.refs_2_.refs_6_
  52.5 0.1 copy.24
  52.6 0.1 copy.26.refs_6_.refs_3_.refs_7_
  52.8 2.3 %copy.33 = bf16[24,64,512]{2,0,1:T(8,128)(2,1)S(1)} copy(bf16[24,64,512]{2,1,0:T(8,128)(2,1)} %get-tuple-element.29) | data formatting | bytes 3145728 | tf_op jit(solution)/shard_map/pallas_call | solution.py:67
  55.1 12.8 %all-to-all-done.1.refs_0_ = bf16[32,64,128]{2,1,0:T(8,128)(2,1)S(1)} async-done(((bf16[32,64,128]{2,1,0:T(8,128)(2,1)}), bf16[32,64,128]{2,1,0:T(8,128)(2,1)S(1)}, u32[]{:S(2)}, u32[]{:S(2)}) %all-to-all-start.1) | async-done | bytes 524320 | tf_op jit(solution)/shard_map/all_to_all | solution.py:913
  68.0 2.5 %shard_map.127 = (bf16[64,2048]{1,0:T(8,128)(2,1)S(1)}, bf16[80,512]{1,0:T(8,128)(2,1)S(1)}, bf16[80,512]{1,0:T(8,128)(2,1)S(1)}) custom-call(bf16[32,64,128]{2,1,0:T(8,128)(2,1)S(1)} %all-to-all-done.1.refs_0_, s32[1,2048]{1,0:T(1,128)S(1)} %bitcast.23, bf16[64,2048]{1,0:T(8,128)(2,1)S(1)} %copy-done.6, s32[9,2048]{1,0:T(8,128)S(1)} %copy-done.5, ...), custom_call_target="tpu_custom_call" | custom-call | tf_op jit(solution)/shard_map/pallas_call | solution.py:30
  70.5 2.9 %collective-permute-start.4 = (bf16[80,512]{1,0:T(8,128)(2,1)S(1)}, bf16[80,512]{1,0:T(8,128)(2,1)S(1)}, u32[]{:S(2)}, u32[]{:S(2)}) collective-permute-start(bf16[80,512]{1,0:T(8,128)(2,1)S(1)} %get-tuple-element.34), channel_id=1, source_target_pairs={{0,1},{1,2},{2,3},{3,4},{4,5},{5,6},{6,7},{7,8},{8,9},{9,10},{10,1... | collective-permute-start | bytes 245768 | tf_op jit(solution)/shard_map/ppermute | solution.py:853
  73.4 5.5 %collective-permute-start.5 = (bf16[80,512]{1,0:T(8,128)(2,1)S(1)}, bf16[80,512]{1,0:T(8,128)(2,1)S(1)}, u32[]{:S(2)}, u32[]{:S(2)}) collective-permute-start(bf16[80,512]{1,0:T(8,128)(2,1)S(1)} %get-tuple-element.35), channel_id=1, source_target_pairs={{1,0},{2,1},{3,2},{4,3},{5,4},{6,5},{7,6},{8,7},{9,8},{10,9},{11,1... | collective-permute-start | bytes 245768 | tf_op jit(solution)/shard_map/ppermute | solution.py:854
  78.9 5.9 %shard_map.128 = (bf16[6,64,256]{2,1,0:T(8,128)(2,1)S(1)}, bf16[64,1024]{1,0:T(8,128)(2,1)S(1)}) custom-call(bf16[64,2048]{1,0:T(8,128)(2,1)S(1)} %get-tuple-element.31.refs_0_, s32[9,2048]{1,0:T(8,128)S(1)} %copy-done.5, bf16[64,576]{1,0:T(8,128)(2,1)S(1)} %copy.25.refs_5_.refs_2_.refs_6_, bf16[64,576]{1,0:T(8,128)(2,1)S(1)} %copy.26.refs_6_.refs_3_.refs_7_), custom_call_target="tpu_custom_call" | custom-call | tf_op jit(solution)/shard_map/pallas_call | solution.py:30
  84.9 4.0 %shard_map.129 = bf16[64,2048]{1,0:T(8,128)(2,1)} custom-call(bf16[64,2048]{1,0:T(8,128)(2,1)S(1)} %get-tuple-element.31.refs_0_, bf16[6,64,256]{2,1,0:T(8,128)(2,1)S(1)} %get-tuple-element.32.refs_1_, bf16[64,1024]{1,0:T(8,128)(2,1)S(1)} %get-tuple-element.33.refs_2_, bf16[80,512]{1,0:T(8,128)(2,1)S(1)} %collective-permute-done.4.refs_3_, ...), custom_call_target="tpu_custom_call" | custom-call | tf_op jit(solution)/shard_map/pallas_call | solution.py:30
  (47 shorter events, 0.1 us)
Async XLA Ops:
  5.6 14.7 %all-to-all-start = ((bf16[32,16,128]{2,1,0:T(8,128)(2,1)}), bf16[32,16,128]{2,1,0:T(8,128)(2,1)S(1)}, u32[]{:S(2)}, u32[]{:S(2)}) async-start(bf16[32,16,128]{2,1,0:T(8,128)(2,1)} %get-tuple-element.21), calls=%async_computation | async-start | bytes 262144 | tf_op jit(solution)/shard_map/all_to_all | solution.py:192
  12.7 10.7 %collective-permute-start.1 = (bf16[144,512]{1,0:T(8,128)(2,1)}, bf16[144,512]{1,0:T(8,128)(2,1)S(1)}, u32[]{:S(2)}, u32[]{:S(2)}) collective-permute-start(bf16[144,512]{1,0:T(8,128)(2,1)} %get-tuple-element.20.refs_3_), channel_id=1, source_target_pairs={{1,0},{2,1},{3,2},{4,3},{5,4},{6,5},{7,6},{9,8},{10,9},{11,10},{12... | collective-permute-start | bytes 442376 | tf_op jit(solution)/shard_map/ppermute | solution.py:854
  14.0 6.3 %copy-start.11 = (bf16[3,3,64,64]{3,2,1,0:T(8,128)(2,1)S(1)}, bf16[3,3,64,64]{3,2,1,0:T(8,128)(2,1)}, u32[]{:S(2)}) copy-start(bf16[3,3,64,64]{3,2,1,0:T(8,128)(2,1)} %refs_2_.4) | copy-start | bytes 221188
  14.0 6.3 %copy-start.12 = (bf16[3,3,64,64]{3,2,1,0:T(8,128)(2,1)S(1)}, bf16[3,3,64,64]{3,2,1,0:T(8,128)(2,1)}, u32[]{:S(2)}) copy-start(bf16[3,3,64,64]{3,2,1,0:T(8,128)(2,1)} %refs_3_.2) | copy-start | bytes 221188
  14.0 6.3 %copy-start.14 = (s32[1,4096]{1,0:T(1,128)S(1)}, s32[1,4096]{1,0:T(1,128)}, u32[]{:S(2)}) copy-start(s32[1,4096]{1,0:T(1,128)} %refs_1_.2) | copy-start | bytes 49156
  14.0 10.3 %copy-start.10 = (bf16[144,512]{1,0:T(8,128)(2,1)S(1)}, bf16[144,512]{1,0:T(8,128)(2,1)}, u32[]{:S(2)}) copy-start(bf16[144,512]{1,0:T(8,128)(2,1)} %get-tuple-element.20.refs_3_) | copy-start | bytes 442372
  14.0 10.3 %collective-permute-start = (bf16[144,512]{1,0:T(8,128)(2,1)}, bf16[144,512]{1,0:T(8,128)(2,1)S(1)}, u32[]{:S(2)}, u32[]{:S(2)}) collective-permute-start(bf16[144,512]{1,0:T(8,128)(2,1)} %get-tuple-element.19), channel_id=1, source_target_pairs={{0,1},{1,2},{2,3},{3,4},{4,5},{5,6},{6,7},{8,9},{9,10},{10,11},{11... | collective-permute-start | bytes 442376 | tf_op jit(solution)/shard_map/ppermute | solution.py:853
  20.1 9.8 %copy-start = (bf16[64,24,512]{2,0,1:T(8,128)(2,1)}, bf16[64,24,512]{2,0,1:T(8,128)(2,1)S(1)}, u32[]{:S(2)}) copy-start(bf16[64,24,512]{2,0,1:T(8,128)(2,1)S(1)} %copy.34) | copy-start | bytes 4718596
  20.3 9.6 %copy-start.2 = (bf16[32,16,128]{2,1,0:T(8,128)(2,1)}, bf16[32,16,128]{2,1,0:T(8,128)(2,1)S(1)}, u32[]{:S(2)}) copy-start(bf16[32,16,128]{2,1,0:T(8,128)(2,1)S(1)} %all-to-all-done.refs_0_.refs_1_.refs_8_) | copy-start | bytes 393220
  23.3 2.9 %copy-start.18 = (s32[16,256]{1,0:T(8,128)}, s32[16,256]{1,0:T(8,128)S(1)}, u32[]{:S(2)}) copy-start(s32[16,256]{1,0:T(8,128)S(1)} %get-tuple-element.26.refs_11_) | copy-start | bytes 49156
  23.3 4.6 %copy-start.8 = (bf16[384,256]{1,0:T(8,128)(2,1)}, bf16[384,256]{1,0:T(8,128)(2,1)S(1)}, u32[]{:S(2)}) copy-start(bf16[384,256]{1,0:T(8,128)(2,1)S(1)} %get-tuple-element.27.refs_13_) | copy-start | bytes 589828
  23.3 5.2 %copy-start.9 = (bf16[384,256]{1,0:T(8,128)(2,1)}, bf16[384,256]{1,0:T(8,128)(2,1)S(1)}, u32[]{:S(2)}) copy-start(bf16[384,256]{1,0:T(8,128)(2,1)S(1)} %get-tuple-element.28.refs_14_) | copy-start | bytes 589828
  23.3 6.5 %copy-start.13 = (s32[32,128]{1,0:T(8,128)}, s32[32,128]{1,0:T(8,128)S(1)}, u32[]{:S(2)}) copy-start(s32[32,128]{1,0:T(8,128)S(1)} %get-tuple-element.25.refs_9_.refs_10_) | copy-start | bytes 49156
  23.4 6.5 %copy-start.3 = (bf16[144,512]{1,0:T(8,128)(2,1)}, bf16[144,512]{1,0:T(8,128)(2,1)S(1)}, u32[]{:S(2)}) copy-start(bf16[144,512]{1,0:T(8,128)(2,1)S(1)} %collective-permute-done.1.refs_2_.refs_3_) | copy-start | bytes 442372
  24.3 5.6 %copy-start.4 = (bf16[144,512]{1,0:T(8,128)(2,1)}, bf16[144,512]{1,0:T(8,128)(2,1)S(1)}, u32[]{:S(2)}) copy-start(bf16[144,512]{1,0:T(8,128)(2,1)S(1)} %collective-permute-done.refs_1_.refs_2_) | copy-start | bytes 442372
  24.6 5.3 %copy-start.15 = (bf16[256,128]{1,0:T(8,128)(2,1)}, bf16[256,128]{1,0:T(8,128)(2,1)S(1)}, u32[]{:S(2)}) copy-start(bf16[256,128]{1,0:T(8,128)(2,1)S(1)} %get-tuple-element.24.refs_5_) | copy-start | bytes 196612
  24.6 5.3 %copy-start.16 = (bf16[256,128]{1,0:T(8,128)(2,1)}, bf16[256,128]{1,0:T(8,128)(2,1)S(1)}, u32[]{:S(2)}) copy-start(bf16[256,128]{1,0:T(8,128)(2,1)S(1)} %get-tuple-element.23.refs_6_) | copy-start | bytes 196612
  24.6 3.9 %collective-permute-start.2 = (bf16[256,128]{1,0:T(8,128)(2,1)S(1)}, bf16[256,128]{1,0:T(8,128)(2,1)S(1)}, u32[]{:S(2)}, u32[]{:S(2)}) collective-permute-start(bf16[256,128]{1,0:T(8,128)(2,1)S(1)} %get-tuple-element.23.refs_6_), channel_id=1, source_target_pairs={{0,8},{8,16},{16,24},{24,0},{1,9},{9,17},{17,25},{25,1},{2,10},{10... | collective-permute-start | bytes 196616 | tf_op jit(solution)/shard_map/ppermute | solution.py:853
  26.2 3.7 %collective-permute-start.3 = (bf16[256,128]{1,0:T(8,128)(2,1)S(1)}, bf16[256,128]{1,0:T(8,128)(2,1)S(1)}, u32[]{:S(2)}, u32[]{:S(2)}) collective-permute-start(bf16[256,128]{1,0:T(8,128)(2,1)S(1)} %get-tuple-element.24.refs_5_), channel_id=1, source_target_pairs={{8,0},{16,8},{24,16},{0,24},{9,1},{17,9},{25,17},{1,25},{10,2},{18... | collective-permute-start | bytes 196616 | tf_op jit(solution)/shard_map/ppermute | solution.py:854
  27.9 0.6 copy-start.7
  28.5 1.4 %copy-start.21 = (bf16[256,128]{1,0:T(8,128)(2,1)}, bf16[256,128]{1,0:T(8,128)(2,1)S(1)}, u32[]{:S(2)}) copy-start(bf16[256,128]{1,0:T(8,128)(2,1)S(1)} %collective-permute-done.2.refs_3_) | copy-start | bytes 196612
  29.9 0.6 copy-start.22
  30.5 21.7 %copy-start.19 = (bf16[9,64,64]{2,1,0:T(8,128)(2,1)S(1)}, bf16[9,64,64]{2,1,0:T(8,128)(2,1)}, u32[]{:S(2)}) copy-start(bf16[9,64,64]{2,1,0:T(8,128)(2,1)} %param.16) | copy-start | bytes 221188
  30.5 22.0 %copy-start.20 = (bf16[9,64,64]{2,1,0:T(8,128)(2,1)S(1)}, bf16[9,64,64]{2,1,0:T(8,128)(2,1)}, u32[]{:S(2)}) copy-start(bf16[9,64,64]{2,1,0:T(8,128)(2,1)} %param.17) | copy-start | bytes 221188
  48.0 19.9 %all-to-all-start.1 = ((bf16[32,64,128]{2,1,0:T(8,128)(2,1)}), bf16[32,64,128]{2,1,0:T(8,128)(2,1)S(1)}, u32[]{:S(2)}, u32[]{:S(2)}) async-start(bf16[32,64,128]{2,1,0:T(8,128)(2,1)} %get-tuple-element.30), calls=%async_computation.1 | async-start | bytes 1048576 | tf_op jit(solution)/shard_map/all_to_all | solution.py:913
  52.8 15.2 %copy-start.5 = (s32[9,2048]{1,0:T(8,128)S(1)}, s32[9,2048]{1,0:T(8,128)}, u32[]{:S(2)}) copy-start(s32[9,2048]{1,0:T(8,128)} %refs_5_.2) | copy-start | bytes 221188
  52.8 15.2 %copy-start.6 = (bf16[64,2048]{1,0:T(8,128)(2,1)S(1)}, bf16[64,2048]{1,0:T(8,128)(2,1)}, u32[]{:S(2)}) copy-start(bf16[64,2048]{1,0:T(8,128)(2,1)} %refs_2_.5) | copy-start | bytes 786436
  52.8 15.2 %copy-start.17 = (s32[2048]{0:T(1024)S(1)}, s32[2048]{0:T(1024)}, u32[]{:S(2)}) copy-start(s32[2048]{0:T(1024)} %param.18) | copy-start | bytes 24580
  55.1 29.7 %copy-start.1 = (bf16[24,64,512]{2,0,1:T(8,128)(2,1)}, bf16[24,64,512]{2,0,1:T(8,128)(2,1)S(1)}, u32[]{:S(2)}) copy-start(bf16[24,64,512]{2,0,1:T(8,128)(2,1)S(1)} %copy.33) | copy-start | bytes 4718596
  70.5 14.4 %collective-permute-start.4 = (bf16[80,512]{1,0:T(8,128)(2,1)S(1)}, bf16[80,512]{1,0:T(8,128)(2,1)S(1)}, u32[]{:S(2)}, u32[]{:S(2)}) collective-permute-start(bf16[80,512]{1,0:T(8,128)(2,1)S(1)} %get-tuple-element.34), channel_id=1, source_target_pairs={{0,1},{1,2},{2,3},{3,4},{4,5},{5,6},{6,7},{7,8},{8,9},{9,10},{10,1... | collective-permute-start | bytes 245768 | tf_op jit(solution)/shard_map/ppermute | solution.py:853
  73.4 11.5 %collective-permute-start.5 = (bf16[80,512]{1,0:T(8,128)(2,1)S(1)}, bf16[80,512]{1,0:T(8,128)(2,1)S(1)}, u32[]{:S(2)}, u32[]{:S(2)}) collective-permute-start(bf16[80,512]{1,0:T(8,128)(2,1)S(1)} %get-tuple-element.35), channel_id=1, source_target_pairs={{1,0},{2,1},{3,2},{4,3},{5,4},{6,5},{7,6},{8,7},{9,8},{10,9},{11,1... | collective-permute-start | bytes 245768 | tf_op jit(solution)/shard_map/ppermute | solution.py:854

commit v4 on v3

--- a/solution.py
+++ b/solution.py
@@ -127,9 +127,10 @@
     )
     code = coded(fold(cells))
     for row_ref, out_ref in zip(rows, payloads):
-        size = row_ref.shape[0]
-        out_ref[0:size] = row_ref[...]
-        out_ref[size:] = code
+        size = row_ref.shape[1]
+        out_ref[0:size] = row_ref[0]
+        out_ref[size : 2 * size] = row_ref[1]
+        out_ref[2 * size :] = code
 
 
 def slot_table_body(
@@ -164,23 +165,29 @@
     return around
 
 
-def heat_table(ocean, slots, cells, low, high, capacity, faces, tiles):
+def heat_table(ocean, slots, cells, air, capacity, faces, tiles):
     devices = faces * tiles
     around = neighbourhoods(faces, tiles)
-    ins = [ocean, slots.reshape(1, -1), cells, low, high]
-    payload = jax.ShapeDtypeStruct((low.shape[0] + 16, low.shape[1]), BF)
+    rows, channels, cols = air.shape
+    ins = [ocean, slots.reshape(1, -1), cells]
+    payload = jax.ShapeDtypeStruct((2 * channels + 16, cols), BF)
+    every = slice(None)
     if capacity == LANES:
         spread = (around.reshape(-1, 1) == np.arange(devices)).astype(np.float32)
         return call(
             spread_table_body,
             (jax.ShapeDtypeStruct((devices, 16, LANES), BF), payload, payload),
-            ins + [jnp.asarray(spread, BF)],
-            parts={0: (slice(0, 16), slice(None))},
+            ins + [air, air, jnp.asarray(spread, BF)],
+            parts={
+                0: (slice(0, 16), every),
+                3: (slice(0, 2), every, every),
+                4: (slice(rows - 2, rows), every, every),
+            },
             limit=VMEM_WHOLE,
         )
-    rows = devices * capacity // LANES
+    table = jax.ShapeDtypeStruct((devices * capacity // LANES, LANES), BF)
     table, low, high = call(
-        slot_table_body, (jax.ShapeDtypeStruct((rows, LANES), BF), payload, payload), ins
+        slot_table_body, (table, payload, payload), ins + [air[:2], air[rows - 2 :]]
     )
     table = table.reshape(devices, capacity)
     table = jnp.where((around >= 0)[:, :, None], table[np.maximum(around, 0)], jnp.inf)
@@ -683,8 +690,8 @@
     shift = depth.bit_length() - 1
     width = 256
 
-    def block(b, carry):
-        lanes = pl.ds(pl.multiple_of(b * width, width), width)
+    def block(b):
+        lanes = lanes_at(b, width)
         slot = slot_ref[:, lanes]
         low = one_hot(slot & (depth - 1), depth)
         high = slot >> shift
@@ -695,10 +702,9 @@
         for g in range(1, groups):
             total = jnp.where(high == g, got[g * channels : (g + 1) * channels], total)
         out_ref[:, lanes] = (ocean_ref[:, lanes].astype(F32) + total).astype(BF)
-        return carry
 
     channels, cells = ocean_ref.shape
-    lax.fori_loop(0, cells // width, block, 0)
+    for_chunks(cells // width, 2, block)
     reach = 2 * HALO
     for ref, first, start in ((head_ref, 0, 0), (tail_ref, cells - reach, cells - HALO)):
         ref[0:channels] = out_ref[:, first : first + reach]
@@ -760,19 +766,16 @@
     for b in range(blocks - 2):
         local[b, 0:taps] = own_positions(index_ref, b + 1)
 
-    def hide(b, carry):
+    def hide(b):
         hide_block(hidden_ref, b, values, b, local[b, 0:taps], first_ref)
-        return carry
-
-    lax.fori_loop(0, blocks - 2, hide, 0)
-
-    def finish(b, carry):
+
+    for_chunks(blocks - 2, 2, hide)
+
+    def finish(b):
         mixed = neighbour_block(hidden_ref, b, local[b + 1, 0:taps], second_ref[...])
-        lanes = pl.ds(pl.multiple_of(b * HALO, HALO), HALO)
-        out_ref[:, lanes] = (values[b + 2].astype(F32) + mixed).astype(BF)
-        return carry
-
-    lax.fori_loop(0, blocks - 4, finish, 0)
+        out_ref[:, lanes_at(b, HALO)] = (values[b + 2].astype(F32) + mixed).astype(BF)
+
+    for_chunks(blocks - 4, 2, finish)
 
 
 def ocean_inner(own, index, first, second):
@@ -874,17 +877,14 @@
     capacity = slot_space // devices
     channels, rows, cols = atmos.shape
 
-    def two_rows(first):
-        return jnp.transpose(atmos[:, first : first + 2], (1, 0, 2)).reshape(2 * channels, cols)
+    air = jnp.transpose(atmos, (1, 0, 2))
 
     table, low, high = heat_table(
-        ocean, marine_coupling_slot, coupling_air_cells, two_rows(0), two_rows(rows - 2),
-        capacity, faces, tiles,
+        ocean, marine_coupling_slot, coupling_air_cells, air, capacity, faces, tiles
     )
     above, below = from_neighbours(low, high, "tile")
     heat = heat_slots(table, both)
 
-    air = jnp.transpose(atmos, (1, 0, 2))
     field, first, second, before, live_cells = scatter_own(
         heat, coupling_air_cells, air_conv_first_weight, air_conv_second_weight, rows, cols
     )

time: 89.4 us -> 89.2 us (level)
  waiting for transfers between devices: 15.3 us -> 16.8 us
  Pallas kernels: 37.1 us -> 35.8 us
    transpose x3 -> x0, local copies, waits for them, and re-layouts: 2.76 us -> none  [two_rows(): jnp.transpose(atmos[:, first:first + 2], (1, 0, 2))]
    unnamed x47, local copies, waits for them, and re-layouts: 3.18 us -> 5.87 us
    all_to_all x1, waiting for transfers between devices: 0.2 us -> 2.3 us  [heat_slots(): got = lax.all_to_all(table, both, split_axis=0, concat_axis=0, tiled=True)]
    pallas_call x6, Pallas kernels: 17.4 us -> 15.9 us  [call(): pl.pallas_call(plain, out_shape=outs, in_specs=[VMEM if i in touched else...]
  transfers between devices with their start and end apart: 8 -> 8, of which waited for: 4 -> 4; matrix products, arithmetic and copies ran while one was open for 5% -> 3% of each run, Pallas kernels for 12% -> 11%
where the time goes in v4:
time: 89.2 us; the launch traced here: 88.8 us
  Pallas kernels  35.8 us (40%)
  starting transfers between devices  26.5 us (30%)
  waiting for transfers between devices  16.8 us (19%)
  local copies, waits for them, and re-layouts  8.79 us (10%)
  between operations  0.92 us (1%)
    pallas_call x2, Pallas kernels, call(): pl.pallas_call(kernel, out_shape=outs, in_specs=[ANY] * len(ins), out_spe...  19.8 us
    pallas_call x6, Pallas kernels, call(): pl.pallas_call(plain, out_shape=outs, in_specs=[VMEM if i in touched else...  15.9 us
    all_to_all x1, waiting for transfers between devices, shards(): lax.all_to_all(outgoing, both, split_axis=0, concat_axis=0, tiled=True)  12.8 us
    ppermute x3, starting transfers between devices, from_neighbours(): lax.ppermute(high, axis, [(i, (i + 1) % count) for i in range(ends)])  8.44 us
    all_to_all x1, starting transfers between devices, heat_slots(): got = lax.all_to_all(table, both, split_axis=0, concat_axis=0, tiled=True)  7.1 us
    ppermute x3, starting transfers between devices, from_neighbours(): after = lax.ppermute(low, axis, [((i + 1) % count, i) for i in range(ends)])  6.83 us
    unnamed x47, local copies, waits for them, and re-layouts  5.87 us
    all_to_all x1, starting transfers between devices, shards(): lax.all_to_all(outgoing, both, split_axis=0, concat_axis=0, tiled=True)  4.11 us
  transfers between devices with their start and end apart: 8, of which 4 were waited for; matrix products, arithmetic and copies ran while one was open for 3% of the time, Pallas kernels for 11%

profile of v4, /device:TPU:1, one launch (start us, length us, event | category | flops | bytes accessed | tf_op | source)
XLA Modules:
  0.0 88.8 jit_solution(5786620765060700380)
XLA Ops:
  0.6 3.0 %copy.30 = bf16[64,24,512]{2,0,1:T(8,128)(2,1)} copy(bf16[64,24,512]{2,1,0:T(8,128)(2,1)} %param.11) | data formatting | bytes 3145728 | tf_op args[0]
  3.7 2.3 %shard_map.122 = (bf16[32,16,128]{2,1,0:T(8,128)(2,1)}, bf16[144,512]{1,0:T(8,128)(2,1)}, bf16[144,512]{1,0:T(8,128)(2,1)}) custom-call(bf16[64,2048]{1,0:T(8,128)(2,1)} %refs_2_.5, s32[1,2048]{1,0:T(1,128)} %bitcast.18, s32[1,4096]{1,0:T(1,128)} %refs_1_.2, bf16[24,64,512]{2,1,0:T(8,128)(2,1)} %bitcast.12, bf16[24,64,512]{2,1,0:T(8,128)(2,1)} %bitcast.13, ...), custom_call_target="tpu_custom_call" | custom-call | tf_op jit(solution)/shard_map/pallas_call | solution.py:67
  6.0 7.1 %all-to-all-start = ((bf16[32,16,128]{2,1,0:T(8,128)(2,1)}), bf16[32,16,128]{2,1,0:T(8,128)(2,1)S(1)}, u32[]{:S(2)}, u32[]{:S(2)}) async-start(bf16[32,16,128]{2,1,0:T(8,128)(2,1)} %get-tuple-element.21), calls=%async_computation | async-start | bytes 262144 | tf_op jit(solution)/shard_map/all_to_all | solution.py:199
  13.1 1.3 %collective-permute-start.1 = (bf16[144,512]{1,0:T(8,128)(2,1)}, bf16[144,512]{1,0:T(8,128)(2,1)S(1)}, u32[]{:S(2)}, u32[]{:S(2)}) collective-permute-start(bf16[144,512]{1,0:T(8,128)(2,1)} %get-tuple-element.20.refs_3_), channel_id=1, source_target_pairs={{1,0},{2,1},{3,2},{4,3},{5,4},{6,5},{7,6},{9,8},{10,9},{11,10},{12... | collective-permute-start | bytes 442376 | tf_op jit(solution)/shard_map/ppermute | solution.py:857
  14.4 4.0 %collective-permute-start = (bf16[144,512]{1,0:T(8,128)(2,1)}, bf16[144,512]{1,0:T(8,128)(2,1)S(1)}, u32[]{:S(2)}, u32[]{:S(2)}) collective-permute-start(bf16[144,512]{1,0:T(8,128)(2,1)} %get-tuple-element.19), channel_id=1, source_target_pairs={{0,1},{1,2},{2,3},{3,4},{4,5},{5,6},{6,7},{8,9},{9,10},{10,11},{11... | collective-permute-start | bytes 442376 | tf_op jit(solution)/shard_map/ppermute | solution.py:856
  18.4 2.3 %all-to-all-done.refs_0_.refs_1_.refs_8_ = bf16[32,16,128]{2,1,0:T(8,128)(2,1)S(1)} async-done(((bf16[32,16,128]{2,1,0:T(8,128)(2,1)}), bf16[32,16,128]{2,1,0:T(8,128)(2,1)S(1)}, u32[]{:S(2)}, u32[]{:S(2)}) %all-to-all-start) | async-done | bytes 131104 | tf_op jit(solution)/shard_map/all_to_all | solution.py:199
  20.7 3.0 %shard_map.123 = (f32[24,512]{1,0:T(8,128)S(1)}, bf16[384,256]{1,0:T(8,128)(2,1)S(1)}, bf16[384,256]{1,0:T(8,128)(2,1)S(1)}, s32[32,128]{1,0:T(8,128)S(1)}, s32[16,256]{1,0:T(8,128)S(1)}) custom-call(bf16[32,16,128]{2,1,0:T(8,128)(2,1)S(1)} %all-to-all-done.refs_0_.refs_1_.refs_8_, s32[1,4096]{1,0:T(1,128)S(1)} %copy-done.14, ...), custom_call_target="tpu_custom_call" | custom-call | tf_op jit(solution)/shard_map/pallas_call | solution.py:30
  23.8 0.6 copy-done.18
  24.4 0.4 collective-permute-done.refs_1_.refs_2_
  24.7 1.0 %copy-done.10 = bf16[144,512]{1,0:T(8,128)(2,1)S(1)} copy-done((bf16[144,512]{1,0:T(8,128)(2,1)S(1)}, bf16[144,512]{1,0:T(8,128)(2,1)}, u32[]{:S(2)}) %copy-start.10) | copy-done | bytes 147480
  25.7 0.3 shard_map.124
  26.0 1.5 %collective-permute-start.2 = (bf16[256,128]{1,0:T(8,128)(2,1)S(1)}, bf16[256,128]{1,0:T(8,128)(2,1)S(1)}, u32[]{:S(2)}, u32[]{:S(2)}) collective-permute-start(bf16[256,128]{1,0:T(8,128)(2,1)S(1)} %get-tuple-element.23.refs_6_), channel_id=1, source_target_pairs={{0,8},{8,16},{16,24},{24,0},{1,9},{9,17},{17,25},{25,1},{2,10},{10... | collective-permute-start | bytes 196616 | tf_op jit(solution)/shard_map/ppermute | solution.py:856
  27.6 1.7 %shard_map.125.refs_7_ = f32[32,512]{1,0:T(8,128)S(1)} custom-call(f32[24,512]{1,0:T(8,128)S(1)} %get-tuple-element.22.refs_4_.refs_0_, bf16[32,16,128]{2,1,0:T(8,128)(2,1)S(1)} %all-to-all-done.refs_0_.refs_1_.refs_8_, bf16[144,512]{1,0:T(8,128)(2,1)S(1)} %collective-permute-done.refs_1_.refs_2_, bf16[144,512]{1,0:T(8,128)(2,1)S(1)} %collective-permute-done.1.refs_2_.refs_3_), custom_call_target="tpu_custom_call" | custom-call | tf_op jit(solution)/shard_map/pallas_call | solution.py:30
  29.3 0.6 copy-done.7
  29.9 1.3 %collective-permute-done.3.refs_4_ = bf16[256,128]{1,0:T(8,128)(2,1)S(1)} collective-permute-done((bf16[256,128]{1,0:T(8,128)(2,1)S(1)}, bf16[256,128]{1,0:T(8,128)(2,1)S(1)}, u32[]{:S(2)}, u32[]{:S(2)}) %collective-permute-start.3) | collective-permute-done | bytes 65568 | tf_op jit(solution)/shard_map/ppermute | solution.py:857
  31.3 0.6 copy-done.22
  31.9 17.5 %shard_map.126 = (bf16[24,64,512]{2,1,0:T(8,128)(2,1)}, bf16[32,64,128]{2,1,0:T(8,128)(2,1)}) custom-call(bf16[24,64,512]{2,1,0:T(8,128)(2,1)} %bitcast.14, bf16[144,512]{1,0:T(8,128)(2,1)} %copy-done.4, bf16[144,512]{1,0:T(8,128)(2,1)} %copy-done.3, bf16[256,128]{1,0:T(8,128)(2,1)} %copy-done.21, bf16[256,128]{1,0:T(8,128)(2,1)} %copy-done.22, ...), custom_call_target="tpu_custom_call" | custom-call | tf_op jit(solution)/shard_map/pallas_call | solution.py:67
  49.4 4.1 %all-to-all-start.1 = ((bf16[32,64,128]{2,1,0:T(8,128)(2,1)}), bf16[32,64,128]{2,1,0:T(8,128)(2,1)S(1)}, u32[]{:S(2)}, u32[]{:S(2)}) async-start(bf16[32,64,128]{2,1,0:T(8,128)(2,1)} %get-tuple-element.30), calls=%async_computation.1 | async-start | bytes 1048576 | tf_op jit(solution)/shard_map/all_to_all | solution.py:913
  53.5 0.1 copy.19
  53.7 0.1 copy.21.refs_5_.refs_2_.refs_6_
  53.9 0.1 copy.20
  54.0 0.1 copy.22.refs_6_.refs_3_.refs_7_
  54.2 0.0 copy-start.6
  54.2 0.0 copy-start.17
  54.2 2.3 %copy.29 = bf16[24,64,512]{2,0,1:T(8,128)(2,1)S(1)} copy(bf16[24,64,512]{2,1,0:T(8,128)(2,1)} %get-tuple-element.29) | data formatting | bytes 3145728 | tf_op jit(solution)/shard_map/pallas_call | solution.py:67
  56.5 0.0 copy-start.1
  56.5 12.8 %all-to-all-done.1.refs_0_ = bf16[32,64,128]{2,1,0:T(8,128)(2,1)S(1)} async-done(((bf16[32,64,128]{2,1,0:T(8,128)(2,1)}), bf16[32,64,128]{2,1,0:T(8,128)(2,1)S(1)}, u32[]{:S(2)}, u32[]{:S(2)}) %all-to-all-start.1) | async-done | bytes 524320 | tf_op jit(solution)/shard_map/all_to_all | solution.py:913
  69.3 1.9 %shard_map.127 = (bf16[64,2048]{1,0:T(8,128)(2,1)S(1)}, bf16[80,512]{1,0:T(8,128)(2,1)S(1)}, bf16[80,512]{1,0:T(8,128)(2,1)S(1)}) custom-call(bf16[32,64,128]{2,1,0:T(8,128)(2,1)S(1)} %all-to-all-done.1.refs_0_, s32[1,2048]{1,0:T(1,128)S(1)} %bitcast.19, bf16[64,2048]{1,0:T(8,128)(2,1)S(1)} %copy-done.6, s32[9,2048]{1,0:T(8,128)S(1)} %copy-done.5, ...), custom_call_target="tpu_custom_call" | custom-call | tf_op jit(solution)/shard_map/pallas_call | solution.py:30
  71.2 2.9 %collective-permute-start.4 = (bf16[80,512]{1,0:T(8,128)(2,1)S(1)}, bf16[80,512]{1,0:T(8,128)(2,1)S(1)}, u32[]{:S(2)}, u32[]{:S(2)}) collective-permute-start(bf16[80,512]{1,0:T(8,128)(2,1)S(1)} %get-tuple-element.34), channel_id=1, source_target_pairs={{0,1},{1,2},{2,3},{3,4},{4,5},{5,6},{6,7},{7,8},{8,9},{9,10},{10,1... | collective-permute-start | bytes 245768 | tf_op jit(solution)/shard_map/ppermute | solution.py:856
  74.2 5.5 %collective-permute-start.5 = (bf16[80,512]{1,0:T(8,128)(2,1)S(1)}, bf16[80,512]{1,0:T(8,128)(2,1)S(1)}, u32[]{:S(2)}, u32[]{:S(2)}) collective-permute-start(bf16[80,512]{1,0:T(8,128)(2,1)S(1)} %get-tuple-element.35), channel_id=1, source_target_pairs={{1,0},{2,1},{3,2},{4,3},{5,4},{6,5},{7,6},{8,7},{9,8},{10,9},{11,1... | collective-permute-start | bytes 245768 | tf_op jit(solution)/shard_map/ppermute | solution.py:857
  79.7 5.0 %shard_map.128 = (bf16[6,64,256]{2,1,0:T(8,128)(2,1)S(1)}, bf16[64,1024]{1,0:T(8,128)(2,1)S(1)}) custom-call(bf16[64,2048]{1,0:T(8,128)(2,1)S(1)} %get-tuple-element.31.refs_0_, s32[9,2048]{1,0:T(8,128)S(1)} %copy-done.5, bf16[64,576]{1,0:T(8,128)(2,1)S(1)} %copy.21.refs_5_.refs_2_.refs_6_, bf16[64,576]{1,0:T(8,128)(2,1)S(1)} %copy.22.refs_6_.refs_3_.refs_7_), custom_call_target="tpu_custom_call" | custom-call | tf_op jit(solution)/shard_map/pallas_call | solution.py:30
  84.8 4.0 %shard_map.129 = bf16[64,2048]{1,0:T(8,128)(2,1)} custom-call(bf16[64,2048]{1,0:T(8,128)(2,1)S(1)} %get-tuple-element.31.refs_0_, bf16[6,64,256]{2,1,0:T(8,128)(2,1)S(1)} %get-tuple-element.32.refs_1_, bf16[64,1024]{1,0:T(8,128)(2,1)S(1)} %get-tuple-element.33.refs_2_, bf16[80,512]{1,0:T(8,128)(2,1)S(1)} %collective-permute-done.4.refs_3_, ...), custom_call_target="tpu_custom_call" | custom-call | tf_op jit(solution)/shard_map/pallas_call | solution.py:30
  (44 shorter events, 0.1 us)
Async XLA Ops:
  3.7 17.1 %copy-start.11 = (bf16[3,3,64,64]{3,2,1,0:T(8,128)(2,1)S(1)}, bf16[3,3,64,64]{3,2,1,0:T(8,128)(2,1)}, u32[]{:S(2)}) copy-start(bf16[3,3,64,64]{3,2,1,0:T(8,128)(2,1)} %refs_2_.4) | copy-start | bytes 221188
  3.7 17.1 %copy-start.12 = (bf16[3,3,64,64]{3,2,1,0:T(8,128)(2,1)S(1)}, bf16[3,3,64,64]{3,2,1,0:T(8,128)(2,1)}, u32[]{:S(2)}) copy-start(bf16[3,3,64,64]{3,2,1,0:T(8,128)(2,1)} %refs_3_.2) | copy-start | bytes 221188
  3.7 17.1 %copy-start.14 = (s32[1,4096]{1,0:T(1,128)S(1)}, s32[1,4096]{1,0:T(1,128)}, u32[]{:S(2)}) copy-start(s32[1,4096]{1,0:T(1,128)} %refs_1_.2) | copy-start | bytes 49156
  3.7 21.1 %copy-start = (bf16[64,24,512]{2,0,1:T(8,128)(2,1)S(1)}, bf16[64,24,512]{2,0,1:T(8,128)(2,1)}, u32[]{:S(2)}) copy-start(bf16[64,24,512]{2,0,1:T(8,128)(2,1)} %copy.30) | copy-start | bytes 4718596
  6.0 14.7 %all-to-all-start = ((bf16[32,16,128]{2,1,0:T(8,128)(2,1)}), bf16[32,16,128]{2,1,0:T(8,128)(2,1)S(1)}, u32[]{:S(2)}, u32[]{:S(2)}) async-start(bf16[32,16,128]{2,1,0:T(8,128)(2,1)} %get-tuple-element.21), calls=%async_computation | async-start | bytes 262144 | tf_op jit(solution)/shard_map/all_to_all | solution.py:199
  13.1 11.2 %collective-permute-start.1 = (bf16[144,512]{1,0:T(8,128)(2,1)}, bf16[144,512]{1,0:T(8,128)(2,1)S(1)}, u32[]{:S(2)}, u32[]{:S(2)}) collective-permute-start(bf16[144,512]{1,0:T(8,128)(2,1)} %get-tuple-element.20.refs_3_), channel_id=1, source_target_pairs={{1,0},{2,1},{3,2},{4,3},{5,4},{6,5},{7,6},{9,8},{10,9},{11,10},{12... | collective-permute-start | bytes 442376 | tf_op jit(solution)/shard_map/ppermute | solution.py:857
  14.4 10.3 %collective-permute-start = (bf16[144,512]{1,0:T(8,128)(2,1)}, bf16[144,512]{1,0:T(8,128)(2,1)S(1)}, u32[]{:S(2)}, u32[]{:S(2)}) collective-permute-start(bf16[144,512]{1,0:T(8,128)(2,1)} %get-tuple-element.19), channel_id=1, source_target_pairs={{0,1},{1,2},{2,3},{3,4},{4,5},{5,6},{6,7},{8,9},{9,10},{10,11},{11... | collective-permute-start | bytes 442376 | tf_op jit(solution)/shard_map/ppermute | solution.py:856
  20.7 10.5 %copy-start.2 = (bf16[32,16,128]{2,1,0:T(8,128)(2,1)}, bf16[32,16,128]{2,1,0:T(8,128)(2,1)S(1)}, u32[]{:S(2)}) copy-start(bf16[32,16,128]{2,1,0:T(8,128)(2,1)S(1)} %all-to-all-done.refs_0_.refs_1_.refs_8_) | copy-start | bytes 393220
  23.8 0.6 copy-start.18
  24.4 4.9 %copy-start.8 = (bf16[384,256]{1,0:T(8,128)(2,1)}, bf16[384,256]{1,0:T(8,128)(2,1)S(1)}, u32[]{:S(2)}) copy-start(bf16[384,256]{1,0:T(8,128)(2,1)S(1)} %get-tuple-element.27.refs_13_) | copy-start | bytes 589828
  24.4 5.6 %copy-start.9 = (bf16[384,256]{1,0:T(8,128)(2,1)}, bf16[384,256]{1,0:T(8,128)(2,1)S(1)}, u32[]{:S(2)}) copy-start(bf16[384,256]{1,0:T(8,128)(2,1)S(1)} %get-tuple-element.28.refs_14_) | copy-start | bytes 589828
  24.4 6.9 %copy-start.13 = (s32[32,128]{1,0:T(8,128)}, s32[32,128]{1,0:T(8,128)S(1)}, u32[]{:S(2)}) copy-start(s32[32,128]{1,0:T(8,128)S(1)} %get-tuple-element.25.refs_9_.refs_10_) | copy-start | bytes 49156
  24.4 6.9 %copy-start.3 = (bf16[144,512]{1,0:T(8,128)(2,1)}, bf16[144,512]{1,0:T(8,128)(2,1)S(1)}, u32[]{:S(2)}) copy-start(bf16[144,512]{1,0:T(8,128)(2,1)S(1)} %collective-permute-done.1.refs_2_.refs_3_) | copy-start | bytes 442372
  24.7 6.5 %copy-start.4 = (bf16[144,512]{1,0:T(8,128)(2,1)}, bf16[144,512]{1,0:T(8,128)(2,1)S(1)}, u32[]{:S(2)}) copy-start(bf16[144,512]{1,0:T(8,128)(2,1)S(1)} %collective-permute-done.refs_1_.refs_2_) | copy-start | bytes 442372
  24.7 1.0 %copy-start.10 = (bf16[144,512]{1,0:T(8,128)(2,1)S(1)}, bf16[144,512]{1,0:T(8,128)(2,1)}, u32[]{:S(2)}) copy-start(bf16[144,512]{1,0:T(8,128)(2,1)} %get-tuple-element.20.refs_3_) | copy-start | bytes 442372
  26.0 5.3 %copy-start.15 = (bf16[256,128]{1,0:T(8,128)(2,1)}, bf16[256,128]{1,0:T(8,128)(2,1)S(1)}, u32[]{:S(2)}) copy-start(bf16[256,128]{1,0:T(8,128)(2,1)S(1)} %get-tuple-element.24.refs_5_) | copy-start | bytes 196612
  26.0 5.3 %copy-start.16 = (bf16[256,128]{1,0:T(8,128)(2,1)}, bf16[256,128]{1,0:T(8,128)(2,1)S(1)}, u32[]{:S(2)}) copy-start(bf16[256,128]{1,0:T(8,128)(2,1)S(1)} %get-tuple-element.23.refs_6_) | copy-start | bytes 196612
  26.0 3.9 %collective-permute-start.2 = (bf16[256,128]{1,0:T(8,128)(2,1)S(1)}, bf16[256,128]{1,0:T(8,128)(2,1)S(1)}, u32[]{:S(2)}, u32[]{:S(2)}) collective-permute-start(bf16[256,128]{1,0:T(8,128)(2,1)S(1)} %get-tuple-element.23.refs_6_), channel_id=1, source_target_pairs={{0,8},{8,16},{16,24},{24,0},{1,9},{9,17},{17,25},{25,1},{2,10},{10... | collective-permute-start | bytes 196616 | tf_op jit(solution)/shard_map/ppermute | solution.py:856
  27.6 3.7 %collective-permute-start.3 = (bf16[256,128]{1,0:T(8,128)(2,1)S(1)}, bf16[256,128]{1,0:T(8,128)(2,1)S(1)}, u32[]{:S(2)}, u32[]{:S(2)}) collective-permute-start(bf16[256,128]{1,0:T(8,128)(2,1)S(1)} %get-tuple-element.24.refs_5_), channel_id=1, source_target_pairs={{8,0},{16,8},{24,16},{0,24},{9,1},{17,9},{25,17},{1,25},{10,2},{18... | collective-permute-start | bytes 196616 | tf_op jit(solution)/shard_map/ppermute | solution.py:857
  29.3 0.6 copy-start.7
  29.9 1.4 %copy-start.21 = (bf16[256,128]{1,0:T(8,128)(2,1)}, bf16[256,128]{1,0:T(8,128)(2,1)S(1)}, u32[]{:S(2)}) copy-start(bf16[256,128]{1,0:T(8,128)(2,1)S(1)} %collective-permute-done.2.refs_3_) | copy-start | bytes 196612
  31.3 0.6 copy-start.22
  31.9 21.6 %copy-start.19 = (bf16[9,64,64]{2,1,0:T(8,128)(2,1)S(1)}, bf16[9,64,64]{2,1,0:T(8,128)(2,1)}, u32[]{:S(2)}) copy-start(bf16[9,64,64]{2,1,0:T(8,128)(2,1)} %param.16) | copy-start | bytes 221188
  31.9 22.0 %copy-start.20 = (bf16[9,64,64]{2,1,0:T(8,128)(2,1)S(1)}, bf16[9,64,64]{2,1,0:T(8,128)(2,1)}, u32[]{:S(2)}) copy-start(bf16[9,64,64]{2,1,0:T(8,128)(2,1)} %param.17) | copy-start | bytes 221188
  49.4 19.9 %all-to-all-start.1 = ((bf16[32,64,128]{2,1,0:T(8,128)(2,1)}), bf16[32,64,128]{2,1,0:T(8,128)(2,1)S(1)}, u32[]{:S(2)}, u32[]{:S(2)}) async-start(bf16[32,64,128]{2,1,0:T(8,128)(2,1)} %get-tuple-element.30), calls=%async_computation.1 | async-start | bytes 1048576 | tf_op jit(solution)/shard_map/all_to_all | solution.py:913
  54.2 15.2 %copy-start.5 = (s32[9,2048]{1,0:T(8,128)S(1)}, s32[9,2048]{1,0:T(8,128)}, u32[]{:S(2)}) copy-start(s32[9,2048]{1,0:T(8,128)} %refs_5_.2) | copy-start | bytes 221188
  54.2 15.2 %copy-start.6 = (bf16[64,2048]{1,0:T(8,128)(2,1)S(1)}, bf16[64,2048]{1,0:T(8,128)(2,1)}, u32[]{:S(2)}) copy-start(bf16[64,2048]{1,0:T(8,128)(2,1)} %refs_2_.5) | copy-start | bytes 786436
  54.2 15.2 %copy-start.17 = (s32[2048]{0:T(1024)S(1)}, s32[2048]{0:T(1024)}, u32[]{:S(2)}) copy-start(s32[2048]{0:T(1024)} %param.18) | copy-start | bytes 24580
  56.5 28.2 %copy-start.1 = (bf16[24,64,512]{2,0,1:T(8,128)(2,1)}, bf16[24,64,512]{2,0,1:T(8,128)(2,1)S(1)}, u32[]{:S(2)}) copy-start(bf16[24,64,512]{2,0,1:T(8,128)(2,1)S(1)} %copy.29) | copy-start | bytes 4718596
  71.2 13.5 %collective-permute-start.4 = (bf16[80,512]{1,0:T(8,128)(2,1)S(1)}, bf16[80,512]{1,0:T(8,128)(2,1)S(1)}, u32[]{:S(2)}, u32[]{:S(2)}) collective-permute-start(bf16[80,512]{1,0:T(8,128)(2,1)S(1)} %get-tuple-element.34), channel_id=1, source_target_pairs={{0,1},{1,2},{2,3},{3,4},{4,5},{5,6},{6,7},{7,8},{8,9},{9,10},{10,1... | collective-permute-start | bytes 245768 | tf_op jit(solution)/shard_map/ppermute | solution.py:856
  74.2 10.6 %collective-permute-start.5 = (bf16[80,512]{1,0:T(8,128)(2,1)S(1)}, bf16[80,512]{1,0:T(8,128)(2,1)S(1)}, u32[]{:S(2)}, u32[]{:S(2)}) collective-permute-start(bf16[80,512]{1,0:T(8,128)(2,1)S(1)} %get-tuple-element.35), channel_id=1, source_target_pairs={{1,0},{2,1},{3,2},{4,3},{5,4},{6,5},{7,6},{8,7},{9,8},{10,9},{11,1... | collective-permute-start | bytes 245768 | tf_op jit(solution)/shard_map/ppermute | solution.py:857

commit v5 on v3

--- a/solution.py
+++ b/solution.py
@@ -683,8 +683,8 @@
     shift = depth.bit_length() - 1
     width = 256
 
-    def block(b, carry):
-        lanes = pl.ds(pl.multiple_of(b * width, width), width)
+    def block(b):
+        lanes = lanes_at(b, width)
         slot = slot_ref[:, lanes]
         low = one_hot(slot & (depth - 1), depth)
         high = slot >> shift
@@ -695,10 +695,9 @@
         for g in range(1, groups):
             total = jnp.where(high == g, got[g * channels : (g + 1) * channels], total)
         out_ref[:, lanes] = (ocean_ref[:, lanes].astype(F32) + total).astype(BF)
-        return carry
 
     channels, cells = ocean_ref.shape
-    lax.fori_loop(0, cells // width, block, 0)
+    for_chunks(cells // width, 2, block)
     reach = 2 * HALO
     for ref, first, start in ((head_ref, 0, 0), (tail_ref, cells - reach, cells - HALO)):
         ref[0:channels] = out_ref[:, first : first + reach]
@@ -760,19 +759,16 @@
     for b in range(blocks - 2):
         local[b, 0:taps] = own_positions(index_ref, b + 1)
 
-    def hide(b, carry):
+    def hide(b):
         hide_block(hidden_ref, b, values, b, local[b, 0:taps], first_ref)
-        return carry
-
-    lax.fori_loop(0, blocks - 2, hide, 0)
-
-    def finish(b, carry):
+
+    for_chunks(blocks - 2, 2, hide)
+
+    def finish(b):
         mixed = neighbour_block(hidden_ref, b, local[b + 1, 0:taps], second_ref[...])
-        lanes = pl.ds(pl.multiple_of(b * HALO, HALO), HALO)
-        out_ref[:, lanes] = (values[b + 2].astype(F32) + mixed).astype(BF)
-        return carry
-
-    lax.fori_loop(0, blocks - 4, finish, 0)
+        out_ref[:, lanes_at(b, HALO)] = (values[b + 2].astype(F32) + mixed).astype(BF)
+
+    for_chunks(blocks - 4, 2, finish)
 
 
 def ocean_inner(own, index, first, second):

time: 89.4 us -> 88 us (0.984)
  Pallas kernels: 37.1 us -> 35.6 us
    pallas_call x6, Pallas kernels: 17.4 us -> 15.9 us  [call(): pl.pallas_call(plain, out_shape=outs, in_specs=[VMEM if i in touched else...]
  transfers between devices with their start and end apart: 8 -> 8, of which waited for: 4 -> 4; matrix products, arithmetic and copies ran while one was open for 5% -> 6% of each run, Pallas kernels for 12% -> 11%
where the time goes in v5:
time: 88 us; the launch traced here: 87.5 us
  Pallas kernels  35.6 us (40%)
  starting transfers between devices  26.8 us (30%)
  waiting for transfers between devices  15.3 us (17%)
  local copies, waits for them, and re-layouts  8.85 us (10%)
  between operations  1 us (1%)
    pallas_call x2, Pallas kernels, call(): pl.pallas_call(kernel, out_shape=outs, in_specs=[ANY] * len(ins), out_spe...  19.7 us
    pallas_call x6, Pallas kernels, call(): pl.pallas_call(plain, out_shape=outs, in_specs=[VMEM if i in touched else...  15.9 us
    all_to_all x1, waiting for transfers between devices, shards(): lax.all_to_all(outgoing, both, split_axis=0, concat_axis=0, tiled=True)  12.8 us
    ppermute x3, starting transfers between devices, from_neighbours(): lax.ppermute(high, axis, [(i, (i + 1) % count) for i in range(ends)])  8.56 us
    all_to_all x1, starting transfers between devices, heat_slots(): got = lax.all_to_all(table, both, split_axis=0, concat_axis=0, tiled=True)  7.1 us
    ppermute x3, starting transfers between devices, from_neighbours(): after = lax.ppermute(low, axis, [((i + 1) % count, i) for i in range(ends)])  6.84 us
    all_to_all x1, starting transfers between devices, shards(): lax.all_to_all(outgoing, both, split_axis=0, concat_axis=0, tiled=True)  4.25 us
    unnamed x47, local copies, waits for them, and re-layouts  3.18 us
  transfers between devices with their start and end apart: 8, of which 4 were waited for; matrix products, arithmetic and copies ran while one was open for 6% of the time, Pallas kernels for 11%

profile of v5, /device:TPU:1, one launch (start us, length us, event | category | flops | bytes accessed | tf_op | source)
XLA Modules:
  0.0 87.5 jit_solution(9377035189855200728)
XLA Ops:
  0.6 1.4 %slice_bitcast_fusion = (bf16[2,64,512]{2,0,1:T(2,128)(2,1)S(1)}, bf16[2,64,512]{2,0,1:T(2,128)(2,1)S(1)}) fusion(bf16[64,24,512]{2,1,0:T(8,128)(2,1)} %param.11), kind=kLoop, calls=%fused_computation.2 | loop fusion | bytes 524288 | tf_op jit(solution)/shard_map/transpose | solution.py:874
  2.0 0.7 copy.20
  2.7 0.7 copy.21
  3.4 2.2 %shard_map.122 = (bf16[32,16,128]{2,1,0:T(8,128)(2,1)}, bf16[144,512]{1,0:T(8,128)(2,1)}, bf16[144,512]{1,0:T(8,128)(2,1)}) custom-call(bf16[64,2048]{1,0:T(8,128)(2,1)} %refs_2_.5, s32[1,2048]{1,0:T(1,128)} %bitcast.22, s32[1,4096]{1,0:T(1,128)} %refs_1_.2, bf16[128,512]{1,0:T(8,128)(2,1)} %bitcast.26, bf16[128,512]{1,0:T(8,128)(2,1)} %bitcast.27, ...), custom_call_target="tpu_custom_call" | custom-call | tf_op jit(solution)/shard_map/pallas_call | solution.py:67
  5.6 7.1 %all-to-all-start = ((bf16[32,16,128]{2,1,0:T(8,128)(2,1)}), bf16[32,16,128]{2,1,0:T(8,128)(2,1)S(1)}, u32[]{:S(2)}, u32[]{:S(2)}) async-start(bf16[32,16,128]{2,1,0:T(8,128)(2,1)} %get-tuple-element.21), calls=%async_computation | async-start | bytes 262144 | tf_op jit(solution)/shard_map/all_to_all | solution.py:192
  12.7 1.3 %collective-permute-start.1 = (bf16[144,512]{1,0:T(8,128)(2,1)}, bf16[144,512]{1,0:T(8,128)(2,1)S(1)}, u32[]{:S(2)}, u32[]{:S(2)}) collective-permute-start(bf16[144,512]{1,0:T(8,128)(2,1)} %get-tuple-element.20.refs_3_), channel_id=1, source_target_pairs={{1,0},{2,1},{3,2},{4,3},{5,4},{6,5},{7,6},{9,8},{10,9},{11,10},{12... | collective-permute-start | bytes 442376 | tf_op jit(solution)/shard_map/ppermute | solution.py:850
  14.0 0.0 copy-start.14
  14.0 4.1 %collective-permute-start = (bf16[144,512]{1,0:T(8,128)(2,1)}, bf16[144,512]{1,0:T(8,128)(2,1)S(1)}, u32[]{:S(2)}, u32[]{:S(2)}) collective-permute-start(bf16[144,512]{1,0:T(8,128)(2,1)} %get-tuple-element.19), channel_id=1, source_target_pairs={{0,1},{1,2},{2,3},{3,4},{4,5},{5,6},{6,7},{8,9},{9,10},{10,11},{11... | collective-permute-start | bytes 442376 | tf_op jit(solution)/shard_map/ppermute | solution.py:849
  18.2 1.9 %copy.34 = bf16[64,24,512]{2,0,1:T(8,128)(2,1)S(1)} copy(bf16[64,24,512]{2,1,0:T(8,128)(2,1)} %param.11) | data formatting | bytes 3145728 | tf_op args[0]
  20.1 0.2 all-to-all-done.refs_0_.refs_1_.refs_8_
  20.3 3.0 %shard_map.123 = (f32[24,512]{1,0:T(8,128)S(1)}, bf16[384,256]{1,0:T(8,128)(2,1)S(1)}, bf16[384,256]{1,0:T(8,128)(2,1)S(1)}, s32[32,128]{1,0:T(8,128)S(1)}, s32[16,256]{1,0:T(8,128)S(1)}) custom-call(bf16[32,16,128]{2,1,0:T(8,128)(2,1)S(1)} %all-to-all-done.refs_0_.refs_1_.refs_8_, s32[1,4096]{1,0:T(1,128)S(1)} %copy-done.14, ...), custom_call_target="tpu_custom_call" | custom-call | tf_op jit(solution)/shard_map/pallas_call | solution.py:30
  23.3 0.0 copy-start.8
  23.4 0.9 %collective-permute-done.refs_1_.refs_2_ = bf16[144,512]{1,0:T(8,128)(2,1)S(1)} collective-permute-done((bf16[144,512]{1,0:T(8,128)(2,1)}, bf16[144,512]{1,0:T(8,128)(2,1)S(1)}, u32[]{:S(2)}, u32[]{:S(2)}) %collective-permute-start) | collective-permute-done | bytes 147488 | tf_op jit(solution)/shard_map/ppermute | solution.py:849
  24.3 0.3 shard_map.124
  24.6 1.5 %collective-permute-start.2 = (bf16[256,128]{1,0:T(8,128)(2,1)S(1)}, bf16[256,128]{1,0:T(8,128)(2,1)S(1)}, u32[]{:S(2)}, u32[]{:S(2)}) collective-permute-start(bf16[256,128]{1,0:T(8,128)(2,1)S(1)} %get-tuple-element.23.refs_6_), channel_id=1, source_target_pairs={{0,8},{8,16},{16,24},{24,0},{1,9},{9,17},{17,25},{25,1},{2,10},{10... | collective-permute-start | bytes 196616 | tf_op jit(solution)/shard_map/ppermute | solution.py:849
  26.2 1.7 %shard_map.125.refs_7_ = f32[32,512]{1,0:T(8,128)S(1)} custom-call(f32[24,512]{1,0:T(8,128)S(1)} %get-tuple-element.22.refs_4_.refs_0_, bf16[32,16,128]{2,1,0:T(8,128)(2,1)S(1)} %all-to-all-done.refs_0_.refs_1_.refs_8_, bf16[144,512]{1,0:T(8,128)(2,1)S(1)} %collective-permute-done.refs_1_.refs_2_, bf16[144,512]{1,0:T(8,128)(2,1)S(1)} %collective-permute-done.1.refs_2_.refs_3_), custom_call_target="tpu_custom_call" | custom-call | tf_op jit(solution)/shard_map/pallas_call | solution.py:30
  27.9 0.6 copy-done.7
  28.5 1.4 %collective-permute-done.3.refs_4_ = bf16[256,128]{1,0:T(8,128)(2,1)S(1)} collective-permute-done((bf16[256,128]{1,0:T(8,128)(2,1)S(1)}, bf16[256,128]{1,0:T(8,128)(2,1)S(1)}, u32[]{:S(2)}, u32[]{:S(2)}) %collective-permute-start.3) | collective-permute-done | bytes 65568 | tf_op jit(solution)/shard_map/ppermute | solution.py:850
  29.9 0.6 copy-done.22
  30.5 17.5 %shard_map.126 = (bf16[24,64,512]{2,1,0:T(8,128)(2,1)}, bf16[32,64,128]{2,1,0:T(8,128)(2,1)}) custom-call(bf16[24,64,512]{2,1,0:T(8,128)(2,1)} %bitcast.19, bf16[144,512]{1,0:T(8,128)(2,1)} %copy-done.4, bf16[144,512]{1,0:T(8,128)(2,1)} %copy-done.3, bf16[256,128]{1,0:T(8,128)(2,1)} %copy-done.21, bf16[256,128]{1,0:T(8,128)(2,1)} %copy-done.22, ...), custom_call_target="tpu_custom_call" | custom-call | tf_op jit(solution)/shard_map/pallas_call | solution.py:67
  48.0 4.3 %all-to-all-start.1 = ((bf16[32,64,128]{2,1,0:T(8,128)(2,1)}), bf16[32,64,128]{2,1,0:T(8,128)(2,1)S(1)}, u32[]{:S(2)}, u32[]{:S(2)}) async-start(bf16[32,64,128]{2,1,0:T(8,128)(2,1)} %get-tuple-element.30), calls=%async_computation.1 | async-start | bytes 1048576 | tf_op jit(solution)/shard_map/all_to_all | solution.py:909
  52.3 0.1 copy.23
  52.4 0.1 copy.25.refs_5_.refs_2_.refs_6_
  52.6 0.1 copy.24
  52.7 0.1 copy.26.refs_6_.refs_3_.refs_7_
  52.9 2.3 %copy.33 = bf16[24,64,512]{2,0,1:T(8,128)(2,1)S(1)} copy(bf16[24,64,512]{2,1,0:T(8,128)(2,1)} %get-tuple-element.29) | data formatting | bytes 3145728 | tf_op jit(solution)/shard_map/pallas_call | solution.py:67
  55.3 12.8 %all-to-all-done.1.refs_0_ = bf16[32,64,128]{2,1,0:T(8,128)(2,1)S(1)} async-done(((bf16[32,64,128]{2,1,0:T(8,128)(2,1)}), bf16[32,64,128]{2,1,0:T(8,128)(2,1)S(1)}, u32[]{:S(2)}, u32[]{:S(2)}) %all-to-all-start.1) | async-done | bytes 524320 | tf_op jit(solution)/shard_map/all_to_all | solution.py:909
  68.1 1.9 %shard_map.127 = (bf16[64,2048]{1,0:T(8,128)(2,1)S(1)}, bf16[80,512]{1,0:T(8,128)(2,1)S(1)}, bf16[80,512]{1,0:T(8,128)(2,1)S(1)}) custom-call(bf16[32,64,128]{2,1,0:T(8,128)(2,1)S(1)} %all-to-all-done.1.refs_0_, s32[1,2048]{1,0:T(1,128)S(1)} %bitcast.23, bf16[64,2048]{1,0:T(8,128)(2,1)S(1)} %copy-done.6, s32[9,2048]{1,0:T(8,128)S(1)} %copy-done.5, ...), custom_call_target="tpu_custom_call" | custom-call | tf_op jit(solution)/shard_map/pallas_call | solution.py:30
  70.0 2.9 %collective-permute-start.4 = (bf16[80,512]{1,0:T(8,128)(2,1)S(1)}, bf16[80,512]{1,0:T(8,128)(2,1)S(1)}, u32[]{:S(2)}, u32[]{:S(2)}) collective-permute-start(bf16[80,512]{1,0:T(8,128)(2,1)S(1)} %get-tuple-element.34), channel_id=1, source_target_pairs={{0,1},{1,2},{2,3},{3,4},{4,5},{5,6},{6,7},{7,8},{8,9},{9,10},{10,1... | collective-permute-start | bytes 245768 | tf_op jit(solution)/shard_map/ppermute | solution.py:849
  72.9 5.5 %collective-permute-start.5 = (bf16[80,512]{1,0:T(8,128)(2,1)S(1)}, bf16[80,512]{1,0:T(8,128)(2,1)S(1)}, u32[]{:S(2)}, u32[]{:S(2)}) collective-permute-start(bf16[80,512]{1,0:T(8,128)(2,1)S(1)} %get-tuple-element.35), channel_id=1, source_target_pairs={{1,0},{2,1},{3,2},{4,3},{5,4},{6,5},{7,6},{8,7},{9,8},{10,9},{11,1... | collective-permute-start | bytes 245768 | tf_op jit(solution)/shard_map/ppermute | solution.py:850
  78.4 5.0 %shard_map.128 = (bf16[6,64,256]{2,1,0:T(8,128)(2,1)S(1)}, bf16[64,1024]{1,0:T(8,128)(2,1)S(1)}) custom-call(bf16[64,2048]{1,0:T(8,128)(2,1)S(1)} %get-tuple-element.31.refs_0_, s32[9,2048]{1,0:T(8,128)S(1)} %copy-done.5, bf16[64,576]{1,0:T(8,128)(2,1)S(1)} %copy.25.refs_5_.refs_2_.refs_6_, bf16[64,576]{1,0:T(8,128)(2,1)S(1)} %copy.26.refs_6_.refs_3_.refs_7_), custom_call_target="tpu_custom_call" | custom-call | tf_op jit(solution)/shard_map/pallas_call | solution.py:30
  83.5 4.0 %shard_map.129 = bf16[64,2048]{1,0:T(8,128)(2,1)} custom-call(bf16[64,2048]{1,0:T(8,128)(2,1)S(1)} %get-tuple-element.31.refs_0_, bf16[6,64,256]{2,1,0:T(8,128)(2,1)S(1)} %get-tuple-element.32.refs_1_, bf16[64,1024]{1,0:T(8,128)(2,1)S(1)} %get-tuple-element.33.refs_2_, bf16[80,512]{1,0:T(8,128)(2,1)S(1)} %collective-permute-done.4.refs_3_, ...), custom_call_target="tpu_custom_call" | custom-call | tf_op jit(solution)/shard_map/pallas_call | solution.py:30
  (47 shorter events, 0.1 us)
Async XLA Ops:
  5.6 14.7 %all-to-all-start = ((bf16[32,16,128]{2,1,0:T(8,128)(2,1)}), bf16[32,16,128]{2,1,0:T(8,128)(2,1)S(1)}, u32[]{:S(2)}, u32[]{:S(2)}) async-start(bf16[32,16,128]{2,1,0:T(8,128)(2,1)} %get-tuple-element.21), calls=%async_computation | async-start | bytes 262144 | tf_op jit(solution)/shard_map/all_to_all | solution.py:192
  12.7 10.7 %collective-permute-start.1 = (bf16[144,512]{1,0:T(8,128)(2,1)}, bf16[144,512]{1,0:T(8,128)(2,1)S(1)}, u32[]{:S(2)}, u32[]{:S(2)}) collective-permute-start(bf16[144,512]{1,0:T(8,128)(2,1)} %get-tuple-element.20.refs_3_), channel_id=1, source_target_pairs={{1,0},{2,1},{3,2},{4,3},{5,4},{6,5},{7,6},{9,8},{10,9},{11,10},{12... | collective-permute-start | bytes 442376 | tf_op jit(solution)/shard_map/ppermute | solution.py:850
  14.0 6.3 %copy-start.11 = (bf16[3,3,64,64]{3,2,1,0:T(8,128)(2,1)S(1)}, bf16[3,3,64,64]{3,2,1,0:T(8,128)(2,1)}, u32[]{:S(2)}) copy-start(bf16[3,3,64,64]{3,2,1,0:T(8,128)(2,1)} %refs_2_.4) | copy-start | bytes 221188
  14.0 6.3 %copy-start.12 = (bf16[3,3,64,64]{3,2,1,0:T(8,128)(2,1)S(1)}, bf16[3,3,64,64]{3,2,1,0:T(8,128)(2,1)}, u32[]{:S(2)}) copy-start(bf16[3,3,64,64]{3,2,1,0:T(8,128)(2,1)} %refs_3_.2) | copy-start | bytes 221188
  14.0 6.3 %copy-start.14 = (s32[1,4096]{1,0:T(1,128)S(1)}, s32[1,4096]{1,0:T(1,128)}, u32[]{:S(2)}) copy-start(s32[1,4096]{1,0:T(1,128)} %refs_1_.2) | copy-start | bytes 49156
  14.0 10.3 %copy-start.10 = (bf16[144,512]{1,0:T(8,128)(2,1)S(1)}, bf16[144,512]{1,0:T(8,128)(2,1)}, u32[]{:S(2)}) copy-start(bf16[144,512]{1,0:T(8,128)(2,1)} %get-tuple-element.20.refs_3_) | copy-start | bytes 442372
  14.0 10.3 %collective-permute-start = (bf16[144,512]{1,0:T(8,128)(2,1)}, bf16[144,512]{1,0:T(8,128)(2,1)S(1)}, u32[]{:S(2)}, u32[]{:S(2)}) collective-permute-start(bf16[144,512]{1,0:T(8,128)(2,1)} %get-tuple-element.19), channel_id=1, source_target_pairs={{0,1},{1,2},{2,3},{3,4},{4,5},{5,6},{6,7},{8,9},{9,10},{10,11},{11... | collective-permute-start | bytes 442376 | tf_op jit(solution)/shard_map/ppermute | solution.py:849
  20.1 9.8 %copy-start = (bf16[64,24,512]{2,0,1:T(8,128)(2,1)}, bf16[64,24,512]{2,0,1:T(8,128)(2,1)S(1)}, u32[]{:S(2)}) copy-start(bf16[64,24,512]{2,0,1:T(8,128)(2,1)S(1)} %copy.34) | copy-start | bytes 4718596
  20.3 9.6 %copy-start.2 = (bf16[32,16,128]{2,1,0:T(8,128)(2,1)}, bf16[32,16,128]{2,1,0:T(8,128)(2,1)S(1)}, u32[]{:S(2)}) copy-start(bf16[32,16,128]{2,1,0:T(8,128)(2,1)S(1)} %all-to-all-done.refs_0_.refs_1_.refs_8_) | copy-start | bytes 393220
  23.3 2.9 %copy-start.18 = (s32[16,256]{1,0:T(8,128)}, s32[16,256]{1,0:T(8,128)S(1)}, u32[]{:S(2)}) copy-start(s32[16,256]{1,0:T(8,128)S(1)} %get-tuple-element.26.refs_11_) | copy-start | bytes 49156
  23.3 4.6 %copy-start.8 = (bf16[384,256]{1,0:T(8,128)(2,1)}, bf16[384,256]{1,0:T(8,128)(2,1)S(1)}, u32[]{:S(2)}) copy-start(bf16[384,256]{1,0:T(8,128)(2,1)S(1)} %get-tuple-element.27.refs_13_) | copy-start | bytes 589828
  23.3 5.2 %copy-start.9 = (bf16[384,256]{1,0:T(8,128)(2,1)}, bf16[384,256]{1,0:T(8,128)(2,1)S(1)}, u32[]{:S(2)}) copy-start(bf16[384,256]{1,0:T(8,128)(2,1)S(1)} %get-tuple-element.28.refs_14_) | copy-start | bytes 589828
  23.3 6.5 %copy-start.13 = (s32[32,128]{1,0:T(8,128)}, s32[32,128]{1,0:T(8,128)S(1)}, u32[]{:S(2)}) copy-start(s32[32,128]{1,0:T(8,128)S(1)} %get-tuple-element.25.refs_9_.refs_10_) | copy-start | bytes 49156
  23.4 6.5 %copy-start.3 = (bf16[144,512]{1,0:T(8,128)(2,1)}, bf16[144,512]{1,0:T(8,128)(2,1)S(1)}, u32[]{:S(2)}) copy-start(bf16[144,512]{1,0:T(8,128)(2,1)S(1)} %collective-permute-done.1.refs_2_.refs_3_) | copy-start | bytes 442372
  24.3 5.6 %copy-start.4 = (bf16[144,512]{1,0:T(8,128)(2,1)}, bf16[144,512]{1,0:T(8,128)(2,1)S(1)}, u32[]{:S(2)}) copy-start(bf16[144,512]{1,0:T(8,128)(2,1)S(1)} %collective-permute-done.refs_1_.refs_2_) | copy-start | bytes 442372
  24.6 5.3 %copy-start.15 = (bf16[256,128]{1,0:T(8,128)(2,1)}, bf16[256,128]{1,0:T(8,128)(2,1)S(1)}, u32[]{:S(2)}) copy-start(bf16[256,128]{1,0:T(8,128)(2,1)S(1)} %get-tuple-element.24.refs_5_) | copy-start | bytes 196612
  24.6 5.3 %copy-start.16 = (bf16[256,128]{1,0:T(8,128)(2,1)}, bf16[256,128]{1,0:T(8,128)(2,1)S(1)}, u32[]{:S(2)}) copy-start(bf16[256,128]{1,0:T(8,128)(2,1)S(1)} %get-tuple-element.23.refs_6_) | copy-start | bytes 196612
  24.6 3.9 %collective-permute-start.2 = (bf16[256,128]{1,0:T(8,128)(2,1)S(1)}, bf16[256,128]{1,0:T(8,128)(2,1)S(1)}, u32[]{:S(2)}, u32[]{:S(2)}) collective-permute-start(bf16[256,128]{1,0:T(8,128)(2,1)S(1)} %get-tuple-element.23.refs_6_), channel_id=1, source_target_pairs={{0,8},{8,16},{16,24},{24,0},{1,9},{9,17},{17,25},{25,1},{2,10},{10... | collective-permute-start | bytes 196616 | tf_op jit(solution)/shard_map/ppermute | solution.py:849
  26.2 3.7 %collective-permute-start.3 = (bf16[256,128]{1,0:T(8,128)(2,1)S(1)}, bf16[256,128]{1,0:T(8,128)(2,1)S(1)}, u32[]{:S(2)}, u32[]{:S(2)}) collective-permute-start(bf16[256,128]{1,0:T(8,128)(2,1)S(1)} %get-tuple-element.24.refs_5_), channel_id=1, source_target_pairs={{8,0},{16,8},{24,16},{0,24},{9,1},{17,9},{25,17},{1,25},{10,2},{18... | collective-permute-start | bytes 196616 | tf_op jit(solution)/shard_map/ppermute | solution.py:850
  27.9 0.6 copy-start.7
  28.5 1.4 %copy-start.21 = (bf16[256,128]{1,0:T(8,128)(2,1)}, bf16[256,128]{1,0:T(8,128)(2,1)S(1)}, u32[]{:S(2)}) copy-start(bf16[256,128]{1,0:T(8,128)(2,1)S(1)} %collective-permute-done.2.refs_3_) | copy-start | bytes 196612
  29.9 0.6 copy-start.22
  30.5 21.8 %copy-start.19 = (bf16[9,64,64]{2,1,0:T(8,128)(2,1)S(1)}, bf16[9,64,64]{2,1,0:T(8,128)(2,1)}, u32[]{:S(2)}) copy-start(bf16[9,64,64]{2,1,0:T(8,128)(2,1)} %param.16) | copy-start | bytes 221188
  30.5 22.1 %copy-start.20 = (bf16[9,64,64]{2,1,0:T(8,128)(2,1)S(1)}, bf16[9,64,64]{2,1,0:T(8,128)(2,1)}, u32[]{:S(2)}) copy-start(bf16[9,64,64]{2,1,0:T(8,128)(2,1)} %param.17) | copy-start | bytes 221188
  48.0 20.0 %all-to-all-start.1 = ((bf16[32,64,128]{2,1,0:T(8,128)(2,1)}), bf16[32,64,128]{2,1,0:T(8,128)(2,1)S(1)}, u32[]{:S(2)}, u32[]{:S(2)}) async-start(bf16[32,64,128]{2,1,0:T(8,128)(2,1)} %get-tuple-element.30), calls=%async_computation.1 | async-start | bytes 1048576 | tf_op jit(solution)/shard_map/all_to_all | solution.py:909
  52.9 15.2 %copy-start.5 = (s32[9,2048]{1,0:T(8,128)S(1)}, s32[9,2048]{1,0:T(8,128)}, u32[]{:S(2)}) copy-start(s32[9,2048]{1,0:T(8,128)} %refs_5_.2) | copy-start | bytes 221188
  52.9 15.2 %copy-start.6 = (bf16[64,2048]{1,0:T(8,128)(2,1)S(1)}, bf16[64,2048]{1,0:T(8,128)(2,1)}, u32[]{:S(2)}) copy-start(bf16[64,2048]{1,0:T(8,128)(2,1)} %refs_2_.5) | copy-start | bytes 786436
  52.9 15.2 %copy-start.17 = (s32[2048]{0:T(1024)S(1)}, s32[2048]{0:T(1024)}, u32[]{:S(2)}) copy-start(s32[2048]{0:T(1024)} %param.18) | copy-start | bytes 24580
  55.3 28.2 %copy-start.1 = (bf16[24,64,512]{2,0,1:T(8,128)(2,1)}, bf16[24,64,512]{2,0,1:T(8,128)(2,1)S(1)}, u32[]{:S(2)}) copy-start(bf16[24,64,512]{2,0,1:T(8,128)(2,1)S(1)} %copy.33) | copy-start | bytes 4718596
  70.0 13.5 %collective-permute-start.4 = (bf16[80,512]{1,0:T(8,128)(2,1)S(1)}, bf16[80,512]{1,0:T(8,128)(2,1)S(1)}, u32[]{:S(2)}, u32[]{:S(2)}) collective-permute-start(bf16[80,512]{1,0:T(8,128)(2,1)S(1)} %get-tuple-element.34), channel_id=1, source_target_pairs={{0,1},{1,2},{2,3},{3,4},{4,5},{5,6},{6,7},{7,8},{8,9},{9,10},{10,1... | collective-permute-start | bytes 245768 | tf_op jit(solution)/shard_map/ppermute | solution.py:849
  72.9 10.6 %collective-permute-start.5 = (bf16[80,512]{1,0:T(8,128)(2,1)S(1)}, bf16[80,512]{1,0:T(8,128)(2,1)S(1)}, u32[]{:S(2)}, u32[]{:S(2)}) collective-permute-start(bf16[80,512]{1,0:T(8,128)(2,1)S(1)} %get-tuple-element.35), channel_id=1, source_target_pairs={{1,0},{2,1},{3,2},{4,3},{5,4},{6,5},{7,6},{8,7},{9,8},{10,9},{11,1... | collective-permute-start | bytes 245768 | tf_op jit(solution)/shard_map/ppermute | solution.py:850

commit v6 on v5

--- a/solution.py
+++ b/solution.py
@@ -589,7 +589,7 @@
     rows, channels, cols = next_ref.shape
     shift = cols.bit_length() - 1
     tiles, width = list_ref.shape
-    group, many = 6, 2
+    group, many = 6, 4
     compact[...] = jnp.zeros(compact.shape, BF)
 
     def pick(tile):
@@ -612,11 +612,14 @@
 
     last = number_ref[number_ref.shape[0] - 1, number_ref.shape[1] - 1] + 1
     tiles_live = (last + (width - 1)) >> 8
-    lax.fori_loop(0, tiles_live >> 1, step, 0)
-
-    @pl.when((tiles_live & 1) == 1)
-    def _():
-        pick(tiles_live - 1)
+    steps = tiles_live >> 2
+    lax.fori_loop(0, steps, step, 0)
+
+    def single(tile, carry):
+        pick(tile)
+        return carry
+
+    lax.fori_loop(steps * many, tiles_live, single, 0)
 
 
 def spread_live(compact, before_ref, number_ref, send_ref):
@@ -633,7 +636,7 @@
         for part in range(width // LANES):
             send_ref[2 * i + part] = total[:, part * LANES : (part + 1) * LANES]
 
-    for_chunks(send_ref.shape[0] * LANES // width, 4, spread)
+    for_chunks(send_ref.shape[0] * LANES // width, 8, spread)
 
 
 def atmosphere(
@@ -697,7 +700,7 @@
         out_ref[:, lanes] = (ocean_ref[:, lanes].astype(F32) + total).astype(BF)
 
     channels, cells = ocean_ref.shape
-    for_chunks(cells // width, 2, block)
+    for_chunks(cells // width, 4, block)
     reach = 2 * HALO
     for ref, first, start in ((head_ref, 0, 0), (tail_ref, cells - reach, cells - HALO)):
         ref[0:channels] = out_ref[:, first : first + reach]
@@ -762,13 +765,13 @@
     def hide(b):
         hide_block(hidden_ref, b, values, b, local[b, 0:taps], first_ref)
 
-    for_chunks(blocks - 2, 2, hide)
+    for_chunks(blocks - 2, 3, hide)
 
     def finish(b):
         mixed = neighbour_block(hidden_ref, b, local[b + 1, 0:taps], second_ref[...])
         out_ref[:, lanes_at(b, HALO)] = (values[b + 2].astype(F32) + mixed).astype(BF)
 
-    for_chunks(blocks - 4, 2, finish)
+    for_chunks(blocks - 4, 4, finish)
 
 
 def ocean_inner(own, index, first, second):

time: 88 us -> 86.5 us (0.983)
  Pallas kernels: 35.6 us -> 33.5 us
    pallas_call x2, Pallas kernels: 19.7 us -> 18.4 us  [call(): pl.pallas_call(kernel, out_shape=outs, in_specs=[ANY] * len(ins), out_spe...]
where the time goes in v6:
time: 86.5 us; the launch traced here: 86 us
  Pallas kernels  33.5 us (39%)
  starting transfers between devices  27.3 us (32%)
  waiting for transfers between devices  15.3 us (18%)
  local copies, waits for them, and re-layouts  8.85 us (10%)
  between operations  1 us (1%)
    pallas_call x2, Pallas kernels, call(): pl.pallas_call(kernel, out_shape=outs, in_specs=[ANY] * len(ins), out_spe...  18.4 us
    pallas_call x6, Pallas kernels, call(): pl.pallas_call(plain, out_shape=outs, in_specs=[VMEM if i in touched else...  15.1 us
    all_to_all x1, waiting for transfers between devices, shards(): lax.all_to_all(outgoing, both, split_axis=0, concat_axis=0, tiled=True)  12.8 us
    ppermute x3, starting transfers between devices, from_neighbours(): lax.ppermute(high, axis, [(i, (i + 1) % count) for i in range(ends)])  8.57 us
    all_to_all x1, starting transfers between devices, heat_slots(): got = lax.all_to_all(table, both, split_axis=0, concat_axis=0, tiled=True)  7.1 us
    ppermute x3, starting transfers between devices, from_neighbours(): after = lax.ppermute(low, axis, [((i + 1) % count, i) for i in range(ends)])  6.83 us
    all_to_all x1, starting transfers between devices, shards(): lax.all_to_all(outgoing, both, split_axis=0, concat_axis=0, tiled=True)  4.83 us
    unnamed x47, local copies, waits for them, and re-layouts  3.18 us
  transfers between devices with their start and end apart: 8, of which 4 were waited for; matrix products, arithmetic and copies ran while one was open for 6% of the time, Pallas kernels for 11%

profile of v6, /device:TPU:1, one launch (start us, length us, event | category | flops | bytes accessed | tf_op | source)
XLA Modules:
  0.0 86.0 jit_solution(11717605200877390739)
XLA Ops:
  0.6 1.4 %slice_bitcast_fusion = (bf16[2,64,512]{2,0,1:T(2,128)(2,1)S(1)}, bf16[2,64,512]{2,0,1:T(2,128)(2,1)S(1)}) fusion(bf16[64,24,512]{2,1,0:T(8,128)(2,1)} %param.11), kind=kLoop, calls=%fused_computation.2 | loop fusion | bytes 524288 | tf_op jit(solution)/shard_map/transpose | solution.py:877
  2.0 0.7 copy.20
  2.7 0.7 copy.21
  3.4 2.2 %shard_map.122 = (bf16[32,16,128]{2,1,0:T(8,128)(2,1)}, bf16[144,512]{1,0:T(8,128)(2,1)}, bf16[144,512]{1,0:T(8,128)(2,1)}) custom-call(bf16[64,2048]{1,0:T(8,128)(2,1)} %refs_2_.5, s32[1,2048]{1,0:T(1,128)} %bitcast.22, s32[1,4096]{1,0:T(1,128)} %refs_1_.2, bf16[128,512]{1,0:T(8,128)(2,1)} %bitcast.26, bf16[128,512]{1,0:T(8,128)(2,1)} %bitcast.27, ...), custom_call_target="tpu_custom_call" | custom-call | tf_op jit(solution)/shard_map/pallas_call | solution.py:67
  5.6 7.1 %all-to-all-start = ((bf16[32,16,128]{2,1,0:T(8,128)(2,1)}), bf16[32,16,128]{2,1,0:T(8,128)(2,1)S(1)}, u32[]{:S(2)}, u32[]{:S(2)}) async-start(bf16[32,16,128]{2,1,0:T(8,128)(2,1)} %get-tuple-element.21), calls=%async_computation | async-start | bytes 262144 | tf_op jit(solution)/shard_map/all_to_all | solution.py:192
  12.7 1.3 %collective-permute-start.1 = (bf16[144,512]{1,0:T(8,128)(2,1)}, bf16[144,512]{1,0:T(8,128)(2,1)S(1)}, u32[]{:S(2)}, u32[]{:S(2)}) collective-permute-start(bf16[144,512]{1,0:T(8,128)(2,1)} %get-tuple-element.20.refs_3_), channel_id=1, source_target_pairs={{1,0},{2,1},{3,2},{4,3},{5,4},{6,5},{7,6},{9,8},{10,9},{11,10},{12... | collective-permute-start | bytes 442376 | tf_op jit(solution)/shard_map/ppermute | solution.py:853
  14.0 0.0 copy-start.11
  14.0 4.1 %collective-permute-start = (bf16[144,512]{1,0:T(8,128)(2,1)}, bf16[144,512]{1,0:T(8,128)(2,1)S(1)}, u32[]{:S(2)}, u32[]{:S(2)}) collective-permute-start(bf16[144,512]{1,0:T(8,128)(2,1)} %get-tuple-element.19), channel_id=1, source_target_pairs={{0,1},{1,2},{2,3},{3,4},{4,5},{5,6},{6,7},{8,9},{9,10},{10,11},{11... | collective-permute-start | bytes 442376 | tf_op jit(solution)/shard_map/ppermute | solution.py:852
  18.2 1.9 %copy.34 = bf16[64,24,512]{2,0,1:T(8,128)(2,1)S(1)} copy(bf16[64,24,512]{2,1,0:T(8,128)(2,1)} %param.11) | data formatting | bytes 3145728 | tf_op args[0]
  20.1 0.0 copy-start
  20.1 0.2 all-to-all-done.refs_0_.refs_1_.refs_8_
  20.3 3.0 %shard_map.123 = (f32[24,512]{1,0:T(8,128)S(1)}, bf16[384,256]{1,0:T(8,128)(2,1)S(1)}, bf16[384,256]{1,0:T(8,128)(2,1)S(1)}, s32[32,128]{1,0:T(8,128)S(1)}, s32[16,256]{1,0:T(8,128)S(1)}) custom-call(bf16[32,16,128]{2,1,0:T(8,128)(2,1)S(1)} %all-to-all-done.refs_0_.refs_1_.refs_8_, s32[1,4096]{1,0:T(1,128)S(1)} %copy-done.14, ...), custom_call_target="tpu_custom_call" | custom-call | tf_op jit(solution)/shard_map/pallas_call | solution.py:30
  23.4 0.9 %collective-permute-done.refs_1_.refs_2_ = bf16[144,512]{1,0:T(8,128)(2,1)S(1)} collective-permute-done((bf16[144,512]{1,0:T(8,128)(2,1)}, bf16[144,512]{1,0:T(8,128)(2,1)S(1)}, u32[]{:S(2)}, u32[]{:S(2)}) %collective-permute-start) | collective-permute-done | bytes 147488 | tf_op jit(solution)/shard_map/ppermute | solution.py:852
  24.3 0.3 shard_map.124
  24.6 1.5 %collective-permute-start.2 = (bf16[256,128]{1,0:T(8,128)(2,1)S(1)}, bf16[256,128]{1,0:T(8,128)(2,1)S(1)}, u32[]{:S(2)}, u32[]{:S(2)}) collective-permute-start(bf16[256,128]{1,0:T(8,128)(2,1)S(1)} %get-tuple-element.23.refs_6_), channel_id=1, source_target_pairs={{0,8},{8,16},{16,24},{24,0},{1,9},{9,17},{17,25},{25,1},{2,10},{10... | collective-permute-start | bytes 196616 | tf_op jit(solution)/shard_map/ppermute | solution.py:852
  26.2 1.7 %shard_map.125.refs_7_ = f32[32,512]{1,0:T(8,128)S(1)} custom-call(f32[24,512]{1,0:T(8,128)S(1)} %get-tuple-element.22.refs_4_.refs_0_, bf16[32,16,128]{2,1,0:T(8,128)(2,1)S(1)} %all-to-all-done.refs_0_.refs_1_.refs_8_, bf16[144,512]{1,0:T(8,128)(2,1)S(1)} %collective-permute-done.refs_1_.refs_2_, bf16[144,512]{1,0:T(8,128)(2,1)S(1)} %collective-permute-done.1.refs_2_.refs_3_), custom_call_target="tpu_custom_call" | custom-call | tf_op jit(solution)/shard_map/pallas_call | solution.py:30
  27.9 0.6 copy-done.7
  28.5 1.4 %collective-permute-done.3.refs_4_ = bf16[256,128]{1,0:T(8,128)(2,1)S(1)} collective-permute-done((bf16[256,128]{1,0:T(8,128)(2,1)S(1)}, bf16[256,128]{1,0:T(8,128)(2,1)S(1)}, u32[]{:S(2)}, u32[]{:S(2)}) %collective-permute-start.3) | collective-permute-done | bytes 65568 | tf_op jit(solution)/shard_map/ppermute | solution.py:853
  29.9 0.6 copy-done.22
  30.5 16.3 %shard_map.126 = (bf16[24,64,512]{2,1,0:T(8,128)(2,1)}, bf16[32,64,128]{2,1,0:T(8,128)(2,1)}) custom-call(bf16[24,64,512]{2,1,0:T(8,128)(2,1)} %bitcast.19, bf16[144,512]{1,0:T(8,128)(2,1)} %copy-done.4, bf16[144,512]{1,0:T(8,128)(2,1)} %copy-done.3, bf16[256,128]{1,0:T(8,128)(2,1)} %copy-done.21, bf16[256,128]{1,0:T(8,128)(2,1)} %copy-done.22, ...), custom_call_target="tpu_custom_call" | custom-call | tf_op jit(solution)/shard_map/pallas_call | solution.py:67
  46.8 4.8 %all-to-all-start.1 = ((bf16[32,64,128]{2,1,0:T(8,128)(2,1)}), bf16[32,64,128]{2,1,0:T(8,128)(2,1)S(1)}, u32[]{:S(2)}, u32[]{:S(2)}) async-start(bf16[32,64,128]{2,1,0:T(8,128)(2,1)} %get-tuple-element.30), calls=%async_computation.1 | async-start | bytes 1048576 | tf_op jit(solution)/shard_map/all_to_all | solution.py:912
  51.6 0.1 copy.23
  51.8 0.1 copy.25.refs_5_.refs_2_.refs_6_
  51.9 0.1 copy.24
  52.1 0.1 copy.26.refs_6_.refs_3_.refs_7_
  52.2 2.3 %copy.33 = bf16[24,64,512]{2,0,1:T(8,128)(2,1)S(1)} copy(bf16[24,64,512]{2,1,0:T(8,128)(2,1)} %get-tuple-element.29) | data formatting | bytes 3145728 | tf_op jit(solution)/shard_map/pallas_call | solution.py:67
  54.6 12.8 %all-to-all-done.1.refs_0_ = bf16[32,64,128]{2,1,0:T(8,128)(2,1)S(1)} async-done(((bf16[32,64,128]{2,1,0:T(8,128)(2,1)}), bf16[32,64,128]{2,1,0:T(8,128)(2,1)S(1)}, u32[]{:S(2)}, u32[]{:S(2)}) %all-to-all-start.1) | async-done | bytes 524320 | tf_op jit(solution)/shard_map/all_to_all | solution.py:912
  67.4 1.6 %shard_map.127 = (bf16[64,2048]{1,0:T(8,128)(2,1)S(1)}, bf16[80,512]{1,0:T(8,128)(2,1)S(1)}, bf16[80,512]{1,0:T(8,128)(2,1)S(1)}) custom-call(bf16[32,64,128]{2,1,0:T(8,128)(2,1)S(1)} %all-to-all-done.1.refs_0_, s32[1,2048]{1,0:T(1,128)S(1)} %bitcast.23, bf16[64,2048]{1,0:T(8,128)(2,1)S(1)} %copy-done.6, s32[9,2048]{1,0:T(8,128)S(1)} %copy-done.5, ...), custom_call_target="tpu_custom_call" | custom-call | tf_op jit(solution)/shard_map/pallas_call | solution.py:30
  69.0 2.9 %collective-permute-start.4 = (bf16[80,512]{1,0:T(8,128)(2,1)S(1)}, bf16[80,512]{1,0:T(8,128)(2,1)S(1)}, u32[]{:S(2)}, u32[]{:S(2)}) collective-permute-start(bf16[80,512]{1,0:T(8,128)(2,1)S(1)} %get-tuple-element.34), channel_id=1, source_target_pairs={{0,1},{1,2},{2,3},{3,4},{4,5},{5,6},{6,7},{7,8},{8,9},{9,10},{10,1... | collective-permute-start | bytes 245768 | tf_op jit(solution)/shard_map/ppermute | solution.py:852
  71.9 5.5 %collective-permute-start.5 = (bf16[80,512]{1,0:T(8,128)(2,1)S(1)}, bf16[80,512]{1,0:T(8,128)(2,1)S(1)}, u32[]{:S(2)}, u32[]{:S(2)}) collective-permute-start(bf16[80,512]{1,0:T(8,128)(2,1)S(1)} %get-tuple-element.35), channel_id=1, source_target_pairs={{1,0},{2,1},{3,2},{4,3},{5,4},{6,5},{7,6},{8,7},{9,8},{10,9},{11,1... | collective-permute-start | bytes 245768 | tf_op jit(solution)/shard_map/ppermute | solution.py:853
  77.5 4.5 %shard_map.128 = (bf16[6,64,256]{2,1,0:T(8,128)(2,1)S(1)}, bf16[64,1024]{1,0:T(8,128)(2,1)S(1)}) custom-call(bf16[64,2048]{1,0:T(8,128)(2,1)S(1)} %get-tuple-element.31.refs_0_, s32[9,2048]{1,0:T(8,128)S(1)} %copy-done.5, bf16[64,576]{1,0:T(8,128)(2,1)S(1)} %copy.25.refs_5_.refs_2_.refs_6_, bf16[64,576]{1,0:T(8,128)(2,1)S(1)} %copy.26.refs_6_.refs_3_.refs_7_), custom_call_target="tpu_custom_call" | custom-call | tf_op jit(solution)/shard_map/pallas_call | solution.py:30
  82.0 4.0 %shard_map.129 = bf16[64,2048]{1,0:T(8,128)(2,1)} custom-call(bf16[64,2048]{1,0:T(8,128)(2,1)S(1)} %get-tuple-element.31.refs_0_, bf16[6,64,256]{2,1,0:T(8,128)(2,1)S(1)} %get-tuple-element.32.refs_1_, bf16[64,1024]{1,0:T(8,128)(2,1)S(1)} %get-tuple-element.33.refs_2_, bf16[80,512]{1,0:T(8,128)(2,1)S(1)} %collective-permute-done.4.refs_3_, ...), custom_call_target="tpu_custom_call" | custom-call | tf_op jit(solution)/shard_map/pallas_call | solution.py:30
  (47 shorter events, 0.1 us)
Async XLA Ops:
  5.6 14.7 %all-to-all-start = ((bf16[32,16,128]{2,1,0:T(8,128)(2,1)}), bf16[32,16,128]{2,1,0:T(8,128)(2,1)S(1)}, u32[]{:S(2)}, u32[]{:S(2)}) async-start(bf16[32,16,128]{2,1,0:T(8,128)(2,1)} %get-tuple-element.21), calls=%async_computation | async-start | bytes 262144 | tf_op jit(solution)/shard_map/all_to_all | solution.py:192
  12.7 10.7 %collective-permute-start.1 = (bf16[144,512]{1,0:T(8,128)(2,1)}, bf16[144,512]{1,0:T(8,128)(2,1)S(1)}, u32[]{:S(2)}, u32[]{:S(2)}) collective-permute-start(bf16[144,512]{1,0:T(8,128)(2,1)} %get-tuple-element.20.refs_3_), channel_id=1, source_target_pairs={{1,0},{2,1},{3,2},{4,3},{5,4},{6,5},{7,6},{9,8},{10,9},{11,10},{12... | collective-permute-start | bytes 442376 | tf_op jit(solution)/shard_map/ppermute | solution.py:853
  14.0 6.3 %copy-start.11 = (bf16[3,3,64,64]{3,2,1,0:T(8,128)(2,1)S(1)}, bf16[3,3,64,64]{3,2,1,0:T(8,128)(2,1)}, u32[]{:S(2)}) copy-start(bf16[3,3,64,64]{3,2,1,0:T(8,128)(2,1)} %refs_2_.4) | copy-start | bytes 221188
  14.0 6.3 %copy-start.12 = (bf16[3,3,64,64]{3,2,1,0:T(8,128)(2,1)S(1)}, bf16[3,3,64,64]{3,2,1,0:T(8,128)(2,1)}, u32[]{:S(2)}) copy-start(bf16[3,3,64,64]{3,2,1,0:T(8,128)(2,1)} %refs_3_.2) | copy-start | bytes 221188
  14.0 6.3 %copy-start.14 = (s32[1,4096]{1,0:T(1,128)S(1)}, s32[1,4096]{1,0:T(1,128)}, u32[]{:S(2)}) copy-start(s32[1,4096]{1,0:T(1,128)} %refs_1_.2) | copy-start | bytes 49156
  14.0 10.3 %copy-start.10 = (bf16[144,512]{1,0:T(8,128)(2,1)S(1)}, bf16[144,512]{1,0:T(8,128)(2,1)}, u32[]{:S(2)}) copy-start(bf16[144,512]{1,0:T(8,128)(2,1)} %get-tuple-element.20.refs_3_) | copy-start | bytes 442372
  14.0 10.3 %collective-permute-start = (bf16[144,512]{1,0:T(8,128)(2,1)}, bf16[144,512]{1,0:T(8,128)(2,1)S(1)}, u32[]{:S(2)}, u32[]{:S(2)}) collective-permute-start(bf16[144,512]{1,0:T(8,128)(2,1)} %get-tuple-element.19), channel_id=1, source_target_pairs={{0,1},{1,2},{2,3},{3,4},{4,5},{5,6},{6,7},{8,9},{9,10},{10,11},{11... | collective-permute-start | bytes 442376 | tf_op jit(solution)/shard_map/ppermute | solution.py:852
  20.1 9.8 %copy-start = (bf16[64,24,512]{2,0,1:T(8,128)(2,1)}, bf16[64,24,512]{2,0,1:T(8,128)(2,1)S(1)}, u32[]{:S(2)}) copy-start(bf16[64,24,512]{2,0,1:T(8,128)(2,1)S(1)} %copy.34) | copy-start | bytes 4718596
  20.3 9.6 %copy-start.2 = (bf16[32,16,128]{2,1,0:T(8,128)(2,1)}, bf16[32,16,128]{2,1,0:T(8,128)(2,1)S(1)}, u32[]{:S(2)}) copy-start(bf16[32,16,128]{2,1,0:T(8,128)(2,1)S(1)} %all-to-all-done.refs_0_.refs_1_.refs_8_) | copy-start | bytes 393220
  23.3 2.9 %copy-start.18 = (s32[16,256]{1,0:T(8,128)}, s32[16,256]{1,0:T(8,128)S(1)}, u32[]{:S(2)}) copy-start(s32[16,256]{1,0:T(8,128)S(1)} %get-tuple-element.26.refs_11_) | copy-start | bytes 49156
  23.3 4.6 %copy-start.8 = (bf16[384,256]{1,0:T(8,128)(2,1)}, bf16[384,256]{1,0:T(8,128)(2,1)S(1)}, u32[]{:S(2)}) copy-start(bf16[384,256]{1,0:T(8,128)(2,1)S(1)} %get-tuple-element.27.refs_13_) | copy-start | bytes 589828
  23.3 5.2 %copy-start.9 = (bf16[384,256]{1,0:T(8,128)(2,1)}, bf16[384,256]{1,0:T(8,128)(2,1)S(1)}, u32[]{:S(2)}) copy-start(bf16[384,256]{1,0:T(8,128)(2,1)S(1)} %get-tuple-element.28.refs_14_) | copy-start | bytes 589828
  23.3 6.5 %copy-start.13 = (s32[32,128]{1,0:T(8,128)}, s32[32,128]{1,0:T(8,128)S(1)}, u32[]{:S(2)}) copy-start(s32[32,128]{1,0:T(8,128)S(1)} %get-tuple-element.25.refs_9_.refs_10_) | copy-start | bytes 49156
  23.4 6.5 %copy-start.3 = (bf16[144,512]{1,0:T(8,128)(2,1)}, bf16[144,512]{1,0:T(8,128)(2,1)S(1)}, u32[]{:S(2)}) copy-start(bf16[144,512]{1,0:T(8,128)(2,1)S(1)} %collective-permute-done.1.refs_2_.refs_3_) | copy-start | bytes 442372
  24.3 5.6 %copy-start.4 = (bf16[144,512]{1,0:T(8,128)(2,1)}, bf16[144,512]{1,0:T(8,128)(2,1)S(1)}, u32[]{:S(2)}) copy-start(bf16[144,512]{1,0:T(8,128)(2,1)S(1)} %collective-permute-done.refs_1_.refs_2_) | copy-start | bytes 442372
  24.6 5.3 %copy-start.15 = (bf16[256,128]{1,0:T(8,128)(2,1)}, bf16[256,128]{1,0:T(8,128)(2,1)S(1)}, u32[]{:S(2)}) copy-start(bf16[256,128]{1,0:T(8,128)(2,1)S(1)} %get-tuple-element.24.refs_5_) | copy-start | bytes 196612
  24.6 5.3 %copy-start.16 = (bf16[256,128]{1,0:T(8,128)(2,1)}, bf16[256,128]{1,0:T(8,128)(2,1)S(1)}, u32[]{:S(2)}) copy-start(bf16[256,128]{1,0:T(8,128)(2,1)S(1)} %get-tuple-element.23.refs_6_) | copy-start | bytes 196612
  24.6 3.9 %collective-permute-start.2 = (bf16[256,128]{1,0:T(8,128)(2,1)S(1)}, bf16[256,128]{1,0:T(8,128)(2,1)S(1)}, u32[]{:S(2)}, u32[]{:S(2)}) collective-permute-start(bf16[256,128]{1,0:T(8,128)(2,1)S(1)} %get-tuple-element.23.refs_6_), channel_id=1, source_target_pairs={{0,8},{8,16},{16,24},{24,0},{1,9},{9,17},{17,25},{25,1},{2,10},{10... | collective-permute-start | bytes 196616 | tf_op jit(solution)/shard_map/ppermute | solution.py:852
  26.2 3.7 %collective-permute-start.3 = (bf16[256,128]{1,0:T(8,128)(2,1)S(1)}, bf16[256,128]{1,0:T(8,128)(2,1)S(1)}, u32[]{:S(2)}, u32[]{:S(2)}) collective-permute-start(bf16[256,128]{1,0:T(8,128)(2,1)S(1)} %get-tuple-element.24.refs_5_), channel_id=1, source_target_pairs={{8,0},{16,8},{24,16},{0,24},{9,1},{17,9},{25,17},{1,25},{10,2},{18... | collective-permute-start | bytes 196616 | tf_op jit(solution)/shard_map/ppermute | solution.py:853
  27.9 0.6 copy-start.7
  28.5 1.4 %copy-start.21 = (bf16[256,128]{1,0:T(8,128)(2,1)}, bf16[256,128]{1,0:T(8,128)(2,1)S(1)}, u32[]{:S(2)}) copy-start(bf16[256,128]{1,0:T(8,128)(2,1)S(1)} %collective-permute-done.2.refs_3_) | copy-start | bytes 196612
  29.9 0.6 copy-start.22
  30.5 21.1 %copy-start.19 = (bf16[9,64,64]{2,1,0:T(8,128)(2,1)S(1)}, bf16[9,64,64]{2,1,0:T(8,128)(2,1)}, u32[]{:S(2)}) copy-start(bf16[9,64,64]{2,1,0:T(8,128)(2,1)} %param.16) | copy-start | bytes 221188
  30.5 21.4 %copy-start.20 = (bf16[9,64,64]{2,1,0:T(8,128)(2,1)S(1)}, bf16[9,64,64]{2,1,0:T(8,128)(2,1)}, u32[]{:S(2)}) copy-start(bf16[9,64,64]{2,1,0:T(8,128)(2,1)} %param.17) | copy-start | bytes 221188
  46.8 20.6 %all-to-all-start.1 = ((bf16[32,64,128]{2,1,0:T(8,128)(2,1)}), bf16[32,64,128]{2,1,0:T(8,128)(2,1)S(1)}, u32[]{:S(2)}, u32[]{:S(2)}) async-start(bf16[32,64,128]{2,1,0:T(8,128)(2,1)} %get-tuple-element.30), calls=%async_computation.1 | async-start | bytes 1048576 | tf_op jit(solution)/shard_map/all_to_all | solution.py:912
  52.2 15.2 %copy-start.5 = (s32[9,2048]{1,0:T(8,128)S(1)}, s32[9,2048]{1,0:T(8,128)}, u32[]{:S(2)}) copy-start(s32[9,2048]{1,0:T(8,128)} %refs_5_.2) | copy-start | bytes 221188
  52.2 15.2 %copy-start.6 = (bf16[64,2048]{1,0:T(8,128)(2,1)S(1)}, bf16[64,2048]{1,0:T(8,128)(2,1)}, u32[]{:S(2)}) copy-start(bf16[64,2048]{1,0:T(8,128)(2,1)} %refs_2_.5) | copy-start | bytes 786436
  52.2 15.2 %copy-start.17 = (s32[2048]{0:T(1024)S(1)}, s32[2048]{0:T(1024)}, u32[]{:S(2)}) copy-start(s32[2048]{0:T(1024)} %param.18) | copy-start | bytes 24580
  54.6 27.4 %copy-start.1 = (bf16[24,64,512]{2,0,1:T(8,128)(2,1)}, bf16[24,64,512]{2,0,1:T(8,128)(2,1)S(1)}, u32[]{:S(2)}) copy-start(bf16[24,64,512]{2,0,1:T(8,128)(2,1)S(1)} %copy.33) | copy-start | bytes 4718596
  69.0 12.9 %collective-permute-start.4 = (bf16[80,512]{1,0:T(8,128)(2,1)S(1)}, bf16[80,512]{1,0:T(8,128)(2,1)S(1)}, u32[]{:S(2)}, u32[]{:S(2)}) collective-permute-start(bf16[80,512]{1,0:T(8,128)(2,1)S(1)} %get-tuple-element.34), channel_id=1, source_target_pairs={{0,1},{1,2},{2,3},{3,4},{4,5},{5,6},{6,7},{7,8},{8,9},{9,10},{10,1... | collective-permute-start | bytes 245768 | tf_op jit(solution)/shard_map/ppermute | solution.py:852
  71.9 10.0 %collective-permute-start.5 = (bf16[80,512]{1,0:T(8,128)(2,1)S(1)}, bf16[80,512]{1,0:T(8,128)(2,1)S(1)}, u32[]{:S(2)}, u32[]{:S(2)}) collective-permute-start(bf16[80,512]{1,0:T(8,128)(2,1)S(1)} %get-tuple-element.35), channel_id=1, source_target_pairs={{1,0},{2,1},{3,2},{4,3},{5,4},{6,5},{7,6},{8,7},{9,8},{10,9},{11,1... | collective-permute-start | bytes 245768 | tf_op jit(solution)/shard_map/ppermute | solution.py:853
